TPU v7x, 32 devices: a whole 2x2x4 slice. The times are simulated.
32 devices in a mesh: dev: 32 (over z, y, x, core).
Axes of the slice: x: 2, y: 2, z: 4, core: 2. Of those that a mesh axis runs over, the one named last changes fastest.
Arguments:
- tokens: bfloat16 [8192, 2048], P('dev'), may hold values from -6 to 6
- attn_gain: bfloat16 [2048], P('dev'), may hold values from 0.099609375 to 1.8984375
- w_query: bfloat16 [2048, 2048], P('dev'), may hold values from -0.125 to 0.125
- w_key: bfloat16 [2048, 256], P('dev'), may hold values from -0.125 to 0.125
- w_value: bfloat16 [2048, 256], P('dev'), may hold values from -0.125 to 0.125
- w_out: bfloat16 [2048, 2048], P('dev'), may hold values from -2 to 2
- mlp_gain: bfloat16 [2048], P('dev'), may hold values from 0.099609375 to 1.8984375
- w_gate: bfloat16 [2048, 5632], P('dev'), may hold values from -0.125 to 0.125
- w_up: bfloat16 [2048, 5632], P('dev'), may hold values from -0.125 to 0.125
- w_down: bfloat16 [5632, 2048], P('dev'), may hold values from -0.078125 to 0.078125
- cotangent: bfloat16 [8192, 2048], P('dev'), may hold values from -6 to 6
Outputs:
- output: bfloat16 [8192, 2048], P('dev')
- input_grad: bfloat16 [8192, 2048], P('dev')
- attn_gain_grad: float32 [2048], P('dev')
- query_grad: float32 [2048, 2048], P('dev')
- key_grad: float32 [2048, 256], P('dev')
- value_grad: float32 [2048, 256], P('dev')
- out_grad: float32 [2048, 2048], P('dev')
- mlp_gain_grad: float32 [2048], P('dev')
- gate_grad: float32 [2048, 5632], P('dev')
- up_grad: float32 [2048, 5632], P('dev')
- down_grad: float32 [5632, 2048], P('dev')
All inputs are finite; a program needn't handle non-finite values.
Results may differ from a plain program's by a relative error of at most 0.014.
Values may be sent and summed in bfloat16 or wider, within the bound.
No kernel may reach another device: no remote copies, remote signals or barrier semaphores. Data moves between devices by JAX's collectives and lax.ppermute only.
A program may use at most 384 MiB of HBM per device.

v0:
```python
from functools import partial

import jax
import jax.numpy as jnp
from jax import lax
from jax.sharding import PartitionSpec as P

HD = 64
GROUP = 4


EPS = 1e-05
THETA = 10000.0
NEG = -1e30


def passed_along(block, axis, distance):
    devices = range(lax.axis_size(axis))
    route = [(i - distance, i) for i in devices if i - distance in devices]
    return lax.ppermute(block, axis, route)


def contract_rows(left, right):
    return lax.dot_general(
        left, right, (((0,), (0,)), ((), ())), preferred_element_type=jnp.float32
    )


def times_transposed(left, right):
    return lax.dot_general(
        left, right, (((1,), (1,)), ((), ())), preferred_element_type=jnp.float32
    )


def rms_scale(values):
    return lax.rsqrt(jnp.mean(values * values, axis=1, keepdims=True) + EPS)


def rope_tables(positions, head_size):
    half_size = head_size // 2
    frequency = THETA ** (-(jnp.arange(half_size).astype(jnp.float32) * 2.0 / head_size))
    angles = positions.astype(jnp.float32)[:, None] * frequency[None, :]
    return (jnp.cos(angles)[:, None, :], jnp.sin(angles)[:, None, :])


def rotate(values, cosine_table, sine_table):
    half_size = values.shape[-1] // 2
    front_half = values[..., :half_size]
    back_half = values[..., half_size:]
    return jnp.concatenate(
        [
            front_half * cosine_table - back_half * sine_table,
            back_half * cosine_table + front_half * sine_table,
        ],
        axis=-1,
    )


def rotate_back(grads, cosine_table, sine_table):
    half_size = grads.shape[-1] // 2
    front_half = grads[..., :half_size]
    back_half = grads[..., half_size:]
    return jnp.concatenate(
        [
            front_half * cosine_table + back_half * sine_table,
            back_half * cosine_table - front_half * sine_table,
        ],
        axis=-1,
    )


def pair_scores(query_pair, key_block, causal_mask, scale):
    raw_scores = (
        jnp.einsum("hqd,kd->hqk", query_pair, key_block, preferred_element_type=jnp.float32) * scale
    )
    if causal_mask is None:
        return raw_scores
    return jnp.where(causal_mask[None], raw_scores, NEG)


def all_scores(query_pair, key_blocks, group_place, scale):
    row_count = query_pair.shape[1]
    causal_mask = jnp.arange(row_count)[:, None] >= jnp.arange(row_count)[None, :]
    blocks = [pair_scores(query_pair, key_blocks[0], causal_mask, scale)]
    filler = jnp.full(blocks[0].shape, NEG, jnp.float32)
    for offset in range(1, key_blocks.shape[0]):
        blocks.append(
            lax.cond(
                group_place >= offset,
                partial(pair_scores, query_pair, key_blocks[offset], None, scale),
                partial(jnp.asarray, filler),
            )
        )
    return jnp.concatenate(blocks, axis=2)


def block_list(function, count, group_place, shape):
    zeros_block = jnp.zeros(shape, jnp.float32)
    results = [function(0)]
    for offset in range(1, count):
        results.append(
            lax.cond(
                group_place >= offset, partial(function, offset), partial(jnp.asarray, zeros_block)
            )
        )
    return results


def per_device(
    tokens, attn_gain, w_query, w_key, w_value, w_out, mlp_gain, w_gate, w_up, w_down, cotangent
):
    row_count = tokens.shape[0]
    group_place = lax.axis_index("dev") % GROUP
    attn_full = (
        lax.all_gather(attn_gain, "dev", axis=0, tiled=True),
        lax.all_gather(w_query, "dev", axis=0, tiled=True),
        lax.all_gather(w_key, "dev", axis=0, tiled=True),
        lax.all_gather(w_value, "dev", axis=0, tiled=True),
        lax.all_gather(w_out, "dev", axis=0, tiled=True),
    )
    gain_one, query_weight, key_weight, value_weight, out_weight = attn_full
    head_count = query_weight.shape[1] // HD
    kv_heads = key_weight.shape[1] // HD
    pair_count = head_count // 2
    pairs_per_group = head_count // kv_heads // 2
    scale = HD ** (-0.5)
    source = tokens.astype(jnp.float32)
    scale_one = rms_scale(source)
    normed_one = (source * scale_one * gain_one.astype(jnp.float32)).astype(jnp.bfloat16)
    query_lin = jnp.dot(normed_one, query_weight, preferred_element_type=jnp.float32)
    key_lin = jnp.dot(normed_one, key_weight, preferred_element_type=jnp.float32)
    value_low = jnp.dot(normed_one, value_weight, preferred_element_type=jnp.float32).astype(
        jnp.bfloat16
    )
    cosine_table, sine_table = rope_tables(jnp.arange(row_count) + group_place * row_count, HD)
    queries = rotate(query_lin.reshape(row_count, head_count, HD), cosine_table, sine_table).astype(
        jnp.bfloat16
    )
    keys_flat = rotate(key_lin.reshape(row_count, kv_heads, HD), cosine_table, sine_table)
    keys_flat = keys_flat.astype(jnp.bfloat16).reshape(row_count, kv_heads * HD)
    own_pair = jnp.stack([keys_flat, value_low])
    received = [own_pair]
    for offset in range(1, GROUP):
        received.append(passed_along(own_pair, "dev", offset))
    stacked = jnp.stack(received)
    key_all = stacked[:, 0]
    value_all = stacked[:, 1]
    query_pairs = queries.reshape(row_count, pair_count, 2, HD).transpose(1, 2, 0, 3)
    pair_numbers = jnp.arange(pair_count)

    def forward_pair(carried, inputs):
        pair_index, query_pair = inputs
        column_start = pair_index // pairs_per_group * HD
        key_blocks = lax.dynamic_slice_in_dim(key_all, column_start, HD, axis=2)
        value_blocks = lax.dynamic_slice_in_dim(value_all, column_start, HD, axis=2)
        scores = all_scores(query_pair, key_blocks, group_place, scale)
        row_top = jnp.max(scores, axis=2, keepdims=True)
        exponent = jnp.exp(scores - row_top)
        row_total = jnp.sum(exponent, axis=2, keepdims=True)
        probs_low = (exponent / row_total).astype(jnp.bfloat16)

        def weigh(offset):
            return jnp.einsum(
                "hqk,kd->hqd",
                probs_low[:, :, offset * row_count : (offset + 1) * row_count],
                value_blocks[offset],
                preferred_element_type=jnp.float32,
            )

        parts = block_list(weigh, GROUP, group_place, query_pair.shape)
        attended = parts[0]
        for extra in parts[1:]:
            attended = attended + extra
        return (carried, (attended, row_top, row_total))

    _, (attended, row_tops, row_totals) = lax.scan(forward_pair, None, (pair_numbers, query_pairs))
    mixed_low = (
        attended.transpose(2, 0, 1, 3).reshape(row_count, head_count * HD).astype(jnp.bfloat16)
    )
    middle = source + jnp.dot(mixed_low, out_weight, preferred_element_type=jnp.float32)
    mlp_full = (
        lax.all_gather(mlp_gain, "dev", axis=0, tiled=True),
        lax.all_gather(w_gate, "dev", axis=0, tiled=True),
        lax.all_gather(w_up, "dev", axis=0, tiled=True),
        lax.all_gather(w_down, "dev", axis=0, tiled=True),
    )
    gain_two, gate_weight, up_weight, down_weight = mlp_full
    scale_two = rms_scale(middle)
    normed_two = (middle * scale_two * gain_two.astype(jnp.float32)).astype(jnp.bfloat16)
    gate = jnp.dot(normed_two, gate_weight, preferred_element_type=jnp.float32)
    up_proj = jnp.dot(normed_two, up_weight, preferred_element_type=jnp.float32)
    sigmoid_gate = jax.nn.sigmoid(gate)
    silu_gate = gate * sigmoid_gate
    hidden = (silu_gate * up_proj).astype(jnp.bfloat16)
    output = (middle + jnp.dot(hidden, down_weight, preferred_element_type=jnp.float32)).astype(
        jnp.bfloat16
    )
    mlp_back = (
        lax.all_gather(mlp_gain, "dev", axis=0, tiled=True),
        lax.all_gather(w_gate, "dev", axis=0, tiled=True),
        lax.all_gather(w_up, "dev", axis=0, tiled=True),
        lax.all_gather(w_down, "dev", axis=0, tiled=True),
    )
    gain_back, gate_back, up_back, down_back = mlp_back
    down_sum = contract_rows(hidden, cotangent)
    hidden_grad = times_transposed(cotangent, down_back)
    gate_low = (hidden_grad * up_proj * sigmoid_gate * (1.0 + gate * (1.0 - sigmoid_gate))).astype(
        jnp.bfloat16
    )
    up_low = (hidden_grad * silu_gate).astype(jnp.bfloat16)
    gate_sum = contract_rows(normed_two, gate_low)
    up_sum = contract_rows(normed_two, up_low)
    normed_two_grad = times_transposed(gate_low, gate_back) + times_transposed(up_low, up_back)
    gain_two_sum = jnp.sum(normed_two_grad * middle * scale_two, axis=0)
    scaled_two = normed_two_grad * gain_back.astype(jnp.float32)
    middle_grad = (
        cotangent.astype(jnp.float32)
        + scale_two * scaled_two
        - middle * scale_two**3 * jnp.mean(scaled_two * middle, axis=1, keepdims=True)
    )
    mlp_sums = (
        lax.psum_scatter(gain_two_sum, "dev", scatter_dimension=0, tiled=True),
        lax.psum_scatter(gate_sum, "dev", scatter_dimension=0, tiled=True),
        lax.psum_scatter(up_sum, "dev", scatter_dimension=0, tiled=True),
        lax.psum_scatter(down_sum, "dev", scatter_dimension=0, tiled=True),
    )
    attn_back = (
        lax.all_gather(attn_gain, "dev", axis=0, tiled=True),
        lax.all_gather(w_query, "dev", axis=0, tiled=True),
        lax.all_gather(w_key, "dev", axis=0, tiled=True),
        lax.all_gather(w_value, "dev", axis=0, tiled=True),
        lax.all_gather(w_out, "dev", axis=0, tiled=True),
    )
    gain_one_back, query_back, key_back, value_back, out_back = attn_back
    branch_low = middle_grad.astype(jnp.bfloat16)
    out_sum = contract_rows(mixed_low, branch_low)
    mixed_grad = times_transposed(branch_low, out_back).astype(jnp.bfloat16)
    grad_pairs = mixed_grad.reshape(row_count, pair_count, 2, HD).transpose(1, 2, 0, 3)

    def backward_pair(carried, inputs):
        pair_index, query_pair, grad_pair, row_top, row_total = inputs
        column_start = pair_index // pairs_per_group * HD
        key_blocks = lax.dynamic_slice_in_dim(key_all, column_start, HD, axis=2)
        value_blocks = lax.dynamic_slice_in_dim(value_all, column_start, HD, axis=2)
        scores = all_scores(query_pair, key_blocks, group_place, scale)
        attn_probs = jnp.exp(scores - row_top) / row_total
        probs_low = attn_probs.astype(jnp.bfloat16)

        def probe(offset):
            return jnp.einsum(
                "hqd,kd->hqk", grad_pair, value_blocks[offset], preferred_element_type=jnp.float32
            )

        probs_grad = jnp.concatenate(
            block_list(probe, GROUP, group_place, (2, row_count, row_count)), axis=2
        )
        row_delta = jnp.sum(attn_probs * probs_grad, axis=2, keepdims=True)
        score_low = (attn_probs * (probs_grad - row_delta)).astype(jnp.bfloat16)

        def query_part(offset):
            return jnp.einsum(
                "hqk,kd->hqd",
                score_low[:, :, offset * row_count : (offset + 1) * row_count],
                key_blocks[offset],
                preferred_element_type=jnp.float32,
            )

        def key_part(offset):
            block_slice = slice(offset * row_count, (offset + 1) * row_count)
            key_term = (
                jnp.einsum(
                    "hqk,hqd->kd",
                    score_low[:, :, block_slice],
                    query_pair,
                    preferred_element_type=jnp.float32,
                )
                * scale
            )
            value_term = jnp.einsum(
                "hqk,hqd->kd",
                probs_low[:, :, block_slice],
                grad_pair,
                preferred_element_type=jnp.float32,
            )
            return jnp.stack([key_term, value_term])

        query_terms = block_list(query_part, GROUP, group_place, query_pair.shape)
        query_sum = query_terms[0]
        for extra in query_terms[1:]:
            query_sum = query_sum + extra
        kv_terms = jnp.stack(block_list(key_part, GROUP, group_place, (2, row_count, HD)))
        current = lax.dynamic_slice_in_dim(carried, column_start, HD, axis=3)
        carried = lax.dynamic_update_slice_in_dim(carried, current + kv_terms, column_start, axis=3)
        return (carried, query_sum * scale)

    kv_start = jnp.zeros((GROUP, 2, row_count, kv_heads * HD), jnp.float32)
    kv_sums, query_rot = lax.scan(
        backward_pair, kv_start, (pair_numbers, query_pairs, grad_pairs, row_tops, row_totals)
    )
    kv_total = kv_sums[0]
    for offset in range(1, GROUP):
        kv_total = kv_total + passed_along(
            kv_sums[offset].astype(jnp.bfloat16), "dev", -offset
        ).astype(jnp.float32)
    query_rot = query_rot.transpose(2, 0, 1, 3).reshape(row_count, head_count, HD)
    query_low = rotate_back(query_rot, cosine_table, sine_table).reshape(row_count, head_count * HD)
    query_low = query_low.astype(jnp.bfloat16)
    key_low = rotate_back(kv_total[0].reshape(row_count, kv_heads, HD), cosine_table, sine_table)
    key_low = key_low.reshape(row_count, kv_heads * HD).astype(jnp.bfloat16)
    value_low_grad = kv_total[1].astype(jnp.bfloat16)
    query_sum = contract_rows(normed_one, query_low)
    key_sum = contract_rows(normed_one, key_low)
    value_sum = contract_rows(normed_one, value_low_grad)
    normed_one_grad = (
        times_transposed(query_low, query_back)
        + times_transposed(key_low, key_back)
        + times_transposed(value_low_grad, value_back)
    )
    gain_one_sum = jnp.sum(normed_one_grad * source * scale_one, axis=0)
    scaled_one = normed_one_grad * gain_one_back.astype(jnp.float32)
    input_grad = (
        middle_grad
        + scale_one * scaled_one
        - source * scale_one**3 * jnp.mean(scaled_one * source, axis=1, keepdims=True)
    )
    attn_sums = (
        lax.psum_scatter(gain_one_sum, "dev", scatter_dimension=0, tiled=True),
        lax.psum_scatter(query_sum, "dev", scatter_dimension=0, tiled=True),
        lax.psum_scatter(key_sum, "dev", scatter_dimension=0, tiled=True),
        lax.psum_scatter(value_sum, "dev", scatter_dimension=0, tiled=True),
        lax.psum_scatter(out_sum, "dev", scatter_dimension=0, tiled=True),
    )
    return (
        output,
        input_grad.astype(jnp.bfloat16),
        attn_sums[0],
        attn_sums[1],
        attn_sums[2],
        attn_sums[3],
        attn_sums[4],
        mlp_sums[0],
        mlp_sums[1],
        mlp_sums[2],
        mlp_sums[3],
    )


def solution(mesh):
    return jax.shard_map(
        per_device,
        mesh=mesh,
        in_specs=(
            P("dev", None),
            P("dev"),
            P("dev", None),
            P("dev", None),
            P("dev", None),
            P("dev", None),
            P("dev"),
            P("dev", None),
            P("dev", None),
            P("dev", None),
            P("dev", None),
        ),
        out_specs=(
            P("dev", None),
            P("dev", None),
            P("dev"),
            P("dev", None),
            P("dev", None),
            P("dev", None),
            P("dev", None),
            P("dev"),
            P("dev", None),
            P("dev", None),
            P("dev", None),
        ),
        check_vma=False,
    )
```

profile of v0, /device:TPU:1, one launch (start us, length us, event | category | flops | bytes accessed | tf_op | source)
XLA Modules:
  0.0 3440.7 jit_solution(6105685459866484357)
XLA Ops:
  12.5 40.7 %all-reduce.5 = (bf16[2048]{0:T(1024)(128)(2,1)S(1)}, bf16[2048]{0:T(1024)(128)(2,1)S(1)}) all-reduce(bf16[2048]{0:T(1024)(128)(2,1)S(1)} %dynamic-update-slice, bf16[2048]{0:T(1024)(128)(2,1)S(1)} %dynamic-update-slice.1), channel_id=1, replica_groups=mesh['dev'=32] {'dev'}, use_global_device_ids=true, to_apply=%add | all-reduce | flops 4096 | bytes 16384
  54.4 12.9 all-gather.10.cloned.1.call-done
  69.3 53.5 %all-gather.12.cloned.1.call-done = bf16[2048,256]{1,0:T(8,128)(2,1)} async-done(((bf16[64,256]{1,0:T(8,128)(2,1)}), bf16[2048,256]{1,0:T(8,128)(2,1)}) %all-gather.12.cloned.1.call-update) | async-done | bytes 1048592 | tf_op jit(solution)/shard_map/all_gather | solution.py:118
  124.5 3.2 collective-permute-start.2
  130.1 3.5 collective-permute-start
  134.8 9.4 collective-permute-done.2
  146.4 61.3 %all-gather.8.cloned.1.call-done = bf16[2048,2048]{1,0:T(8,128)(2,1)} async-done(((bf16[64,2048]{1,0:T(8,128)(2,1)}), bf16[2048,2048]{1,0:T(8,128)(2,1)}) %all-gather.8.cloned.1.call-update) | async-done | bytes 8388624 | tf_op jit(solution)/shard_map/all_gather | solution.py:116
  207.7 6.8 fusion.124
  216.0 218.4 %while.32 = (s32[]{:T(128)}, bf16[16,2,256,64]{2,3,1,0:T(8,128)(2,1)}, f32[16,2,256,1]{2,1,3,0:T(2,128)}, f32[16,2,256,1]{2,1,3,0:T(2,128)}, bf16[16,2,256,64]{2...) while((s32[]{:T(128)}, ...), condition=%wide.region_19.20_spmd.clone, body=%wide.region_1.19_spmd.sunk.clone | while | flops 141327376 | bytes 23757288 | solution.py:176
  434.4 6.4 multiply_reduce_fusion.3
  441.2 14.4 fusion.127
  455.5 122.6 %all-gather.18.cloned.1.call-done = bf16[2048,5632]{1,0:T(8,128)(2,1)} async-done(((bf16[64,5632]{1,0:T(8,128)(2,1)}), bf16[2048,5632]{1,0:T(8,128)(2,1)}) %all-gather.18.cloned.1.call-update) | async-done | bytes 23068688 | tf_op jit(solution)/shard_map/all_gather | solution.py:184
  578.1 13.3 fusion.128
  591.4 132.4 %all-gather.20.cloned.1.call-done = bf16[5632,2048]{1,0:T(8,128)(2,1)} async-done(((bf16[176,2048]{1,0:T(8,128)(2,1)}), bf16[5632,2048]{1,0:T(8,128)(2,1)}) %all-gather.20.cloned.1.call-update) | async-done | bytes 23068688 | tf_op jit(solution)/shard_map/all_gather | solution.py:185
  723.8 18.9 multiply_convert_fusion.1
  742.7 12.6 fusion.129
  755.2 13.9 multiply_reduce_fusion.1
  772.7 5.7 convolution_convert_fusion
  781.3 366.0 %while.33 = (s32[]{:T(128)}, f32[4,2,256,256]{2,3,1,0:T(8,128)}, f32[16,2,256,64]{2,3,1,0:T(8,128)}, s32[16]{0:T(128)S(1)}, bf16[16,2,256,64]{2,3,1,0:T(8,128)(2...) while((s32[]{:T(128)}, f32[4,2,256,256]{2,3,1,0:T(8,128)}, ...), condition=%wide.region_48.49_spmd.clone, body=%wide.region_22.48_spmd.sunk.clone | while | flops 350750208 | bytes 53101248 | solution.py:297
  791.3 3.1 multiply_convert_fusion.7
  814.2 3.1 multiply_convert_fusion.7
  837.1 3.1 multiply_convert_fusion.7
  860.1 3.1 multiply_convert_fusion.7
  883.0 3.1 multiply_convert_fusion.7
  905.8 3.1 multiply_convert_fusion.7
  928.7 3.1 multiply_convert_fusion.7
  951.5 3.1 multiply_convert_fusion.7
  974.4 3.1 multiply_convert_fusion.7
  997.2 3.1 multiply_convert_fusion.7
  1020.1 3.1 multiply_convert_fusion.7
  1043.0 3.1 multiply_convert_fusion.7
  1153.8 3.2 collective-permute-done.5
  1156.9 137.8 %collective-permute-done.4 = bf16[2,256,256]{1,2,0:T(8,128)(2,1)S(1)} collective-permute-done((bf16[2,256,256]{1,2,0:T(8,128)(2,1)S(1)}, bf16[2,256,256]{1,2,0:T(8,128)(2,1)S(1)}, u32[]{:S(2)}, u32[]{:S(2)}) %collective-permute-start.4) | collective-permute-done | bytes 262176 | tf_op jit(solution)/shard_map/ppermute | solution.py:20
  1303.1 8.3 fusion.119
  1313.0 9.4 fusion.108
  1322.4 19.9 fusion.131
  1342.4 19.8 fusion.132
  1362.6 19.5 fusion.133
  1382.1 6.3 fusion.130
  1388.4 12.2 fusion.95
  1404.3 43.8 %all-reduce.4 = (f32[2048]{0:T(1024)S(1)}, f32[2048]{0:T(1024)S(1)}) all-reduce(f32[2048]{0:T(1024)S(1)} %get-tuple-element.696, f32[2048]{0:T(1024)S(1)} %copy-done.29), channel_id=2, replica_groups=mesh['dev'=32] {'dev'}, use_global_device_ids=true, to_apply=%region_51.52.clone | all-reduce | flops 4096 | bytes 32768
  1449.3 3.2 fusion.101
  1452.5 118.2 %reduce-scatter.12.cloned.1.call-done = f32[64,256]{1,0:T(8,128)} async-done(((f32[2048,256]{1,0:T(8,128)}), f32[64,256]{1,0:T(8,128)}) %reduce-scatter.12.cloned.1.call-update) | async-done | bytes 65552 | tf_op jit(solution)/shard_map/reduce_scatter | solution.py:330
  1570.7 187.2 %reduce-scatter.8.cloned.1.call-done = f32[64,2048]{1,0:T(8,128)} async-done(((f32[2048,2048]{1,0:T(8,128)}), f32[64,2048]{1,0:T(8,128)}) %reduce-scatter.8.cloned.1.call-update) | async-done | bytes 524304 | tf_op jit(solution)/shard_map/reduce_scatter | solution.py:328
  1757.8 187.4 %reduce-scatter.14.cloned.1.call-done = f32[64,2048]{1,0:T(8,128)} async-done(((f32[2048,2048]{1,0:T(8,128)}), f32[64,2048]{1,0:T(8,128)}) %reduce-scatter.14.cloned.1.call-update) | async-done | bytes 524304 | tf_op jit(solution)/shard_map/reduce_scatter | solution.py:331
  1945.2 496.7 %reduce-scatter.16.cloned.1.call-done = f32[64,5632]{1,0:T(8,128)} async-done(((f32[2048,5632]{1,0:T(8,128)}), f32[64,5632]{1,0:T(8,128)}) %reduce-scatter.16.cloned.1.call-update) | async-done | bytes 1441808 | tf_op jit(solution)/shard_map/reduce_scatter | solution.py:223
  2441.9 496.0 %reduce-scatter.18.cloned.1.call-done = f32[64,5632]{1,0:T(8,128)} async-done(((f32[2048,5632]{1,0:T(8,128)}), f32[64,5632]{1,0:T(8,128)}) %reduce-scatter.18.cloned.1.call-update) | async-done | bytes 1441808 | tf_op jit(solution)/shard_map/reduce_scatter | solution.py:224
  2937.9 495.8 %reduce-scatter.20.cloned.1.call-done = f32[176,2048]{1,0:T(8,128)} async-done(((f32[5632,2048]{1,0:T(8,128)}), f32[176,2048]{1,0:T(8,128)}) %reduce-scatter.20.cloned.1.call-update) | async-done | bytes 1441808 | tf_op jit(solution)/shard_map/reduce_scatter | solution.py:225
  (1490 shorter events, 592.6 us)
Async XLA Ops:
  7.2 4.8 copy-start.31
  7.2 5.1 copy-start.32
  7.2 46.0 %copy-start.1 = (bf16[256,2048]{1,0:T(8,128)(2,1)S(1)}, bf16[256,2048]{1,0:T(8,128)(2,1)}, u32[]{:S(2)}) copy-start(bf16[256,2048]{1,0:T(8,128)(2,1)} %param.51) | copy-start | bytes 3145732
  7.2 60.0 %all-gather.10.cloned.1.call-start = ((), (), s32[]{:S(2)}) async-start(), calls=%async_computation.8 | async-start | bytes 1081344 | tf_op jit(solution)/shard_map/all_gather | solution.py:117
  7.9 114.8 %all-gather.12.cloned.1.call-start = ((), (), s32[]{:S(2)}) async-start(), calls=%async_computation.9 | async-start | bytes 1081344 | tf_op jit(solution)/shard_map/all_gather | solution.py:118
  8.7 199.0 %all-gather.8.cloned.1.call-start = ((), (), s32[]{:S(2)}) async-start(), calls=%async_computation.7 | async-start | bytes 8650752 | tf_op jit(solution)/shard_map/all_gather | solution.py:116
  9.4 425.0 %all-gather.14.cloned.1.call-start = ((), (), s32[]{:S(2)}) async-start(), calls=%async_computation.10 | async-start | bytes 8650752 | tf_op jit(solution)/shard_map/all_gather | solution.py:119
  10.0 431.1 %all-gather.16.cloned.1.call-start = ((), (), s32[]{:S(2)}) async-start(), calls=%async_computation.11 | async-start | bytes 23789568 | tf_op jit(solution)/shard_map/all_gather | solution.py:183
  10.6 567.5 %all-gather.18.cloned.1.call-start = ((), (), s32[]{:S(2)}) async-start(), calls=%async_computation.12 | async-start | bytes 23789568 | tf_op jit(solution)/shard_map/all_gather | solution.py:184
  11.2 712.6 %all-gather.20.cloned.1.call-start = ((), (), s32[]{:S(2)}) async-start(), calls=%async_computation.13 | async-start | bytes 23789568 | tf_op jit(solution)/shard_map/all_gather | solution.py:185
  11.9 1440.6 %reduce-scatter.10.cloned.1.call-start = ((), (), s32[]{:S(2)}) async-start(), calls=%async_computation.15 | async-start | bytes 2162688 | tf_op jit(solution)/shard_map/reduce_scatter | solution.py:329
  53.2 154.5 %copy-start.25 = (f32[2048]{0:T(1024)}, f32[2048]{0:T(1024)S(1)}, u32[]{:S(2)}) copy-start(f32[2048]{0:T(1024)S(1)} %convert_element_type.180) | copy-start | bytes 24580
  54.1 153.6 %copy-start.27 = (f32[256]{0:T(256)}, f32[256]{0:T(256)S(1)}, u32[]{:S(2)}) copy-start(f32[256]{0:T(256)S(1)} %get-tuple-element.783) | copy-start | bytes 3076
  54.3 160.2 %copy-start.21 = (f32[256,32]{0,1:T(8,128)}, f32[256,32]{0,1:T(8,128)S(1)}, u32[]{:S(2)}) copy-start(f32[256,32]{0,1:T(8,128)S(1)} %get-tuple-element.780) | copy-start | bytes 98308
  54.3 160.2 %copy-start.23 = (f32[256,32]{0,1:T(8,128)}, f32[256,32]{0,1:T(8,128)S(1)}, u32[]{:S(2)}) copy-start(f32[256,32]{0,1:T(8,128)S(1)} %get-tuple-element.781) | copy-start | bytes 98308
  124.5 19.6 collective-permute-start.2
  127.8 16.4 collective-permute-start.1
  130.1 14.0 collective-permute-start
  440.8 328.3 %copy-start.6 = (f32[256,2048]{1,0:T(8,128)}, f32[256,2048]{1,0:T(8,128)S(1)}, u32[]{:S(2)}) copy-start(f32[256,2048]{1,0:T(8,128)S(1)} %get-tuple-element.787) | copy-start | bytes 6291460
  441.1 137.0 %copy-start.12 = (bf16[256,2048]{1,0:T(8,128)(2,1)}, bf16[256,2048]{1,0:T(8,128)(2,1)S(1)}, u32[]{:S(2)}) copy-start(bf16[256,2048]{1,0:T(8,128)(2,1)S(1)} %multiply_convert_fusion.4) | copy-start | bytes 3145732
  755.2 13.9 copy-start.15
  786.6 3.0 copy-start.9
  832.4 3.0 copy-start.9
  878.2 3.0 copy-start.9
  923.9 3.0 copy-start.9
  946.8 3.0 copy-start.9
  969.6 3.0 copy-start.9
  992.5 3.0 copy-start.9
  1038.2 3.0 copy-start.9
  1061.1 3.0 copy-start.9
  1149.0 147.0 %copy-start.22 = (f32[256,32]{0,1:T(8,128)S(1)}, f32[256,32]{0,1:T(8,128)}, u32[]{:S(2)}) copy-start(f32[256,32]{0,1:T(8,128)} %copy-done.21) | copy-start | bytes 98308
  1149.0 147.0 %copy-start.24 = (f32[256,32]{0,1:T(8,128)S(1)}, f32[256,32]{0,1:T(8,128)}, u32[]{:S(2)}) copy-start(f32[256,32]{0,1:T(8,128)} %copy-done.23) | copy-start | bytes 98308
  1149.0 147.0 %copy-start.2 = (bf16[256,2048]{1,0:T(8,128)(2,1)S(1)}, bf16[256,2048]{1,0:T(8,128)(2,1)}, u32[]{:S(2)}) copy-start(bf16[256,2048]{1,0:T(8,128)(2,1)} %param.51) | copy-start | bytes 3145732
  1149.0 147.0 %copy-start.26 = (f32[2048]{0:T(1024)S(1)}, f32[2048]{0:T(1024)}, u32[]{:S(2)}) copy-start(f32[2048]{0:T(1024)} %copy-done.25) | copy-start | bytes 24580
  1149.0 147.0 %copy-start.28 = (f32[256]{0:T(256)S(1)}, f32[256]{0:T(256)}, u32[]{:S(2)}) copy-start(f32[256]{0:T(256)} %copy-done.27) | copy-start | bytes 3076
  1149.1 7.8 collective-permute-start.5
  1150.5 144.2 %collective-permute-start.4 = (bf16[2,256,256]{1,2,0:T(8,128)(2,1)S(1)}, bf16[2,256,256]{1,2,0:T(8,128)(2,1)S(1)}, u32[]{:S(2)}, u32[]{:S(2)}) collective-permute-start(bf16[2,256,256]{1,2,0:T(8,128)(2,1)S(1)} %get-tuple-element.771), channel_id=1, source_target_pairs={{2,0},{3,1},{4,2},{5,3},{6,4},{7,5},{8,6},{9,7},{10,8},{11,9},{12,... | collective-permute-start | bytes 786440 | tf_op jit(solution)/shard_map/ppermute | solution.py:20
  1151.8 142.9 %collective-permute-start.3 = (bf16[2,256,256]{1,2,0:T(8,128)(2,1)S(1)}, bf16[2,256,256]{1,2,0:T(8,128)(2,1)S(1)}, u32[]{:S(2)}, u32[]{:S(2)}) collective-permute-start(bf16[2,256,256]{1,2,0:T(8,128)(2,1)S(1)} %get-tuple-element.769), channel_id=1, source_target_pairs={{1,0},{2,1},{3,2},{4,3},{5,4},{6,5},{7,6},{8,7},{9,8},{10,9},{11,1... | collective-permute-start | bytes 786440 | tf_op jit(solution)/shard_map/ppermute | solution.py:20
  1298.1 272.6 %reduce-scatter.12.cloned.1.call-start = ((), (), s32[]{:S(2)}) async-start(), calls=%async_computation.16 | async-start | bytes 2162688 | tf_op jit(solution)/shard_map/reduce_scatter | solution.py:330
  1300.1 457.7 %reduce-scatter.8.cloned.1.call-start = ((), (), s32[]{:S(2)}) async-start(), calls=%async_computation.14 | async-start | bytes 17301504 | tf_op jit(solution)/shard_map/reduce_scatter | solution.py:328
  1311.4 633.8 %reduce-scatter.14.cloned.1.call-start = ((), (), s32[]{:S(2)}) async-start(), calls=%async_computation.17 | async-start | bytes 17301504 | tf_op jit(solution)/shard_map/reduce_scatter | solution.py:331
  1322.4 1119.6 %reduce-scatter.16.cloned.1.call-start = ((), (), s32[]{:S(2)}) async-start(), calls=%async_computation.18 | async-start | bytes 47579136 | tf_op jit(solution)/shard_map/reduce_scatter | solution.py:223
  1342.4 1595.6 %reduce-scatter.18.cloned.1.call-start = ((), (), s32[]{:S(2)}) async-start(), calls=%async_computation.19 | async-start | bytes 47579136 | tf_op jit(solution)/shard_map/reduce_scatter | solution.py:224
  1362.3 2071.5 %reduce-scatter.20.cloned.1.call-start = ((), (), s32[]{:S(2)}) async-start(), calls=%async_computation.20 | async-start | bytes 47579136 | tf_op jit(solution)/shard_map/reduce_scatter | solution.py:225
  1382.1 6.3 copy-start.7
  1382.1 6.3 copy-start.13
  1388.4 12.2 copy-start.19
  1402.1 47.2 %copy-start.30 = (f32[256]{0:T(256)S(1)}, f32[256]{0:T(256)}, u32[]{:S(2)}) copy-start(f32[256]{0:T(256)} %get-tuple-element.782) | copy-start | bytes 3076
  (95 other events, 165.5 us)
Sparse Core Ops, SparseCore 0:
  10.9 56.2 all-gather.9
  70.1 52.6 all-gather.11
  125.6 82.0 all-gather.7
  210.4 76.1 all-gather.13
  289.3 143.3 all-gather.15
  435.4 142.6 all-gather.17
  581.0 142.7 all-gather.19
  1298.2 136.7 reduce-scatter.9
  1437.9 132.6 reduce-scatter.11
  1573.4 184.4 reduce-scatter.7
  1760.7 184.4 reduce-scatter.13
  1948.0 493.9 reduce-scatter.15
  2444.8 493.0 reduce-scatter.17
  2940.7 493.0 reduce-scatter.19
where the time goes:
time: 3460 us; the launch traced here: 3440 us
  waiting for transfers between devices  2520 us (73%)
  matrix products  354 us (10%)
  local copies, waits for them, and re-layouts  186 us (5%)
  other arithmetic  174 us (5%)
  loops' own time  94.4 us (3%)
  blocking collectives  84.4 us (2%)
    reduce_scatter x1, waiting for transfers between devices, per_device(): lax.psum_scatter(gate_sum, 'dev', scatter_dimension=0, tiled=True)  497 us
    reduce_scatter x1, waiting for transfers between devices, per_device(): lax.psum_scatter(up_sum, 'dev', scatter_dimension=0, tiled=True)  496 us
    reduce_scatter x1, waiting for transfers between devices, per_device(): lax.psum_scatter(down_sum, 'dev', scatter_dimension=0, tiled=True)  496 us
    reduce_scatter x1, waiting for transfers between devices, per_device(): lax.psum_scatter(out_sum, 'dev', scatter_dimension=0, tiled=True)  187 us
    reduce_scatter x1, waiting for transfers between devices, per_device(): lax.psum_scatter(query_sum, 'dev', scatter_dimension=0, tiled=True)  187 us
    ppermute x6, waiting for transfers between devices, passed_along(): return lax.ppermute(block, axis, route)  150 us
    all_gather x1, waiting for transfers between devices, per_device(): lax.all_gather(w_down, 'dev', axis=0, tiled=True)  132 us
    all_gather x1, waiting for transfers between devices, per_device(): lax.all_gather(w_up, 'dev', axis=0, tiled=True)  123 us
  transfers between devices with their start and end apart: 20, of which 14 were waited for; matrix products, arithmetic and copies ran while one was open for 9% of the time, Pallas kernels for 0%

commit v1 on v0

v1 whole, which is shorter than its diff:
```python
import functools

import jax
import jax.numpy as jnp
from jax import lax
from jax.experimental import pallas as pl
from jax.experimental.pallas import tpu as pltpu
from jax.sharding import PartitionSpec as P

HD = 64
RANKS = 8
GROUP = 4
EPS = 1e-05
THETA = 10000.0
NEG = -1e30
F32 = jnp.float32
BF16 = jnp.bfloat16


def swap(block, bit):
    n = lax.axis_size("dev")
    return lax.ppermute(block, "dev", [(i, i ^ bit) for i in range(n)])


def onward(block):
    n = lax.axis_size("dev")
    return lax.ppermute(block, "dev", [(i, (i + RANKS) % n) for i in range(n)])


def plane_groups():
    n = lax.axis_size("dev")
    return [[p * RANKS + r for r in range(RANKS)] for p in range(n // RANKS)]


def exchange(blocks):
    return lax.all_to_all(
        blocks, "dev", split_axis=0, concat_axis=0, tiled=True, axis_index_groups=plane_groups()
    )


def gather_tokens(block):
    half = block.shape[0] // 2
    one, two, four = swap(block, 1), swap(block, 2), swap(block, 4)
    three, five = swap(two, 1), swap(four, 1)
    six = (swap(two[:half], 4), swap(four[half:], 2))
    seven = tuple(swap(part, 1) for part in six)
    return jnp.concatenate([block, one, two, three, four, five, *six, *seven])


def reduce_tokens(far, near):
    rows = near.shape[0] // 4
    half = rows // 2
    four, five, six, seven = (far[i * rows : (i + 1) * rows] for i in range(4))
    zero, one, two, three = (near[i * rows : (i + 1) * rows] for i in range(4))
    wide = lambda v: v.astype(F32)
    thin = lambda v: v.astype(BF16)
    six = thin(wide(six) + wide(swap(seven, 1)))
    for_four, for_two = swap(six[:half], 2), swap(six[half:], 4)
    four = wide(four) + wide(swap(five, 1))
    two = wide(two) + wide(swap(three, 1))
    two_top, four_low = swap(thin(two[:half]), 2), swap(thin(four[half:]), 4)
    two_low = swap(thin(two[half:] + wide(for_two)), 2)
    four_top = swap(thin(four[:half] + wide(for_four)), 4)
    zero = wide(zero) + wide(swap(one, 1))
    others = jnp.concatenate([wide(two_top) + wide(four_top), wide(two_low) + wide(four_low)])
    return zero + others


def ring_gather(block, plane, planes):
    rows = block.shape[0]
    whole = jnp.zeros((planes * rows, block.shape[1]), block.dtype)
    for step in range(planes):
        place = lax.rem(plane + planes - step, planes)
        whole = lax.dynamic_update_slice_in_dim(whole, block, place * rows, 0)
        if step < planes - 1:
            block = onward(block)
    return whole


def gather_gains(gains, me, plane, planes):
    bit = 1
    while bit < RANKS:
        other = swap(gains, bit)
        gains = jnp.where(
            me & bit,
            jnp.concatenate([other, gains], axis=1),
            jnp.concatenate([gains, other], axis=1),
        )
        bit *= 2
    whole = ring_gather(gains, plane, planes)
    return whole.reshape(planes, 2, -1).transpose(1, 0, 2).reshape(2, -1)


def ring_reduce(terms, plane, planes):
    rows = terms.shape[0] // planes

    def part(place):
        return lax.dynamic_slice_in_dim(terms, place * rows, rows, 0)

    total = part(lax.rem(plane + planes - 1, planes))
    for step in range(planes - 1):
        arrived = onward(total.astype(BF16))
        place = lax.rem(plane + 2 * planes - 2 - step, planes)
        total = part(place) + arrived.astype(F32)
    return total


def dot(left, right):
    return jnp.dot(left, right, preferred_element_type=F32)


def contract_rows(left, right):
    return lax.dot_general(left, right, (((0,), (0,)), ((), ())), preferred_element_type=F32)


def times_transposed(left, right):
    return lax.dot_general(left, right, (((1,), (1,)), ((), ())), preferred_element_type=F32)


def rms_scale(values):
    return lax.rsqrt(jnp.mean(values * values, axis=1, keepdims=True) + EPS)


def rope_tables(length):
    lanes = jnp.arange(2 * HD)
    frequency = THETA ** (-((lanes % (HD // 2)).astype(F32) * 2.0 / HD))
    angles = jnp.arange(length).astype(F32)[:, None] * frequency[None, :]
    sign = jnp.where(lanes % HD < HD // 2, -1.0, 1.0)
    return jnp.cos(angles), jnp.sin(angles) * sign[None, :]


def partner(values):
    lane = lax.broadcasted_iota(jnp.int32, values.shape, 1)
    ahead = pltpu.roll(values, 2 * HD - HD // 2, 1)
    behind = pltpu.roll(values, HD // 2, 1)
    return jnp.where(lane % HD < HD // 2, ahead, behind)


def forward_kernel(heads, rows, m_ref, qkv_ref, cos_ref, sin_ref, mixed_ref, qt_ref, kv_ref, lse_ref):
    mine = m_ref[0]
    width = heads * HD
    blocks = GROUP
    is_key = lax.broadcasted_iota(jnp.int32, (rows, 2 * HD), 1) < HD
    for p in range(blocks):
        span = slice(p * rows, (p + 1) * rows)
        qkv = qkv_ref[0, p ^ mine]
        cosine, sine = cos_ref[span, :], sin_ref[span, :]
        turned = []
        for start in range(0, width, 2 * HD):
            part = qkv[:, start : start + 2 * HD]
            turned.append(part * cosine + partner(part) * sine)
        query = jnp.concatenate(turned, axis=1) * HD ** (-0.5)
        qt_ref[0, :, span] = query.T.astype(BF16)
        part = qkv[:, width : width + 2 * HD]
        kv_ref[0, span, :] = jnp.where(
            is_key, part * cosine + partner(part) * sine, part
        ).astype(BF16)
    kv = kv_ref[0]
    vt = kv.astype(F32).T.astype(BF16)[HD:, :]
    keys = kv[:, :HD]
    ok = lax.broadcasted_iota(jnp.int32, (rows, rows), 0) <= lax.broadcasted_iota(
        jnp.int32, (rows, rows), 1
    )
    for p in range(blocks):
        span = slice(p * rows, (p + 1) * rows)
        outs, tops = [], []
        for h in range(heads):
            query = qt_ref[0, h * HD : (h + 1) * HD, span]
            last = jnp.where(ok, dot(keys[span], query), NEG)
            top = jnp.max(last, axis=0, keepdims=True)
            if p:
                first = dot(keys[: p * rows], query)
                top = jnp.maximum(top, jnp.max(first, axis=0, keepdims=True))
            weight = jnp.exp(last - top)
            total = jnp.sum(weight, axis=0, keepdims=True)
            if p:
                first = jnp.exp(first - top)
                total = total + jnp.sum(first, axis=0, keepdims=True)
            share = 1.0 / total
            out = dot(vt[:, span], (weight * share).astype(BF16))
            if p:
                out = out + dot(vt[:, : p * rows], (first * share).astype(BF16))
            outs.append(out)
            tops.append(top + jnp.log(total))
        mixed_ref[0, p ^ mine] = jnp.concatenate(outs, axis=0).T.astype(BF16)
        tops += [tops[0]] * (8 - heads)
        lse_ref[0, :, span] = jnp.concatenate(tops, axis=0)


def backward_kernel(
    heads, rows, m_ref, qt_ref, kv_ref, lse_ref, mg_ref, cos_ref, sin_ref, dq_ref, dkv_ref, dk_sum, dv_sum
):
    mine = m_ref[0]
    width = heads * HD
    blocks = GROUP
    kv = kv_ref[0]
    kt = kv.astype(F32).T.astype(BF16)[:HD, :]
    keys = kv[:, :HD]
    values = pltpu.roll(kv.astype(F32), HD, 1).astype(BF16)[:, :HD]
    ok = lax.broadcasted_iota(jnp.int32, (rows, rows), 0) <= lax.broadcasted_iota(
        jnp.int32, (rows, rows), 1
    )
    for p in reversed(range(blocks)):
        span = slice(p * rows, (p + 1) * rows)
        reach = (p + 1) * rows
        grad = mg_ref[0, p ^ mine].astype(F32).T.astype(BF16)
        dqs = []
        for h in range(heads):
            query = qt_ref[0, h * HD : (h + 1) * HD, span]
            above = grad[h * HD : (h + 1) * HD, :]
            lse = lse_ref[0, h : h + 1, span]
            scores = dot(keys[:reach], query)
            if p:
                scores = jnp.concatenate(
                    [scores[: p * rows], jnp.where(ok, scores[p * rows :], NEG)], axis=0
                )
            else:
                scores = jnp.where(ok, scores, NEG)
            probs = jnp.exp(scores - lse)
            probs_grad = dot(values[:reach], above)
            delta = jnp.sum(probs * probs_grad, axis=0, keepdims=True)
            score_low = (probs * (probs_grad - delta)).astype(BF16)
            dk = times_transposed(score_low, query)
            dv = times_transposed(probs.astype(BF16), above)
            if p == blocks - 1 and h == 0:
                dk_sum[...] = dk
                dv_sum[...] = dv
            else:
                dk_sum[:reach, :] += dk
                dv_sum[:reach, :] += dv
            dqs.append(dot(kt[:, :reach], score_low))
        dq = jnp.concatenate(dqs, axis=0).T * HD ** (-0.5)
        cosine, sine = cos_ref[span, :], sin_ref[span, :]
        turned = []
        for start in range(0, width, 2 * HD):
            part = dq[:, start : start + 2 * HD]
            turned.append(part * cosine - partner(part) * sine)
        dq_ref[0, p ^ mine] = jnp.concatenate(turned, axis=1).astype(BF16)
    is_key = lax.broadcasted_iota(jnp.int32, (rows, 2 * HD), 1) < HD
    for p in range(blocks):
        span = slice(p * rows, (p + 1) * rows)
        part = jnp.concatenate([dk_sum[span, :], dv_sum[span, :]], axis=1)
        cosine, sine = cos_ref[span, :], sin_ref[span, :]
        dkv_ref[0, p ^ mine] = jnp.where(is_key, part * cosine - partner(part) * sine, part)


def whole_spec(shape):
    zeros = (0,) * (len(shape) - 1)
    return pl.BlockSpec((1,) + shape[1:], lambda s, m: (s,) + zeros)


def same_spec(shape):
    zeros = (0,) * len(shape)
    return pl.BlockSpec(shape, lambda s, m: zeros)


def attend(qkv, tables, mine, heads):
    seqs, _, rows, cols = qkv.shape
    length = GROUP * rows
    width = heads * HD
    shapes = (
        ((seqs, GROUP, rows, width), BF16),
        ((seqs, width, length), BF16),
        ((seqs, length, 2 * HD), BF16),
        ((seqs, 8, length), F32),
    )
    return pl.pallas_call(
        functools.partial(forward_kernel, heads, rows),
        grid_spec=pltpu.PrefetchScalarGridSpec(
            num_scalar_prefetch=1,
            grid=(seqs,),
            in_specs=[whole_spec(qkv.shape), same_spec(tables[0].shape), same_spec(tables[1].shape)],
            out_specs=[whole_spec(shape) for shape, _ in shapes],
        ),
        out_shape=[jax.ShapeDtypeStruct(shape, dtype) for shape, dtype in shapes],
        compiler_params=pltpu.CompilerParams(vmem_limit_bytes=48 * 2**20),
        cost_estimate=pl.CostEstimate(
            flops=seqs * heads * length * length * HD * 8, bytes_accessed=8 * 2**20, transcendentals=seqs * heads * length * length
        ),
        name="attend",
    )(mine, qkv, *tables)


def attend_back(kept, grads, tables, mine, heads):
    queries, kv, lse = kept
    seqs, _, rows, width = grads.shape
    length = GROUP * rows
    shapes = (((seqs, GROUP, rows, width), BF16), ((seqs, GROUP, rows, 2 * HD), F32))
    ins = (queries, kv, lse, grads)
    return pl.pallas_call(
        functools.partial(backward_kernel, heads, rows),
        grid_spec=pltpu.PrefetchScalarGridSpec(
            num_scalar_prefetch=1,
            grid=(seqs,),
            in_specs=[whole_spec(v.shape) for v in ins]
            + [same_spec(tables[0].shape), same_spec(tables[1].shape)],
            out_specs=[whole_spec(shape) for shape, _ in shapes],
            scratch_shapes=[pltpu.VMEM((length, HD), F32), pltpu.VMEM((length, HD), F32)],
        ),
        out_shape=[jax.ShapeDtypeStruct(shape, dtype) for shape, dtype in shapes],
        compiler_params=pltpu.CompilerParams(vmem_limit_bytes=48 * 2**20),
        cost_estimate=pl.CostEstimate(
            flops=seqs * heads * length * length * HD * 20, bytes_accessed=8 * 2**20, transcendentals=seqs * heads * length * length
        ),
        name="attend_back",
    )(mine, *ins, *tables)


def per_device(
    tokens, attn_gain, w_query, w_key, w_value, w_out, mlp_gain, w_gate, w_up, w_down, cotangent
):
    n = lax.axis_size("dev")
    planes = n // RANKS
    me = lax.axis_index("dev")
    plane, rank = me // RANKS, lax.rem(me, RANKS)
    core = lax.rem(me, 2)
    mine = lax.rem(me, GROUP).astype(jnp.int32).reshape(1)
    count, model = tokens.shape
    local = w_query.shape[0]
    heads = w_query.shape[1] // HD // RANKS
    kv_heads = w_key.shape[1] // HD
    width = heads * HD
    units = w_gate.shape[1] // n
    own_units = units * planes
    seqs = RANKS // GROUP
    share = RANKS // kv_heads

    def by_kv(weight):
        parts = weight.reshape(local, kv_heads, 1, HD)
        return jnp.broadcast_to(parts, (local, kv_heads, share, HD)).reshape(local, RANKS, HD)

    def by_unit(weight):
        parts = weight.reshape(local, planes, RANKS, units)
        return parts.transpose(2, 0, 1, 3).reshape(RANKS, local, own_units)

    attn_parts = jnp.concatenate(
        [
            w_query.reshape(local, RANKS, width),
            by_kv(w_key),
            by_kv(w_value),
        ],
        axis=2,
    ).transpose(1, 0, 2)
    attn_cols = width + 2 * HD
    attn_own = exchange(attn_parts).reshape(RANKS * local, attn_cols)
    attn_weight = ring_gather(attn_own, plane, planes)

    gains = gather_gains(jnp.stack([attn_gain, mlp_gain]), me, plane, planes)
    gain_one, gain_two = gains[:1].astype(F32), gains[1:].astype(F32)
    source = tokens.astype(F32)
    scale_one = rms_scale(source)
    plane_source = gather_tokens(tokens).astype(F32)
    normed_one = (plane_source * rms_scale(plane_source) * gain_one).astype(BF16)

    to_rank = [(i, (i % planes) * RANKS + i // planes) for i in range(n)]
    from_rank = [(j, i) for i, j in to_rank]
    out_own = lax.ppermute(w_out, "dev", to_rank)
    out_weight = ring_gather(out_own, plane, planes)

    mlp_parts = jnp.concatenate([by_unit(w_gate), by_unit(w_up)], axis=2)
    mlp_own = exchange(mlp_parts).reshape(RANKS * local, 2 * own_units)
    mlp_weight = ring_gather(mlp_own, plane, planes)
    down_weight = ring_gather(w_down, plane, planes)
    above = gather_tokens(cotangent)

    tables = rope_tables(GROUP * count)
    qkv = dot(normed_one, attn_weight).reshape(seqs, GROUP, count, attn_cols)
    mixed, queries, kv, lse = attend(qkv, tables, mine, heads)
    mixed = mixed.reshape(RANKS * count, width)
    split = GROUP * count

    def summed(left, right):
        far = dot(left[split:], right).astype(BF16)
        near = dot(left[:split], right).astype(BF16)
        return reduce_tokens(far, near)

    def summed_transposed(left, right):
        far = times_transposed(left[split:], right).astype(BF16)
        near = times_transposed(left[:split], right).astype(BF16)
        return reduce_tokens(far, near)

    middle = source + summed(mixed, out_weight)

    scale_two = rms_scale(middle)
    normed_two = gather_tokens((middle * scale_two * gain_two).astype(BF16))
    gate_up = dot(normed_two, mlp_weight)
    gate, up_proj = gate_up[:, :own_units], gate_up[:, own_units:]
    sigmoid_gate = jax.nn.sigmoid(gate)
    silu_gate = gate * sigmoid_gate
    hidden = (silu_gate * up_proj).astype(BF16)
    output = (middle + summed(hidden, down_weight)).astype(BF16)

    down_grad = ring_reduce(contract_rows(hidden, above), plane, planes)
    hidden_grad = times_transposed(above, down_weight)
    gate_low = hidden_grad * up_proj * sigmoid_gate * (1.0 + gate * (1.0 - sigmoid_gate))
    both_low = jnp.concatenate([gate_low.astype(BF16), (hidden_grad * silu_gate).astype(BF16)], axis=1)
    scaled_two = summed_transposed(both_low, mlp_weight) * gain_two
    mlp_total = ring_reduce(contract_rows(normed_two, both_low), plane, planes)
    middle_grad = (
        cotangent.astype(F32)
        + scale_two * scaled_two
        - middle * scale_two**3 * jnp.mean(scaled_two * middle, axis=1, keepdims=True)
    )

    branch = gather_tokens(middle_grad.astype(BF16))
    mixed_grad = times_transposed(branch, out_weight).astype(BF16)
    out_total = ring_reduce(contract_rows(mixed, branch), plane, planes)
    out_grad = lax.ppermute(out_total, "dev", from_rank)
    query_low, dkv = attend_back(
        (queries, kv, lse), mixed_grad.reshape(seqs, GROUP, count, width), tables, mine, heads
    )
    query_low = query_low.reshape(RANKS * count, width)
    dkv = dkv.reshape(RANKS * count, 2 * HD)
    dk, dv = dkv[:, :HD], dkv[:, HD:]
    kept = jnp.where(core == 0, dk, dv)
    sent = swap(jnp.where(core == 0, dv, dk), 1).reshape(-1, 2, count, HD)
    kv_low = (kept + sent[:, ::-1].reshape(kept.shape)).astype(BF16)
    all_low = jnp.concatenate([query_low, kv_low], axis=1)
    back_weight = jnp.concatenate(
        [
            attn_weight[:, :width],
            jnp.where(core == 0, attn_weight[:, width : width + HD], attn_weight[:, width + HD :]),
        ],
        axis=1,
    )
    attn_total = ring_reduce(contract_rows(normed_one, all_low), plane, planes)
    scaled_one = summed_transposed(all_low, back_weight) * gain_one
    input_grad = (
        middle_grad
        + scale_one * scaled_one
        - source * scale_one**3 * jnp.mean(scaled_one * source, axis=1, keepdims=True)
    )

    mlp_back = exchange(mlp_total.astype(BF16).reshape(RANKS, local, 2 * own_units)).astype(F32)

    def in_order(parts):
        parts = parts.reshape(RANKS, local, planes, units).transpose(1, 2, 0, 3)
        return parts.reshape(local, n * units)

    gate_raw = in_order(mlp_back[:, :, :own_units])
    up_raw = in_order(mlp_back[:, :, own_units:])
    mlp_gain_grad = jnp.sum(gate_raw * w_gate, axis=1) + jnp.sum(up_raw * w_up, axis=1)
    mlp_gain_grad = mlp_gain_grad / mlp_gain

    attn_back = exchange(attn_total.astype(BF16).reshape(RANKS, local, width + HD)).astype(F32)
    query_raw = attn_back[:, :, :width].transpose(1, 0, 2).reshape(local, RANKS * width)
    shared = attn_back[:, :, width:].reshape(kv_heads, share, local, HD)
    key_raw = shared[:, 0].transpose(1, 0, 2).reshape(local, kv_heads * HD)
    value_raw = shared[:, 1].transpose(1, 0, 2).reshape(local, kv_heads * HD)
    attn_gain_grad = (
        jnp.sum(query_raw * w_query, axis=1)
        + jnp.sum(key_raw * w_key, axis=1)
        + jnp.sum(value_raw * w_value, axis=1)
    ) / attn_gain
    return (
        output,
        input_grad.astype(BF16),
        attn_gain_grad,
        query_raw,
        key_raw,
        value_raw,
        out_grad,
        mlp_gain_grad,
        gate_raw,
        up_raw,
        down_grad,
    )


def solution(mesh):
    row, vec = P("dev", None), P("dev")
    return jax.shard_map(
        per_device,
        mesh=mesh,
        in_specs=(row, vec, row, row, row, row, vec, row, row, row, row),
        out_specs=(row, row, vec, row, row, row, row, vec, row, row, row),
        check_vma=False,
    )
```

time: 3460 us -> 846 us (0.24)
  waiting for transfers between devices: 2520 us -> 295 us
  matrix products: 354 us -> 125 us
  starting transfers between devices: 14.8 us -> 149 us
  other arithmetic: 174 us -> 77.5 us
  loops' own time: 94.4 us -> 0 us
  blocking collectives: 84.4 us -> 0 us
  local copies, waits for them, and re-layouts: 186 us -> 146 us
  Pallas kernels: 0 us -> 37.9 us
    reduce_scatter x7 -> x0, waiting for transfers between devices: 1980 us -> none  [the longest x1 497 us: per_device(): lax.psum_scatter(gate_sum, 'dev', scatter_dimension=0, tiled=True)]
    all_gather x7 -> x0, waiting for transfers between devices: 383 us -> none  [the longest x1 132 us: per_device(): lax.all_gather(w_down, 'dev', axis=0, tiled=True)]
    dot_general x215 -> x6, matrix products: 209 us -> 41 us  [dot(): return jnp.dot(left, right, preferred_element_type=F32)]
    ppermute x6 -> x109, waiting for transfers between devices: 150 us -> 295 us  [the longest x27 151 us: onward(): return lax.ppermute(block, 'dev', [(i, (i + RANKS) % n) for i in range(n)])]
    ppermute x6 -> x109, starting transfers between devices: 13.7 us -> 120 us  [the longest x80 105 us: swap(): return lax.ppermute(block, 'dev', [(i, i ^ bit) for i in range(n)])]
    another operation x290 -> x0, loops' own time: 94.4 us -> none  [the longest x1 45.1 us: per_device(): lax.scan(backward_pair, kv_start, (pair_numbers, query_pairs, grad_pairs,...]
    unnamed x2 -> x0, blocking collectives: 84.4 us -> none
    sub x17 -> x0, other arithmetic: 52.3 us -> none  [the longest x16 50.1 us: backward_pair(): score_low = (attn_probs * (probs_grad - row_delta)).astype(jnp.bfloat16)]
  transfers between devices with their start and end apart: 20 -> 113, of which waited for: 14 -> 39; matrix products, arithmetic and copies ran while one was open for 9% -> 27% of each run, Pallas kernels for 0% -> 5%
where the time goes in v1:
time: 846 us; the launch traced here: 833 us
  waiting for transfers between devices  295 us (35%)
  starting transfers between devices  149 us (18%)
  local copies, waits for them, and re-layouts  146 us (17%)
  matrix products  125 us (15%)
  other arithmetic  77.5 us (9%)
  Pallas kernels  37.9 us (4%)
    ppermute x27, waiting for transfers between devices, onward(): return lax.ppermute(block, 'dev', [(i, (i + RANKS) % n) for i in range(n)])  151 us
    ppermute x80, waiting for transfers between devices, swap(): return lax.ppermute(block, 'dev', [(i, i ^ bit) for i in range(n)])  113 us
    ppermute x80, starting transfers between devices, swap(): return lax.ppermute(block, 'dev', [(i, i ^ bit) for i in range(n)])  105 us
    unnamed x173, local copies, waits for them, and re-layouts  51.6 us
    dot_general x6, matrix products, times_transposed(): lax.dot_general(left, right, (((1,), (1,)), ((), ())), preferred_element_...  49.5 us
    dot_general x6, matrix products, dot(): return jnp.dot(left, right, preferred_element_type=F32)  41 us
    dot_general x4, matrix products, contract_rows(): lax.dot_general(left, right, (((0,), (0,)), ((), ())), preferred_element_...  34.7 us
    all_to_all x4, starting transfers between devices, exchange(): lax.all_to_all(blocks, 'dev', split_axis=0, concat_axis=0, tiled=True, ax...  28.5 us
  transfers between devices with their start and end apart: 113, of which 39 were waited for; matrix products, arithmetic and copies ran while one was open for 27% of the time, Pallas kernels for 5%

profile of v1, /device:TPU:1, one launch (start us, length us, event | category | flops | bytes accessed | tf_op | source)
XLA Modules:
  0.0 832.5 jit_solution(17327614019268981307)
XLA Ops:
  43.3 4.2 collective-permute-done.13
  47.5 4.2 collective-permute-done.14
  51.7 5.4 collective-permute-start.18
  57.2 7.8 collective-permute-done.18
  66.1 16.0 %all-to-all-start.1 = ((bf16[8,64,1408]{2,1,0:T(8,128)(2,1)}), bf16[8,64,1408]{2,1,0:T(8,128)(2,1)}, u32[]{:S(2)}, u32[]{:S(2)}) async-start(bf16[8,64,1408]{2,1,0:T(8,128)(2,1)} %pad_maximum_fusion.4), calls=%async_computation.1 | async-start | bytes 2883584 | tf_op jit(solution)/shard_map/all_to_all | solution.py:36
  90.5 8.9 %collective-permute-done.15 = bf16[512,384]{0,1:T(8,128)(2,1)S(1)} collective-permute-done((bf16[512,384]{0,1:T(8,128)(2,1)}, bf16[512,384]{0,1:T(8,128)(2,1)S(1)}, u32[]{:S(2)}, u32[]{:S(2)}) %collective-permute-start.15) | collective-permute-done | bytes 393248 | tf_op jit(solution)/shard_map/ppermute | solution.py:27
  100.3 4.8 collective-permute-done.20
  117.3 5.1 collective-permute-done.1
  129.3 22.5 %collective-permute-done.3 = bf16[256,2048]{1,0:T(8,128)(2,1)} collective-permute-done((bf16[256,2048]{1,0:T(8,128)(2,1)S(1)}, bf16[256,2048]{1,0:T(8,128)(2,1)}, u32[]{:S(2)}, u32[]{:S(2)}) %collective-permute-start.3) | collective-permute-done | bytes 1048608 | tf_op jit(solution)/shard_map/ppermute | solution.py:22
  167.7 4.5 collective-permute-done.17
  179.0 6.9 collective-permute-done.6
  192.9 7.7 fusion.11
  200.6 16.9 %attend.1 = (bf16[2,4,256,256]{3,2,1,0:T(8,128)(2,1)S(1)}, bf16[2,256,1024]{2,1,0:T(8,128)(2,1)S(1)}, bf16[2,1024,128]{2,1,0:T(8,128)(2,1)S(1)}, f32[2,8,1024]{2,1,0:T(8,128)S(1)}) custom-call(s32[1]{0:T(128)} %bitcast.m_ref, f32[2,4,256,384]{3,2,1,0:T(8,128)} %bitcast.111, f32[1024,128]{1,0:T(8,128)S(1)} %get-tuple-element.82.cos_ref, ...), custom_call_target="tpu_custom_call" | custom-call | flops 4294967296 | bytes 8388608 | tf_op jit(solution)/shard_map/attend/pallas_call | solution.py:267
  229.2 10.0 %collective-permute-done.27 = bf16[128,2048]{1,0:T(8,128)(2,1)S(1)} collective-permute-done((bf16[128,2048]{1,0:T(8,128)(2,1)S(1)}, bf16[128,2048]{1,0:T(8,128)(2,1)S(1)}, u32[]{:S(2)}, u32[]{:S(2)}) %collective-permute-start.27) | collective-permute-done | bytes 524320 | tf_op jit(solution)/shard_map/ppermute | solution.py:22
  242.0 9.1 %collective-permute-done.29 = bf16[128,2048]{1,0:T(8,128)(2,1)S(1)} collective-permute-done((bf16[128,2048]{1,0:T(8,128)(2,1)S(1)}, bf16[128,2048]{1,0:T(8,128)(2,1)S(1)}, u32[]{:S(2)}, u32[]{:S(2)}) %collective-permute-start.29) | collective-permute-done | bytes 524320 | tf_op jit(solution)/shard_map/ppermute | solution.py:22
  252.7 4.8 collective-permute-start.22
  257.6 4.8 collective-permute-done.28
  265.9 4.8 collective-permute-start.64
  282.8 28.8 %collective-permute-done.42 = bf16[512,1408]{1,0:T(8,128)(2,1)S(1)} collective-permute-done((bf16[512,1408]{1,0:T(8,128)(2,1)S(1)}, bf16[512,1408]{1,0:T(8,128)(2,1)S(1)}, u32[]{:S(2)}, u32[]{:S(2)}) %collective-permute-start.42) | collective-permute-done | bytes 1441824 | tf_op jit(solution)/shard_map/ppermute | solution.py:27
  313.7 6.5 collective-permute-start.34
  323.3 18.4 %collective-permute-done.43 = bf16[512,1408]{1,0:T(8,128)(2,1)S(1)} collective-permute-done((bf16[512,1408]{1,0:T(8,128)(2,1)S(1)}, bf16[512,1408]{1,0:T(8,128)(2,1)S(1)}, u32[]{:S(2)}, u32[]{:S(2)}) %collective-permute-start.43) | collective-permute-done | bytes 1441824 | tf_op jit(solution)/shard_map/ppermute | solution.py:27
  341.9 6.6 collective-permute-start.40
  355.2 17.4 %fusion.62 = f32[2048,1408]{0,1:T(8,128)} fusion(bf16[2048,2048]{1,0:T(8,128)(2,1)} %constant_dynamic-update-slice_fusion.10, bf16[2048,1408]{1,0:T(8,128)(2,1)S(1)} %constant_dynamic-update-slice_fusion.44), kind=kOutput, calls=%fused_computation.244 | convolution fusion | flops 11811160064 | bytes 25690112 | tf_op jit(solution)/shard_map/dot_general | solution.py:109
  372.6 16.4 %multiply_convert_fusion = (bf16[2048,704]{0,1:T(8,128)(2,1)S(1)}, bf16[2048,704]{0,1:T(8,128)(2,1)S(1)}, bf16[2048,704]{0,1:T(8,128)(2,1)}) fusion(f32[2048,1408]{0,1:T(8,128)} %fusion.62, bf16[2048,2048]{1,0:T(8,128)(2,1)} %constant_dynamic-update-slice_fusion.20, bf16[704,2048]{1,0:T(8,128)(2,1)} %constant_dynamic-update-slice_fusion.40), kind=kOutput, calls=%fused_computation.11 | convolution fusion | flops 5927206912 | bytes 31457280 | tf_op jit(solution)/shard_map/dot_general | solution.py:117
  391.4 15.9 %fusion.3 = f32[2048,1408]{1,0:T(8,128)S(1)} fusion(bf16[2048,2048]{1,0:T(8,128)(2,1)} %constant_dynamic-update-slice_fusion.10, bf16[2048,704]{0,1:T(8,128)(2,1)S(1)} %get-tuple-element.34, bf16[2048,704]{0,1:T(8,128)(2,1)S(1)} %get-tuple-element.35), kind=kOutput, calls=%fused_computation.10 | convolution fusion | flops 11822694400 | bytes 25690112 | tf_op jit(solution)/shard_map/dot_general | solution.py:113
  407.4 14.2 %convolution_convert_fusion.3 = bf16[1024,2048]{1,0:T(8,128)(2,1)S(1)} fusion(bf16[2048,1408]{1,0:T(8,128)(2,1)} %copy-done.22, bf16[2048,704]{0,1:T(8,128)(2,1)} %copy-done.64, bf16[2048,704]{0,1:T(8,128)(2,1)} %copy-done.63), kind=kOutput, calls=%fused_computation.19 | convolution fusion | flops 5913444352 | bytes 15728640 | tf_op jit(solution)/shard_map/dot_general | solution.py:117
  421.6 11.8 %convolution_convert_fusion.2 = bf16[1024,2048]{1,0:T(8,128)(2,1)} fusion(bf16[2048,1408]{1,0:T(8,128)(2,1)} %copy-done.22, bf16[2048,704]{0,1:T(8,128)(2,1)} %copy-done.64, bf16[2048,704]{0,1:T(8,128)(2,1)} %copy-done.63), kind=kOutput, calls=%fused_computation.18 | convolution fusion | flops 5913444352 | bytes 15728640 | tf_op jit(solution)/shard_map/dot_general | solution.py:117
  433.4 9.5 %fusion.64 = f32[704,2048]{1,0:T(8,128)S(1)} fusion(bf16[2048,704]{0,1:T(8,128)(2,1)} %get-tuple-element.36, bf16[2048,2048]{1,0:T(8,128)(2,1)} %constant_dynamic-update-slice_fusion.20), kind=kOutput, calls=%fused_computation.246 | convolution fusion | flops 5905580032 | bytes 17039360 | tf_op jit(solution)/shard_map/dot_general | solution.py:113
  442.9 7.6 convolution_convert_fusion.5
  450.5 5.7 convolution_convert_fusion.4
  466.2 9.8 %collective-permute-done.106 = bf16[176,2048]{1,0:T(8,128)(2,1)S(1)} collective-permute-done((bf16[176,2048]{1,0:T(8,128)(2,1)}, bf16[176,2048]{1,0:T(8,128)(2,1)S(1)}, u32[]{:S(2)}, u32[]{:S(2)}) %collective-permute-start.106) | collective-permute-done | bytes 720928 | tf_op jit(solution)/shard_map/ppermute | solution.py:27
  496.3 10.8 %collective-permute-done.103 = bf16[512,1408]{1,0:T(8,128)(2,1)} collective-permute-done((bf16[512,1408]{1,0:T(8,128)(2,1)}, bf16[512,1408]{1,0:T(8,128)(2,1)}, u32[]{:S(2)}, u32[]{:S(2)}) %collective-permute-start.103) | collective-permute-done | bytes 1441824 | tf_op jit(solution)/shard_map/ppermute | solution.py:27
  510.4 12.1 %collective-permute-done.107 = bf16[176,2048]{1,0:T(8,128)(2,1)} collective-permute-done((bf16[176,2048]{1,0:T(8,128)(2,1)}, bf16[176,2048]{1,0:T(8,128)(2,1)}, u32[]{:S(2)}, u32[]{:S(2)}) %collective-permute-start.107) | collective-permute-done | bytes 720928 | tf_op jit(solution)/shard_map/ppermute | solution.py:27
  528.6 5.6 collective-permute-done.52
  537.7 5.8 collective-permute-start.66
  543.5 3.9 collective-permute-done.72
  547.6 4.2 collective-permute-start.47
  558.7 10.3 %collective-permute-done.56 = bf16[128,2048]{1,0:T(8,128)(2,1)S(1)} collective-permute-done((bf16[128,2048]{1,0:T(8,128)(2,1)S(1)}, bf16[128,2048]{1,0:T(8,128)(2,1)S(1)}, u32[]{:S(2)}, u32[]{:S(2)}) %collective-permute-start.56) | collective-permute-done | bytes 524320 | tf_op jit(solution)/shard_map/ppermute | solution.py:22
  580.7 4.7 collective-permute-start.76
  585.4 16.2 %collective-permute-done.108 = bf16[176,2048]{1,0:T(8,128)(2,1)} collective-permute-done((bf16[176,2048]{1,0:T(8,128)(2,1)}, bf16[176,2048]{1,0:T(8,128)(2,1)}, u32[]{:S(2)}, u32[]{:S(2)}) %collective-permute-start.108) | collective-permute-done | bytes 720928 | tf_op jit(solution)/shard_map/ppermute | solution.py:27
  607.0 8.8 %collective-permute-start.80 = (bf16[256,2048]{1,0:T(8,128)(2,1)S(1)}, bf16[256,2048]{1,0:T(8,128)(2,1)S(1)}, u32[]{:S(2)}, u32[]{:S(2)}) collective-permute-start(bf16[256,2048]{1,0:T(8,128)(2,1)S(1)} %collective-permute-done.79), channel_id=1, source_target_pairs={{0,1},{1,0},{2,3},{3,2},{4,5},{5,4},{6,7},{7,6},{8,9},{9,8},{10,11... | collective-permute-start | bytes 3145736 | tf_op jit(solution)/shard_map/ppermute | solution.py:22
  632.5 21.0 %attend_back.1 = (bf16[2,4,256,256]{3,2,1,0:T(8,128)(2,1)S(1)}, f32[2,4,256,128]{3,2,1,0:T(8,128)S(1)}) custom-call(s32[1]{0:T(128)} %bitcast.m_ref, bf16[2,256,1024]{2,1,0:T(8,128)(2,1)S(1)} %get-tuple-element.18.qt_ref, bf16[2,1024,128]{2,1,0:T(8,128)(2,1)S(1)} %copy-done.3, f32[2,8,1024]{2,1,0:T(8,128)S(1)} %get-tuple-element.20.lse_ref, ...), custom_call_target="tpu_custom_call" | custom-call | flops 10737418240 | bytes 8388608 | tf_op jit(solution)/shard_map/attend_back/pallas_call | solution.py:290
  665.3 4.8 all-to-all-start.3
  684.4 6.9 fusion.9
  709.5 19.2 %collective-permute-done.97 = bf16[512,320]{0,1:T(8,128)(2,1)S(1)} collective-permute-done((bf16[512,320]{0,1:T(8,128)(2,1)S(1)}, bf16[512,320]{0,1:T(8,128)(2,1)S(1)}, u32[]{:S(2)}, u32[]{:S(2)}) %collective-permute-start.97) | collective-permute-done | bytes 327712 | tf_op jit(solution)/shard_map/ppermute | solution.py:27
  729.6 23.1 %collective-permute-done.102 = f32[64,2048]{1,0:T(8,128)S(1)} collective-permute-done((f32[64,2048]{1,0:T(8,128)S(1)}, f32[64,2048]{1,0:T(8,128)S(1)}, u32[]{:S(2)}, u32[]{:S(2)}) %collective-permute-start.102) | collective-permute-done | bytes 524320 | tf_op jit(solution)/shard_map/ppermute | solution.py:408
  802.3 8.8 %collective-permute-done.93 = bf16[128,2048]{1,0:T(8,128)(2,1)} collective-permute-done((bf16[128,2048]{1,0:T(8,128)(2,1)}, bf16[128,2048]{1,0:T(8,128)(2,1)}, u32[]{:S(2)}, u32[]{:S(2)}) %collective-permute-start.93) | collective-permute-done | bytes 524320 | tf_op jit(solution)/shard_map/ppermute | solution.py:22
  813.0 9.3 %collective-permute-done.92 = bf16[128,2048]{1,0:T(8,128)(2,1)S(1)} collective-permute-done((bf16[128,2048]{1,0:T(8,128)(2,1)S(1)}, bf16[128,2048]{1,0:T(8,128)(2,1)S(1)}, u32[]{:S(2)}, u32[]{:S(2)}) %collective-permute-start.92) | collective-permute-done | bytes 524320 | tf_op jit(solution)/shard_map/ppermute | solution.py:22
  (534 shorter events, 336.8 us)
Async XLA Ops:
  0.7 108.2 %collective-permute-start.58 = (bf16[256,2048]{1,0:T(8,128)(2,1)}, bf16[256,2048]{1,0:T(8,128)(2,1)}, u32[]{:S(2)}, u32[]{:S(2)}) collective-permute-start(bf16[256,2048]{1,0:T(8,128)(2,1)} %param.21), channel_id=1, source_target_pairs={{0,2},{1,3},{2,0},{3,1},{4,6},{5,7},{6,4},{7,5},{8,10},{9,11},{10,... | collective-permute-start | bytes 3145736 | tf_op jit(solution)/shard_map/ppermute | solution.py:22
  2.8 102.4 %collective-permute-start.57 = (bf16[256,2048]{1,0:T(8,128)(2,1)}, bf16[256,2048]{1,0:T(8,128)(2,1)}, u32[]{:S(2)}, u32[]{:S(2)}) collective-permute-start(bf16[256,2048]{1,0:T(8,128)(2,1)} %param.21), channel_id=1, source_target_pairs={{0,1},{1,0},{2,3},{3,2},{4,5},{5,4},{6,7},{7,6},{8,9},{9,8},{10,11... | collective-permute-start | bytes 3145736 | tf_op jit(solution)/shard_map/ppermute | solution.py:22
  4.9 28.9 %collective-permute-start.9 = (bf16[2,64]{1,0:T(2,128)(2,1)}, bf16[2,64]{1,0:T(2,128)(2,1)S(1)}, u32[]{:S(2)}, u32[]{:S(2)}) collective-permute-start(bf16[2,64]{1,0:T(2,128)(2,1)} %pad_maximum_fusion.8), channel_id=1, source_target_pairs={{0,1},{1,0},{2,3},{3,2},{4,5},{5,4},{6,7},{7,6},{8,9},{9,8},{10,11... | collective-permute-start | bytes 776 | tf_op jit(solution)/shard_map/ppermute | solution.py:22
  8.7 57.3 %all-to-all-start = ((bf16[8,64,384]{2,1,0:T(8,128)(2,1)}), bf16[8,64,384]{2,1,0:T(8,128)(2,1)S(1)}, u32[]{:S(2)}, u32[]{:S(2)}) async-start(bf16[8,64,384]{2,1,0:T(8,128)(2,1)} %copy.60), calls=%async_computation | async-start | bytes 786432 | tf_op jit(solution)/shard_map/all_to_all | solution.py:36
  12.6 75.6 %collective-permute-start.44 = (bf16[176,2048]{1,0:T(8,128)(2,1)}, bf16[176,2048]{1,0:T(8,128)(2,1)}, u32[]{:S(2)}, u32[]{:S(2)}) collective-permute-start(bf16[176,2048]{1,0:T(8,128)(2,1)} %param.20), channel_id=1, source_target_pairs={{0,8},{1,9},{2,10},{3,11},{4,12},{5,13},{6,14},{7,15},{8,16},{9,17... | collective-permute-start | bytes 2162696 | tf_op jit(solution)/shard_map/ppermute | solution.py:27
  13.9 97.4 %collective-permute-start = (bf16[256,2048]{1,0:T(8,128)(2,1)S(1)}, bf16[256,2048]{1,0:T(8,128)(2,1)}, u32[]{:S(2)}, u32[]{:S(2)}) collective-permute-start(bf16[256,2048]{1,0:T(8,128)(2,1)S(1)} %copy-done.5), channel_id=1, source_target_pairs={{0,1},{1,0},{2,3},{3,2},{4,5},{5,4},{6,7},{7,6},{8,9},{9,8},{10,11... | collective-permute-start | bytes 3145736 | tf_op jit(solution)/shard_map/ppermute | solution.py:22
  66.1 94.5 %all-to-all-start.1 = ((bf16[8,64,1408]{2,1,0:T(8,128)(2,1)}), bf16[8,64,1408]{2,1,0:T(8,128)(2,1)}, u32[]{:S(2)}, u32[]{:S(2)}) async-start(bf16[8,64,1408]{2,1,0:T(8,128)(2,1)} %pad_maximum_fusion.4), calls=%async_computation.1 | async-start | bytes 2883584 | tf_op jit(solution)/shard_map/all_to_all | solution.py:36
  105.1 48.6 %collective-permute-start.60 = (bf16[256,2048]{1,0:T(8,128)(2,1)S(1)}, bf16[256,2048]{1,0:T(8,128)(2,1)}, u32[]{:S(2)}, u32[]{:S(2)}) collective-permute-start(bf16[256,2048]{1,0:T(8,128)(2,1)S(1)} %copy-done.27), channel_id=1, source_target_pairs={{0,4},{1,5},{2,6},{3,7},{4,0},{5,1},{6,2},{7,3},{8,12},{9,13},{10,... | collective-permute-start | bytes 3145736 | tf_op jit(solution)/shard_map/ppermute | solution.py:22
  105.2 46.6 %collective-permute-start.3 = (bf16[256,2048]{1,0:T(8,128)(2,1)S(1)}, bf16[256,2048]{1,0:T(8,128)(2,1)}, u32[]{:S(2)}, u32[]{:S(2)}) collective-permute-start(bf16[256,2048]{1,0:T(8,128)(2,1)S(1)} %copy-done.5), channel_id=1, source_target_pairs={{0,4},{1,5},{2,6},{3,7},{4,0},{5,1},{6,2},{7,3},{8,12},{9,13},{10,... | collective-permute-start | bytes 3145736 | tf_op jit(solution)/shard_map/ppermute | solution.py:22
  111.3 51.5 %collective-permute-start.45 = (bf16[176,2048]{1,0:T(8,128)(2,1)}, bf16[176,2048]{1,0:T(8,128)(2,1)}, u32[]{:S(2)}, u32[]{:S(2)}) collective-permute-start(bf16[176,2048]{1,0:T(8,128)(2,1)} %collective-permute-done.44), channel_id=1, source_target_pairs={{0,8},{1,9},{2,10},{3,11},{4,12},{5,13},{6,14},{7,15},{8,16},{9,17... | collective-permute-start | bytes 2162696 | tf_op jit(solution)/shard_map/ppermute | solution.py:27
  117.3 42.4 %collective-permute-start.16 = (bf16[512,384]{0,1:T(8,128)(2,1)S(1)}, bf16[512,384]{0,1:T(8,128)(2,1)S(1)}, u32[]{:S(2)}, u32[]{:S(2)}) collective-permute-start(bf16[512,384]{0,1:T(8,128)(2,1)S(1)} %collective-permute-done.15), channel_id=1, source_target_pairs={{0,8},{1,9},{2,10},{3,11},{4,12},{5,13},{6,14},{7,15},{8,16},{9,17... | collective-permute-start | bytes 1179656 | tf_op jit(solution)/shard_map/ppermute | solution.py:27
  122.4 52.8 %collective-permute-start.2 = (bf16[256,2048]{1,0:T(8,128)(2,1)}, bf16[256,2048]{1,0:T(8,128)(2,1)}, u32[]{:S(2)}, u32[]{:S(2)}) collective-permute-start(bf16[256,2048]{1,0:T(8,128)(2,1)} %collective-permute-done.1), channel_id=1, source_target_pairs={{0,1},{1,0},{2,3},{3,2},{4,5},{5,4},{6,7},{7,6},{8,9},{9,8},{10,11... | collective-permute-start | bytes 3145736 | tf_op jit(solution)/shard_map/ppermute | solution.py:22
  151.8 100.9 %collective-permute-start.62 = (bf16[128,2048]{1,0:T(8,128)(2,1)}, bf16[128,2048]{1,0:T(8,128)(2,1)}, u32[]{:S(2)}, u32[]{:S(2)}) collective-permute-start(bf16[128,2048]{1,0:T(8,128)(2,1)} %slice.404), channel_id=1, source_target_pairs={{0,4},{1,5},{2,6},{3,7},{4,0},{5,1},{6,2},{7,3},{8,12},{9,13},{10,... | collective-permute-start | bytes 1572872 | tf_op jit(solution)/shard_map/ppermute | solution.py:22
  153.6 33.7 %collective-permute-start.4 = (bf16[256,2048]{1,0:T(8,128)(2,1)}, bf16[256,2048]{1,0:T(8,128)(2,1)}, u32[]{:S(2)}, u32[]{:S(2)}) collective-permute-start(bf16[256,2048]{1,0:T(8,128)(2,1)} %collective-permute-done.3), channel_id=1, source_target_pairs={{0,1},{1,0},{2,3},{3,2},{4,5},{5,4},{6,7},{7,6},{8,9},{9,8},{10,11... | collective-permute-start | bytes 3145736 | tf_op jit(solution)/shard_map/ppermute | solution.py:22
  175.3 44.3 %collective-permute-start.59 = (bf16[256,2048]{1,0:T(8,128)(2,1)}, bf16[256,2048]{1,0:T(8,128)(2,1)S(1)}, u32[]{:S(2)}, u32[]{:S(2)}) collective-permute-start(bf16[256,2048]{1,0:T(8,128)(2,1)} %collective-permute-done.58), channel_id=1, source_target_pairs={{0,1},{1,0},{2,3},{3,2},{4,5},{5,4},{6,7},{7,6},{8,9},{9,8},{10,11... | collective-permute-start | bytes 3145736 | tf_op jit(solution)/shard_map/ppermute | solution.py:22
  178.9 61.1 %collective-permute-start.61 = (bf16[256,2048]{1,0:T(8,128)(2,1)}, bf16[256,2048]{1,0:T(8,128)(2,1)S(1)}, u32[]{:S(2)}, u32[]{:S(2)}) collective-permute-start(bf16[256,2048]{1,0:T(8,128)(2,1)} %collective-permute-done.60), channel_id=1, source_target_pairs={{0,1},{1,0},{2,3},{3,2},{4,5},{5,4},{6,7},{7,6},{8,9},{9,8},{10,11... | collective-permute-start | bytes 3145736 | tf_op jit(solution)/shard_map/ppermute | solution.py:22
  188.8 77.1 %collective-permute-start.41 = (bf16[512,1408]{1,0:T(8,128)(2,1)}, bf16[512,1408]{1,0:T(8,128)(2,1)S(1)}, u32[]{:S(2)}, u32[]{:S(2)}) collective-permute-start(bf16[512,1408]{1,0:T(8,128)(2,1)} %bitcast.15), channel_id=1, source_target_pairs={{0,8},{1,9},{2,10},{3,11},{4,12},{5,13},{6,14},{7,15},{8,16},{9,17... | collective-permute-start | bytes 4325384 | tf_op jit(solution)/shard_map/ppermute | solution.py:27
  227.7 29.8 %collective-permute-start.24 = (bf16[128,2048]{1,0:T(8,128)(2,1)S(1)}, bf16[128,2048]{1,0:T(8,128)(2,1)S(1)}, u32[]{:S(2)}, u32[]{:S(2)}) collective-permute-start(bf16[128,2048]{1,0:T(8,128)(2,1)S(1)} %slice.569), channel_id=1, source_target_pairs={{0,2},{1,3},{2,0},{3,1},{4,6},{5,7},{6,4},{7,5},{8,10},{9,11},{10,... | collective-permute-start | bytes 1572872 | tf_op jit(solution)/shard_map/ppermute | solution.py:22
  265.9 46.6 %collective-permute-start.46 = (bf16[176,2048]{1,0:T(8,128)(2,1)}, bf16[176,2048]{1,0:T(8,128)(2,1)S(1)}, u32[]{:S(2)}, u32[]{:S(2)}) collective-permute-start(bf16[176,2048]{1,0:T(8,128)(2,1)} %collective-permute-done.45), channel_id=1, source_target_pairs={{0,8},{1,9},{2,10},{3,11},{4,12},{5,13},{6,14},{7,15},{8,16},{9,17... | collective-permute-start | bytes 2162696 | tf_op jit(solution)/shard_map/ppermute | solution.py:27
  276.1 35.6 %collective-permute-start.42 = (bf16[512,1408]{1,0:T(8,128)(2,1)S(1)}, bf16[512,1408]{1,0:T(8,128)(2,1)S(1)}, u32[]{:S(2)}, u32[]{:S(2)}) collective-permute-start(bf16[512,1408]{1,0:T(8,128)(2,1)S(1)} %collective-permute-done.41), channel_id=1, source_target_pairs={{0,8},{1,9},{2,10},{3,11},{4,12},{5,13},{6,14},{7,15},{8,16},{9,17... | collective-permute-start | bytes 4325384 | tf_op jit(solution)/shard_map/ppermute | solution.py:27
  278.4 35.3 %collective-permute-start.33 = (bf16[256,2048]{1,0:T(8,128)(2,1)S(1)}, bf16[256,2048]{1,0:T(8,128)(2,1)S(1)}, u32[]{:S(2)}, u32[]{:S(2)}) collective-permute-start(bf16[256,2048]{1,0:T(8,128)(2,1)S(1)} %get-tuple-element.29), channel_id=1, source_target_pairs={{0,2},{1,3},{2,0},{3,1},{4,6},{5,7},{6,4},{7,5},{8,10},{9,11},{10,... | collective-permute-start | bytes 3145736 | tf_op jit(solution)/shard_map/ppermute | solution.py:22
  280.7 39.6 %collective-permute-start.35 = (bf16[256,2048]{1,0:T(8,128)(2,1)S(1)}, bf16[256,2048]{1,0:T(8,128)(2,1)S(1)}, u32[]{:S(2)}, u32[]{:S(2)}) collective-permute-start(bf16[256,2048]{1,0:T(8,128)(2,1)S(1)} %get-tuple-element.29), channel_id=1, source_target_pairs={{0,4},{1,5},{2,6},{3,7},{4,0},{5,1},{6,2},{7,3},{8,12},{9,13},{10,... | collective-permute-start | bytes 3145736 | tf_op jit(solution)/shard_map/ppermute | solution.py:22
  280.8 39.9 %collective-permute-start.32 = (bf16[256,2048]{1,0:T(8,128)(2,1)S(1)}, bf16[256,2048]{1,0:T(8,128)(2,1)S(1)}, u32[]{:S(2)}, u32[]{:S(2)}) collective-permute-start(bf16[256,2048]{1,0:T(8,128)(2,1)S(1)} %get-tuple-element.29), channel_id=1, source_target_pairs={{0,1},{1,0},{2,3},{3,2},{4,5},{5,4},{6,7},{7,6},{8,9},{9,8},{10,11... | collective-permute-start | bytes 3145736 | tf_op jit(solution)/shard_map/ppermute | solution.py:22
  311.7 30.0 %collective-permute-start.43 = (bf16[512,1408]{1,0:T(8,128)(2,1)S(1)}, bf16[512,1408]{1,0:T(8,128)(2,1)S(1)}, u32[]{:S(2)}, u32[]{:S(2)}) collective-permute-start(bf16[512,1408]{1,0:T(8,128)(2,1)S(1)} %collective-permute-done.42), channel_id=1, source_target_pairs={{0,8},{1,9},{2,10},{3,11},{4,12},{5,13},{6,14},{7,15},{8,16},{9,17... | collective-permute-start | bytes 4325384 | tf_op jit(solution)/shard_map/ppermute | solution.py:27
  313.7 35.0 %collective-permute-start.34 = (bf16[256,2048]{1,0:T(8,128)(2,1)S(1)}, bf16[256,2048]{1,0:T(8,128)(2,1)S(1)}, u32[]{:S(2)}, u32[]{:S(2)}) collective-permute-start(bf16[256,2048]{1,0:T(8,128)(2,1)S(1)} %collective-permute-done.33), channel_id=1, source_target_pairs={{0,1},{1,0},{2,3},{3,2},{4,5},{5,4},{6,7},{7,6},{8,9},{9,8},{10,11... | collective-permute-start | bytes 3145736 | tf_op jit(solution)/shard_map/ppermute | solution.py:22
  320.7 30.1 %collective-permute-start.36 = (bf16[256,2048]{1,0:T(8,128)(2,1)S(1)}, bf16[256,2048]{1,0:T(8,128)(2,1)S(1)}, u32[]{:S(2)}, u32[]{:S(2)}) collective-permute-start(bf16[256,2048]{1,0:T(8,128)(2,1)S(1)} %collective-permute-done.35), channel_id=1, source_target_pairs={{0,1},{1,0},{2,3},{3,2},{4,5},{5,4},{6,7},{7,6},{8,9},{9,8},{10,11... | collective-permute-start | bytes 3145736 | tf_op jit(solution)/shard_map/ppermute | solution.py:22
  458.5 48.6 %collective-permute-start.103 = (bf16[512,1408]{1,0:T(8,128)(2,1)}, bf16[512,1408]{1,0:T(8,128)(2,1)}, u32[]{:S(2)}, u32[]{:S(2)}) collective-permute-start(bf16[512,1408]{1,0:T(8,128)(2,1)} %dynamic-slice_convert_fusion), channel_id=1, source_target_pairs={{0,8},{1,9},{2,10},{3,11},{4,12},{5,13},{6,14},{7,15},{8,16},{9,17... | collective-permute-start | bytes 4325384 | tf_op jit(solution)/shard_map/ppermute | solution.py:27
  485.9 36.6 %collective-permute-start.107 = (bf16[176,2048]{1,0:T(8,128)(2,1)}, bf16[176,2048]{1,0:T(8,128)(2,1)}, u32[]{:S(2)}, u32[]{:S(2)}) collective-permute-start(bf16[176,2048]{1,0:T(8,128)(2,1)} %add_convert_fusion.8), channel_id=1, source_target_pairs={{0,8},{1,9},{2,10},{3,11},{4,12},{5,13},{6,14},{7,15},{8,16},{9,17... | collective-permute-start | bytes 2162696 | tf_op jit(solution)/shard_map/ppermute | solution.py:27
  487.6 59.9 %collective-permute-start.75 = (bf16[128,2048]{1,0:T(8,128)(2,1)S(1)}, bf16[128,2048]{1,0:T(8,128)(2,1)}, u32[]{:S(2)}, u32[]{:S(2)}) collective-permute-start(bf16[128,2048]{1,0:T(8,128)(2,1)S(1)} %slice.564), channel_id=1, source_target_pairs={{0,4},{1,5},{2,6},{3,7},{4,0},{5,1},{6,2},{7,3},{8,12},{9,13},{10,... | collective-permute-start | bytes 1572872 | tf_op jit(solution)/shard_map/ppermute | solution.py:22
  490.7 34.6 %collective-permute-start.71 = (bf16[128,2048]{1,0:T(8,128)(2,1)}, bf16[128,2048]{1,0:T(8,128)(2,1)}, u32[]{:S(2)}, u32[]{:S(2)}) collective-permute-start(bf16[128,2048]{1,0:T(8,128)(2,1)} %get-tuple-element.69), channel_id=1, source_target_pairs={{0,2},{1,3},{2,0},{3,1},{4,6},{5,7},{6,4},{7,5},{8,10},{9,11},{10,... | collective-permute-start | bytes 1572872 | tf_op jit(solution)/shard_map/ppermute | solution.py:22
  492.3 34.2 %collective-permute-start.73 = (bf16[128,2048]{1,0:T(8,128)(2,1)}, bf16[128,2048]{1,0:T(8,128)(2,1)}, u32[]{:S(2)}, u32[]{:S(2)}) collective-permute-start(bf16[128,2048]{1,0:T(8,128)(2,1)} %get-tuple-element.70), channel_id=1, source_target_pairs={{0,4},{1,5},{2,6},{3,7},{4,0},{5,1},{6,2},{7,3},{8,12},{9,13},{10,... | collective-permute-start | bytes 1572872 | tf_op jit(solution)/shard_map/ppermute | solution.py:22
  507.1 30.6 %collective-permute-start.68 = (bf16[128,2048]{1,0:T(8,128)(2,1)S(1)}, bf16[128,2048]{1,0:T(8,128)(2,1)S(1)}, u32[]{:S(2)}, u32[]{:S(2)}) collective-permute-start(bf16[128,2048]{1,0:T(8,128)(2,1)S(1)} %slice.565), channel_id=1, source_target_pairs={{0,2},{1,3},{2,0},{3,1},{4,6},{5,7},{6,4},{7,5},{8,10},{9,11},{10,... | collective-permute-start | bytes 1572872 | tf_op jit(solution)/shard_map/ppermute | solution.py:22
  537.7 31.4 %collective-permute-start.66 = (bf16[256,2048]{1,0:T(8,128)(2,1)S(1)}, bf16[256,2048]{1,0:T(8,128)(2,1)S(1)}, u32[]{:S(2)}, u32[]{:S(2)}) collective-permute-start(bf16[256,2048]{1,0:T(8,128)(2,1)S(1)} %copy-done.42), channel_id=1, source_target_pairs={{0,1},{1,0},{2,3},{3,2},{4,5},{5,4},{6,7},{7,6},{8,9},{9,8},{10,11... | collective-permute-start | bytes 3145736 | tf_op jit(solution)/shard_map/ppermute | solution.py:22
  558.5 57.4 %collective-permute-start.104 = (bf16[512,1408]{1,0:T(8,128)(2,1)}, bf16[512,1408]{1,0:T(8,128)(2,1)}, u32[]{:S(2)}, u32[]{:S(2)}) collective-permute-start(bf16[512,1408]{1,0:T(8,128)(2,1)} %add_convert_fusion.2), channel_id=1, source_target_pairs={{0,8},{1,9},{2,10},{3,11},{4,12},{5,13},{6,14},{7,15},{8,16},{9,17... | collective-permute-start | bytes 4325384 | tf_op jit(solution)/shard_map/ppermute | solution.py:27
  569.0 32.6 %collective-permute-start.108 = (bf16[176,2048]{1,0:T(8,128)(2,1)}, bf16[176,2048]{1,0:T(8,128)(2,1)}, u32[]{:S(2)}, u32[]{:S(2)}) collective-permute-start(bf16[176,2048]{1,0:T(8,128)(2,1)} %add_convert_fusion.7), channel_id=1, source_target_pairs={{0,8},{1,9},{2,10},{3,11},{4,12},{5,13},{6,14},{7,15},{8,16},{9,17... | collective-permute-start | bytes 2162696 | tf_op jit(solution)/shard_map/ppermute | solution.py:27
  575.6 29.1 %collective-permute-start.79 = (bf16[256,2048]{1,0:T(8,128)(2,1)}, bf16[256,2048]{1,0:T(8,128)(2,1)S(1)}, u32[]{:S(2)}, u32[]{:S(2)}) collective-permute-start(bf16[256,2048]{1,0:T(8,128)(2,1)} %get-tuple-element.26), channel_id=1, source_target_pairs={{0,4},{1,5},{2,6},{3,7},{4,0},{5,1},{6,2},{7,3},{8,12},{9,13},{10,... | collective-permute-start | bytes 3145736 | tf_op jit(solution)/shard_map/ppermute | solution.py:22
  575.6 30.2 %collective-permute-start.77 = (bf16[256,2048]{1,0:T(8,128)(2,1)}, bf16[256,2048]{1,0:T(8,128)(2,1)}, u32[]{:S(2)}, u32[]{:S(2)}) collective-permute-start(bf16[256,2048]{1,0:T(8,128)(2,1)} %get-tuple-element.26), channel_id=1, source_target_pairs={{0,2},{1,3},{2,0},{3,1},{4,6},{5,7},{6,4},{7,5},{8,10},{9,11},{10,... | collective-permute-start | bytes 3145736 | tf_op jit(solution)/shard_map/ppermute | solution.py:22
  580.7 38.7 %collective-permute-start.76 = (bf16[256,2048]{1,0:T(8,128)(2,1)}, bf16[256,2048]{1,0:T(8,128)(2,1)S(1)}, u32[]{:S(2)}, u32[]{:S(2)}) collective-permute-start(bf16[256,2048]{1,0:T(8,128)(2,1)} %get-tuple-element.26), channel_id=1, source_target_pairs={{0,1},{1,0},{2,3},{3,2},{4,5},{5,4},{6,7},{7,6},{8,9},{9,8},{10,11... | collective-permute-start | bytes 3145736 | tf_op jit(solution)/shard_map/ppermute | solution.py:22
  619.4 42.3 %collective-permute-start.105 = (bf16[512,1408]{1,0:T(8,128)(2,1)}, bf16[512,1408]{1,0:T(8,128)(2,1)}, u32[]{:S(2)}, u32[]{:S(2)}) collective-permute-start(bf16[512,1408]{1,0:T(8,128)(2,1)} %add_convert_fusion.1), channel_id=1, source_target_pairs={{0,8},{1,9},{2,10},{3,11},{4,12},{5,13},{6,14},{7,15},{8,16},{9,17... | collective-permute-start | bytes 4325384 | tf_op jit(solution)/shard_map/ppermute | solution.py:27
  631.2 28.6 %collective-permute-start.99 = (bf16[64,2048]{1,0:T(8,128)(2,1)S(1)}, bf16[64,2048]{1,0:T(8,128)(2,1)}, u32[]{:S(2)}, u32[]{:S(2)}) collective-permute-start(bf16[64,2048]{1,0:T(8,128)(2,1)S(1)} %dynamic-slice_convert_fusion.3), channel_id=1, source_target_pairs={{0,8},{1,9},{2,10},{3,11},{4,12},{5,13},{6,14},{7,15},{8,16},{9,17... | collective-permute-start | bytes 786440 | tf_op jit(solution)/shard_map/ppermute | solution.py:27
  665.3 87.7 %all-to-all-start.3 = ((bf16[8,64,1408]{2,1,0:T(8,128)(2,1)}), bf16[8,64,1408]{2,1,0:T(8,128)(2,1)S(1)}, u32[]{:S(2)}, u32[]{:S(2)}) async-start(bf16[8,64,1408]{2,1,0:T(8,128)(2,1)} %bitcast.86), calls=%async_computation.3 | async-start | bytes 2883584 | tf_op jit(solution)/shard_map/all_to_all | solution.py:36
  672.1 29.3 %collective-permute-start.101 = (bf16[64,2048]{1,0:T(8,128)(2,1)}, bf16[64,2048]{1,0:T(8,128)(2,1)}, u32[]{:S(2)}, u32[]{:S(2)}) collective-permute-start(bf16[64,2048]{1,0:T(8,128)(2,1)} %add_convert_fusion.12), channel_id=1, source_target_pairs={{0,8},{1,9},{2,10},{3,11},{4,12},{5,13},{6,14},{7,15},{8,16},{9,17... | collective-permute-start | bytes 786440 | tf_op jit(solution)/shard_map/ppermute | solution.py:27
  695.7 85.5 %collective-permute-start.90 = (bf16[256,2048]{1,0:T(8,128)(2,1)}, bf16[256,2048]{1,0:T(8,128)(2,1)}, u32[]{:S(2)}, u32[]{:S(2)}) collective-permute-start(bf16[256,2048]{1,0:T(8,128)(2,1)} %get-tuple-element.41), channel_id=1, source_target_pairs={{0,1},{1,0},{2,3},{3,2},{4,5},{5,4},{6,7},{7,6},{8,9},{9,8},{10,11... | collective-permute-start | bytes 3145736 | tf_op jit(solution)/shard_map/ppermute | solution.py:22
  698.0 83.2 %collective-permute-start.89 = (bf16[256,2048]{1,0:T(8,128)(2,1)}, bf16[256,2048]{1,0:T(8,128)(2,1)}, u32[]{:S(2)}, u32[]{:S(2)}) collective-permute-start(bf16[256,2048]{1,0:T(8,128)(2,1)} %get-tuple-element.42), channel_id=1, source_target_pairs={{0,1},{1,0},{2,3},{3,2},{4,5},{5,4},{6,7},{7,6},{8,9},{9,8},{10,11... | collective-permute-start | bytes 3145736 | tf_op jit(solution)/shard_map/ppermute | solution.py:22
  703.2 49.6 %collective-permute-start.102 = (f32[64,2048]{1,0:T(8,128)S(1)}, f32[64,2048]{1,0:T(8,128)S(1)}, u32[]{:S(2)}, u32[]{:S(2)}) collective-permute-start(f32[64,2048]{1,0:T(8,128)S(1)} %convert_add_fusion.18), channel_id=1, source_target_pairs={{0,0},{8,1},{16,2},{24,3},{1,4},{9,5},{17,6},{25,7},{2,8},{10,9},{... | collective-permute-start | bytes 1572872 | tf_op jit(solution)/shard_map/ppermute | solution.py:408
  709.4 116.6 %collective-permute-start.86 = (bf16[256,2048]{1,0:T(8,128)(2,1)}, bf16[256,2048]{1,0:T(8,128)(2,1)}, u32[]{:S(2)}, u32[]{:S(2)}) collective-permute-start(bf16[256,2048]{1,0:T(8,128)(2,1)} %get-tuple-element.37), channel_id=1, source_target_pairs={{0,1},{1,0},{2,3},{3,2},{4,5},{5,4},{6,7},{7,6},{8,9},{9,8},{10,11... | collective-permute-start | bytes 3145736 | tf_op jit(solution)/shard_map/ppermute | solution.py:22
  728.6 60.4 %collective-permute-start.87 = (bf16[256,2048]{1,0:T(8,128)(2,1)}, bf16[256,2048]{1,0:T(8,128)(2,1)}, u32[]{:S(2)}, u32[]{:S(2)}) collective-permute-start(bf16[256,2048]{1,0:T(8,128)(2,1)} %get-tuple-element.38), channel_id=1, source_target_pairs={{0,1},{1,0},{2,3},{3,2},{4,5},{5,4},{6,7},{7,6},{8,9},{9,8},{10,11... | collective-permute-start | bytes 3145736 | tf_op jit(solution)/shard_map/ppermute | solution.py:22
  785.1 38.4 %collective-permute-start.95 = (bf16[128,2048]{1,0:T(8,128)(2,1)}, bf16[128,2048]{1,0:T(8,128)(2,1)}, u32[]{:S(2)}, u32[]{:S(2)}) collective-permute-start(bf16[128,2048]{1,0:T(8,128)(2,1)} %slice.562), channel_id=1, source_target_pairs={{0,4},{1,5},{2,6},{3,7},{4,0},{5,1},{6,2},{7,3},{8,12},{9,13},{10,... | collective-permute-start | bytes 1572872 | tf_op jit(solution)/shard_map/ppermute | solution.py:22
  (132 other events, 1835.7 us)

commit v2 on v1

v2 whole, which is shorter than its diff:
```python
import functools

import jax
import jax.numpy as jnp
from jax import lax
from jax.experimental import pallas as pl
from jax.experimental.pallas import tpu as pltpu
from jax.sharding import PartitionSpec as P

HD = 64
RANKS = 8
GROUP = 4
EPS = 1e-05
THETA = 10000.0
NEG = -1e30
F32 = jnp.float32
ANY = pl.BlockSpec(memory_space=pl.ANY)
SCALAR = pl.BlockSpec(memory_space=pltpu.SMEM)
WORK = pl.CostEstimate(flops=1, bytes_accessed=1, transcendentals=0)
BF16 = jnp.bfloat16


def swap(block, bit):
    n = lax.axis_size("dev")
    return lax.ppermute(block, "dev", [(i, i ^ bit) for i in range(n)])


def onward(block):
    n = lax.axis_size("dev")
    return lax.ppermute(block, "dev", [(i, (i + RANKS) % n) for i in range(n)])


def plane_groups():
    n = lax.axis_size("dev")
    return [[p * RANKS + r for r in range(RANKS)] for p in range(n // RANKS)]


def exchange(blocks):
    return lax.all_to_all(
        blocks, "dev", split_axis=0, concat_axis=0, tiled=True, axis_index_groups=plane_groups()
    )


def column_groups():
    n = lax.axis_size("dev")
    return [[p * RANKS + r for p in range(n // RANKS)] for r in range(RANKS)]


def planes_gather(block):
    return lax.all_gather(block, "dev", axis=0, tiled=True, axis_index_groups=column_groups())


def planes_reduce(terms):
    return lax.psum_scatter(
        terms, "dev", scatter_dimension=0, tiled=True, axis_index_groups=column_groups()
    )


def after(value, *earlier):
    return lax.optimization_barrier((value,) + earlier)[0]


def wide(value):
    return value.astype(F32)


def thin(value):
    return value.astype(BF16)


def copy_kernel(count, spots, first_ref, *refs):
    blocks, whole, done = refs[:count], refs[count], refs[count + 1]
    copies = []
    for i, block in enumerate(blocks):
        spot = whole.at[pl.ds(spots(i, first_ref[0]), block.shape[0])]
        copies.append(pltpu.make_async_copy(block, spot, done.at[i]))
        copies[-1].start()
    for copy in copies:
        copy.wait()


def copied(blocks, spots, first, name):
    rows = sum(block.shape[0] for block in blocks)
    return pl.pallas_call(
        functools.partial(copy_kernel, len(blocks), spots),
        in_specs=[SCALAR] + [ANY] * len(blocks),
        out_shape=jax.ShapeDtypeStruct((rows, blocks[0].shape[1]), blocks[0].dtype),
        compiler_params=pltpu.CompilerParams(vmem_limit_bytes=40 * 2**20),
        scratch_shapes=[pltpu.SemaphoreType.DMA((len(blocks),))],
        cost_estimate=WORK,
        name=name,
    )(first, *blocks)


def join(*blocks):
    starts = [0]
    for block in blocks:
        starts.append(starts[-1] + block.shape[0])
    return copied(blocks, lambda i, _: starts[i], jnp.zeros(1, jnp.int32), "join")


def gather_pair(block):
    return swap(block, 2), swap(block, 4)


def gather_last(two, four):
    half = two.shape[0] // 2
    return swap(two[:half], 4), swap(four[half:], 2)


def on_rows(function, ins, outs, name):
    return pl.pallas_call(
        function,
        out_shape=[jax.ShapeDtypeStruct(shape, dtype) for shape, dtype in outs],
        compiler_params=pltpu.CompilerParams(vmem_limit_bytes=40 * 2**20),
        cost_estimate=WORK,
        name=name,
    )(*ins)


def send_kernel(even, peer, to_two, to_four):
    rows = to_two.shape[0]
    half = rows // 2

    def summed(block, start):
        span = slice(block * rows + start, block * rows + start + half)
        return thin(wide(even[span]) + wide(peer[span]))

    to_two[:half] = summed(1, 0)
    to_two[half:] = summed(3, 0)
    to_four[:half] = summed(2, half)
    to_four[half:] = summed(3, half)


def pass_kernel(even, peer, from_two, from_four, to_two, to_four):
    half = to_two.shape[0]

    def summed(block, start, arrived):
        span = slice(block * 2 * half + start, block * 2 * half + start + half)
        return thin(wide(even[span]) + wide(peer[span]) + wide(arrived[half:]))

    to_four[...] = summed(2, 0, from_two)
    to_two[...] = summed(1, half, from_four)


def send_rows(parts):
    rows, cols = parts[0].shape
    shape = ((rows // 4, cols), BF16)
    return on_rows(send_kernel, parts, (shape, shape), "send_rows")


def pass_rows(parts, arrived):
    rows, cols = parts[0].shape
    shape = ((rows // 8, cols), BF16)
    return on_rows(pass_kernel, (*parts, *arrived), (shape, shape), "pass_rows")


def cross(to_two, to_four):
    return swap(to_two, 2), swap(to_four, 4)


def block_sum(even, peer, from_two, from_four, last_two, last_four):
    rows = last_two.shape[0]
    top, low = slice(0, rows), slice(rows, 2 * rows)
    upper = wide(even[top]) + wide(peer[top]) + wide(from_two[top]) + wide(last_four[...])
    lower = wide(even[low]) + wide(peer[low]) + wide(from_four[top]) + wide(last_two[...])
    return jnp.concatenate([upper, lower], axis=0)


def parts_kernel(odd, transposed, near, far, weight, out):
    half = near.shape[0] // 2
    span = slice(half, 2 * half) if odd else slice(0, half)
    multiply = times_transposed if transposed else dot
    out[:half] = thin(multiply(near[span], weight[...]))
    out[half:] = thin(multiply(far[span], weight[...]))


def parts_of(odd, transposed, near, far, weight):
    cols = weight.shape[0 if transposed else 1]
    return on_rows(
        functools.partial(parts_kernel, odd, transposed),
        (near, far, weight),
        (((near.shape[0], cols), BF16),),
        "odd_parts" if odd else "even_parts",
    )[0]


def mean_of(values):
    return jnp.mean(values, axis=1, keepdims=True)


def norm_kernel(gain, *refs):
    out, start = refs[-1], 0
    for block in refs[:-1]:
        values = wide(block[...])
        span = slice(start, start + block.shape[0])
        out[span] = thin(values * rms_scale(values) * gain[...])
        start += block.shape[0]


def normed(gain, *blocks):
    rows = sum(block.shape[0] for block in blocks)
    shape = (rows, blocks[0].shape[1])
    return on_rows(norm_kernel, (gain, *blocks), ((shape, BF16),), "norm")[0]


def middle_kernel(tokens, gain, *refs):
    sums, (middle_ref, normed_ref, scale_ref) = refs[:6], refs[6:]
    middle = wide(tokens[...]) + block_sum(*sums)
    scale = rms_scale(middle)
    middle_ref[...] = middle
    normed_ref[...] = thin(middle * scale * gain[...])
    scale_ref[...] = scale


def middle_back_kernel(above, gain, middle, scale, *refs):
    sums, (grad_ref, branch_ref) = refs[:6], refs[6:]
    scaled = block_sum(*sums) * gain[...]
    middle, scale = middle[...], scale[...]
    grad = wide(above[...]) + scale * scaled - middle * scale**3 * mean_of(scaled * middle)
    grad_ref[...] = grad
    branch_ref[...] = thin(grad)


def output_kernel(middle, *refs):
    refs[-1][...] = thin(middle[...] + block_sum(*refs[:6]))


def input_back_kernel(grad, gain, tokens, *refs):
    scaled = block_sum(*refs[:6]) * gain[...]
    source = wide(tokens[...])
    scale = rms_scale(source)
    whole = grad[...] + scale * scaled - source * scale**3 * mean_of(scaled * source)
    refs[-1][...] = thin(whole)


def attn_parts_kernel(query, key, value, parts):
    width = query.shape[1] // RANKS
    share = RANKS * HD // key.shape[1]
    for j in range(RANKS):
        head = slice(j // share * HD, (j // share + 1) * HD)
        parts[j, :, :width] = query[:, j * width : (j + 1) * width]
        parts[j, :, width:] = jnp.concatenate([key[:, head], value[:, head]], axis=1)


def mlp_parts_kernel(units, gate, up, parts):
    planes = gate.shape[1] // units // RANKS
    for j in range(RANKS):
        pieces = []
        for weight in (gate, up):
            for p in range(planes):
                start = (p * RANKS + j) * units
                pieces.append(weight[:, start : start + units])
        parts[j] = jnp.concatenate(pieces, axis=1)


def lane_sums(grad, weight):
    total = 0.0
    for start in range(0, grad.shape[1], 128):
        span = slice(start, start + 128)
        total = total + grad[:, span] * wide(weight[:, span])
    return jnp.sum(total, axis=1, keepdims=True)


def mlp_back_kernel(units, parts, gate, up, gate_grad, up_grad, gain_sum):
    planes = gate.shape[1] // units // RANKS
    own = planes * units
    for half, grad in enumerate((gate_grad, up_grad)):
        for p in range(planes):
            start = half * own + p * units
            pieces = [parts[j, :, start : start + units] for j in range(RANKS)]
            row = jnp.concatenate(pieces, axis=1)
            grad[:, p * RANKS * units : (p + 1) * RANKS * units] = wide(row)
    gain_sum[...] = lane_sums(gate_grad, gate) + lane_sums(up_grad, up)


def attn_back_kernel(parts, query, key, value, query_grad, key_grad, value_grad, gain_sum):
    width = query.shape[1] // RANKS
    share = RANKS * HD // key.shape[1]
    for j in range(RANKS):
        query_grad[:, j * width : (j + 1) * width] = wide(parts[j, :, :width])
    for first, grad in enumerate((key_grad, value_grad)):
        pieces = [parts[j, :, width:] for j in range(first, RANKS, share)]
        grad[...] = wide(jnp.concatenate(pieces, axis=1))
    gain_sum[...] = (
        lane_sums(query_grad, query) + lane_sums(key_grad, key) + lane_sums(value_grad, value)
    )


def place_rows(blocks, plane):
    planes, rows = len(blocks), blocks[0].shape[0]

    def spot(step, own):
        return lax.rem(own + planes - step, planes) * rows

    if rows % 16 == 0:
        aligned = lambda step, own: pl.multiple_of(spot(step, own), 16)
        return copied(blocks, aligned, plane.astype(jnp.int32).reshape(1), "place_rows")
    whole = jnp.zeros((planes * rows, blocks[0].shape[1]), blocks[0].dtype)
    for step, block in enumerate(blocks):
        whole = lax.dynamic_update_slice_in_dim(whole, block, spot(step, plane), 0)
    return whole


def place_gains(blocks, plane):
    planes, rows = len(blocks), blocks[0].shape[0]
    whole = jnp.zeros((planes * rows, blocks[0].shape[1]), blocks[0].dtype)
    for step, block in enumerate(blocks):
        place = lax.rem(plane + planes - step, planes)
        whole = lax.dynamic_update_slice_in_dim(whole, block, place * rows, 0)
    return whole


def join_gains(gains, other, bit, me):
    return jnp.where(
        me & bit,
        jnp.concatenate([other, gains], axis=1),
        jnp.concatenate([gains, other], axis=1),
    )


def ring_part(terms, step, plane, planes):
    rows = terms.shape[0] // planes
    place = lax.rem(plane + 2 * planes - 1 - step, planes)
    return lax.dynamic_slice_in_dim(terms, place * rows, rows, 0)


def ring_start(terms, plane, planes):
    return thin(ring_part(terms, 0, plane, planes))


def ring_add(terms, step, arrived, plane, planes):
    total = ring_part(terms, step, plane, planes) + wide(arrived)
    return thin(total) if step < planes - 1 else total


def dot(left, right):
    return jnp.dot(left, right, preferred_element_type=F32)


def contract_rows(left, right):
    return lax.dot_general(left, right, (((0,), (0,)), ((), ())), preferred_element_type=F32)


def times_transposed(left, right):
    return lax.dot_general(left, right, (((1,), (1,)), ((), ())), preferred_element_type=F32)


def rms_scale(values):
    return lax.rsqrt(jnp.mean(values * values, axis=1, keepdims=True) + EPS)


def rope_tables(length):
    lanes = jnp.arange(2 * HD)
    frequency = THETA ** (-((lanes % (HD // 2)).astype(F32) * 2.0 / HD))
    angles = jnp.arange(length).astype(F32)[:, None] * frequency[None, :]
    sign = jnp.where(lanes % HD < HD // 2, -1.0, 1.0)
    return jnp.cos(angles), jnp.sin(angles) * sign[None, :]


def slot_of(place, mine):
    turn = place ^ mine
    return ((turn & 1) << 1) | (turn >> 1)


def spot_of(place, mine, rows):
    return pl.ds(pl.multiple_of(slot_of(place, mine) * rows, rows), rows)


def partner(values):
    lane = lax.broadcasted_iota(jnp.int32, values.shape, 1)
    ahead = pltpu.roll(values, 2 * HD - HD // 2, 1)
    behind = pltpu.roll(values, HD // 2, 1)
    return jnp.where(lane % HD < HD // 2, ahead, behind)


def fetch(blocks, whole, done):
    copies, start = [], 0
    for i, block in enumerate(blocks):
        spot = whole.at[pl.ds(start, block.shape[0])]
        copies.append(pltpu.make_async_copy(block, spot, done.at[i]))
        copies[-1].start()
        start += block.shape[0]
    for copy in copies:
        copy.wait()


def forward_kernel(heads, rows, count, m_ref, *refs):
    blocks, refs = refs[:count], refs[count:]
    weight_ref, cos_ref, sin_ref, mixed_ref, qt_ref, kv_ref, lse_ref, normed_ref, done = refs
    fetch(blocks, normed_ref, done)
    mine = m_ref[0]
    width = heads * HD
    blocks = GROUP
    is_key = lax.broadcasted_iota(jnp.int32, (rows, 2 * HD), 1) < HD
    for p in range(blocks):
        span = slice(p * rows, (p + 1) * rows)
        qkv = dot(normed_ref[spot_of(p, mine, rows), :], weight_ref[...])
        cosine, sine = cos_ref[span, :], sin_ref[span, :]
        turned = []
        for start in range(0, width, 2 * HD):
            part = qkv[:, start : start + 2 * HD]
            turned.append(part * cosine + partner(part) * sine)
        query = jnp.concatenate(turned, axis=1) * HD ** (-0.5)
        qt_ref[0, :, span] = query.T.astype(BF16)
        part = qkv[:, width : width + 2 * HD]
        kv_ref[0, span, :] = jnp.where(
            is_key, part * cosine + partner(part) * sine, part
        ).astype(BF16)
    kv = kv_ref[0]
    vt = kv.astype(F32).T.astype(BF16)[HD:, :]
    keys = kv[:, :HD]
    ok = lax.broadcasted_iota(jnp.int32, (rows, rows), 0) <= lax.broadcasted_iota(
        jnp.int32, (rows, rows), 1
    )
    for p in range(blocks):
        span = slice(p * rows, (p + 1) * rows)
        outs, tops = [], []
        for h in range(heads):
            query = qt_ref[0, h * HD : (h + 1) * HD, span]
            last = jnp.where(ok, dot(keys[span], query), NEG)
            top = jnp.max(last, axis=0, keepdims=True)
            if p:
                first = dot(keys[: p * rows], query)
                top = jnp.maximum(top, jnp.max(first, axis=0, keepdims=True))
            weight = jnp.exp(last - top)
            total = jnp.sum(weight, axis=0, keepdims=True)
            if p:
                first = jnp.exp(first - top)
                total = total + jnp.sum(first, axis=0, keepdims=True)
            share = 1.0 / total
            out = dot(vt[:, span], (weight * share).astype(BF16))
            if p:
                out = out + dot(vt[:, : p * rows], (first * share).astype(BF16))
            outs.append(out)
            tops.append(top + jnp.log(total))
        mixed_ref[0, slot_of(p, mine)] = jnp.concatenate(outs, axis=0).T.astype(BF16)
        tops += [tops[0]] * (8 - heads)
        lse_ref[0, :, span] = jnp.concatenate(tops, axis=0)


def backward_kernel(heads, rows, count, m_ref, *refs):
    blocks, refs = refs[:count], refs[count:]
    qt_ref, kv_ref, lse_ref, out_ref, cos_ref, sin_ref, *refs = refs
    dq_ref, kept_ref, sent_ref, dk_sum, dv_sum, branch_ref, done = refs
    fetch(blocks, branch_ref, done)
    mine = m_ref[0]
    width = heads * HD
    blocks = GROUP
    kv = kv_ref[0]
    kt = kv.astype(F32).T.astype(BF16)[:HD, :]
    keys = kv[:, :HD]
    values = pltpu.roll(kv.astype(F32), HD, 1).astype(BF16)[:, :HD]
    ok = lax.broadcasted_iota(jnp.int32, (rows, rows), 0) <= lax.broadcasted_iota(
        jnp.int32, (rows, rows), 1
    )
    for p in reversed(range(blocks)):
        span = slice(p * rows, (p + 1) * rows)
        reach = (p + 1) * rows
        grad = thin(times_transposed(out_ref[...], branch_ref[spot_of(p, mine, rows), :]))
        dqs = []
        for h in range(heads):
            query = qt_ref[0, h * HD : (h + 1) * HD, span]
            above = grad[h * HD : (h + 1) * HD, :]
            lse = lse_ref[0, h : h + 1, span]
            scores = dot(keys[:reach], query)
            if p:
                scores = jnp.concatenate(
                    [scores[: p * rows], jnp.where(ok, scores[p * rows :], NEG)], axis=0
                )
            else:
                scores = jnp.where(ok, scores, NEG)
            probs = jnp.exp(scores - lse)
            probs_grad = dot(values[:reach], above)
            delta = jnp.sum(probs * probs_grad, axis=0, keepdims=True)
            score_low = (probs * (probs_grad - delta)).astype(BF16)
            dk = times_transposed(score_low, query)
            dv = times_transposed(probs.astype(BF16), above)
            if p == blocks - 1 and h == 0:
                dk_sum[...] = dk
                dv_sum[...] = dv
            else:
                dk_sum[:reach, :] += dk
                dv_sum[:reach, :] += dv
            dqs.append(dot(kt[:, :reach], score_low))
        dq = jnp.concatenate(dqs, axis=0).T * HD ** (-0.5)
        cosine, sine = cos_ref[span, :], sin_ref[span, :]
        turned = []
        for start in range(0, width, 2 * HD):
            part = dq[:, start : start + 2 * HD]
            turned.append(part * cosine - partner(part) * sine)
        dq_ref[0, slot_of(p, mine)] = jnp.concatenate(turned, axis=1).astype(BF16)
    is_key = lax.broadcasted_iota(jnp.int32, (rows, 2 * HD), 1) < HD
    for p in range(blocks):
        span = slice(p * rows, (p + 1) * rows)
        part = jnp.concatenate([dk_sum[span, :], dv_sum[span, :]], axis=1)
        cosine, sine = cos_ref[span, :], sin_ref[span, :]
        part = jnp.where(is_key, part * cosine - partner(part) * sine, part)
        turned = pltpu.roll(part, HD, 1)
        even = (mine & 1) == 0
        kept_ref[0, slot_of(p, mine)] = jnp.where(even, part, turned)[:, :HD]
        sent_ref[0, slot_of(p, mine ^ 1)] = jnp.where(even, turned, part)[:, :HD]


def same_spec(shape):
    zeros = (0,) * len(shape)
    return pl.BlockSpec(shape, lambda i, m: zeros)


def attention_call(kernel, mine, blocks, others, shapes, scratch, name):
    length = sum(block.shape[0] for block in blocks)
    return pl.pallas_call(
        kernel,
        grid_spec=pltpu.PrefetchScalarGridSpec(
            num_scalar_prefetch=1,
            grid=(1,),
            in_specs=[ANY] * len(blocks) + [same_spec(v.shape) for v in others],
            out_specs=[same_spec(shape) for shape, _ in shapes],
            scratch_shapes=scratch
            + [
                pltpu.VMEM((length, blocks[0].shape[1]), BF16),
                pltpu.SemaphoreType.DMA((len(blocks),)),
            ],
        ),
        out_shape=[jax.ShapeDtypeStruct(shape, dtype) for shape, dtype in shapes],
        compiler_params=pltpu.CompilerParams(vmem_limit_bytes=48 * 2**20),
        cost_estimate=WORK,
        name=name,
    )(mine, *blocks, *others)


def attend(blocks, weight, tables, mine, heads):
    length = tables[0].shape[0]
    rows, width = length // GROUP, heads * HD
    shapes = (
        ((1, GROUP, rows, width), BF16),
        ((1, width, length), BF16),
        ((1, length, 2 * HD), BF16),
        ((1, 8, length), F32),
    )
    kernel = functools.partial(forward_kernel, heads, rows, len(blocks))
    return attention_call(kernel, mine, blocks, (weight, *tables), shapes, [], "attend")


def attend_back(kept, blocks, out_weight, tables, mine, heads):
    length = tables[0].shape[0]
    rows, width = length // GROUP, heads * HD
    half = ((1, GROUP, rows, HD), F32)
    shapes = (((1, GROUP, rows, width), BF16), half, half)
    scratch = [pltpu.VMEM((length, HD), F32), pltpu.VMEM((length, HD), F32)]
    kernel = functools.partial(backward_kernel, heads, rows, len(blocks))
    others = (*kept, out_weight, *tables)
    return attention_call(kernel, mine, blocks, others, shapes, scratch, "attend_back")


class Clock:
    def __init__(self):
        self.past = ()

    def __call__(self, value):
        return after(value, *self.past) if self.past else value

    def tick(self, *values):
        self.past = values


def per_device(
    tokens, attn_gain, w_query, w_key, w_value, w_out, mlp_gain, w_gate, w_up, w_down, cotangent
):
    n = lax.axis_size("dev")
    planes = n // RANKS
    me = lax.axis_index("dev")
    plane, rank = me // RANKS, lax.rem(me, RANKS)
    core = lax.rem(me, 2)
    mine = lax.rem(me, GROUP).astype(jnp.int32).reshape(1)
    count, model = tokens.shape
    local = w_query.shape[0]
    heads = w_query.shape[1] // HD // RANKS
    kv_heads = w_key.shape[1] // HD
    width = heads * HD
    units = w_gate.shape[1] // n
    own_units = units * planes
    seqs = RANKS // GROUP
    share = RANKS // kv_heads

    to_rank = [(i, (i % planes) * RANKS + i // planes) for i in range(n)]
    from_rank = [(j, i) for i, j in to_rank]
    attn_cols = width + 2 * HD
    clock = Clock()

    def finish(ring, *tail):
        while len(ring) < planes:
            ring = ring + [onward(ring[-1])]
        return ring

    (attn_parts,) = on_rows(
        attn_parts_kernel,
        (w_query, w_key, w_value),
        (((RANKS, local, attn_cols), BF16),),
        "attn_parts",
    )
    attn_own = exchange(attn_parts).reshape(RANKS * local, attn_cols)
    gains = after(jnp.stack([attn_gain, mlp_gain]), attn_parts)
    gain_ring = [gains]
    for step in range(1, planes):
        route = [(i, (i + RANKS * step) % n) for i in range(n)]
        gain_ring.append(lax.ppermute(gains, "dev", route))
    gains = place_gains(gain_ring, plane)
    for bit in (1, 2, 4):
        gains = join_gains(gains, swap(gains, bit), bit, me)
    gain_rows = gains.reshape(planes, 2, -1).transpose(1, 0, 2)
    gain_one, gain_two = jnp.split(gain_rows.reshape(2, model).astype(F32), 2)
    out_ring = [lax.ppermute(after(w_out, attn_parts), "dev", to_rank)]
    (mlp_parts,) = on_rows(
        functools.partial(mlp_parts_kernel, units),
        (w_gate, w_up),
        (((RANKS, local, 2 * own_units), BF16),),
        "mlp_parts",
    )
    tables = rope_tables(GROUP * count)
    clock.tick(gain_one, gain_two, mlp_parts, *tables)
    attn_own = clock(attn_own)
    clock.tick(attn_own, out_ring[0])
    two, four = gather_pair(clock(tokens))
    attn_ring = [attn_own, onward(clock(attn_own))]
    clock.tick(attn_ring[1])
    attn_ring.append(onward(clock(attn_ring[1])))
    out_ring.append(onward(clock(out_ring[0])))
    clock.tick(two, four, attn_ring[2], out_ring[1])
    six = gather_last(clock(two), clock(four))
    attn_ring.append(onward(clock(attn_ring[2])))
    near_even = normed(gain_one, clock(tokens), two)
    near_odd = swap(near_even, 1)
    out_ring.append(onward(clock(out_ring[1])))
    clock.tick(near_odd, attn_ring[3], out_ring[2], *six)
    mlp_own = exchange(clock(mlp_parts)).reshape(RANKS * local, 2 * own_units)
    attn_weight = place_rows(finish([clock(block) for block in attn_ring]), plane)
    far_even = normed(gain_one, clock(four), *six)
    far_odd = swap(far_even, 1)
    clock.tick(attn_weight, far_even)
    out_ring.append(onward(clock(out_ring[2])))
    down_ring = [w_down, onward(clock(w_down))]
    above_two, above_four = gather_pair(clock(cotangent))

    near_one_even, near_one_odd, far_one_even, far_one_odd = near_even, near_odd, far_even, far_odd
    near_mixed, *near_kept = attend((clock(near_even), near_odd), attn_weight, tables, mine, heads)
    clock.tick(near_mixed, far_odd, out_ring[3], mlp_own, down_ring[1])
    down_ring.append(onward(clock(down_ring[1])))
    mlp_weight = planes_gather(clock(mlp_own))
    far_mixed, *far_kept = attend((clock(far_even), far_odd), attn_weight, tables, mine, heads)
    far_mixed, near_mixed = far_mixed.reshape(-1, width), near_mixed.reshape(-1, width)
    clock.tick(far_mixed, above_two, above_four, down_ring[2])
    down_ring.append(onward(clock(down_ring[2])))
    above_six = gather_last(clock(above_two), clock(above_four))
    out_weight = place_rows(finish([clock(block) for block in out_ring]), plane)
    odd = parts_of(True, False, clock(near_mixed), far_mixed, out_weight)
    peer = swap(odd, 1)
    even = parts_of(False, False, after(near_mixed, odd), far_mixed, out_weight)
    clock.tick(even, peer, *above_six)
    parts = (clock(even), peer)
    clock.tick(*send_rows(parts))
    arrived = cross(*(clock(part) for part in clock.past))
    even_above = join(clock(cotangent), above_two, above_four, *above_six)
    odd_above = swap(even_above, 1)
    clock.tick(*arrived, odd_above)
    arrived = [clock(part) for part in arrived]
    last = cross(*pass_rows(parts, arrived))
    clock.tick(*last)
    last = [clock(part) for part in last]
    middle, own_two, scale_two = on_rows(
        middle_kernel,
        (tokens, gain_two, *parts, *arrived, *last),
        (((count, model), F32), ((count, model), BF16), ((count, 1), F32)),
        "middle",
    )

    clock.tick(own_two)
    two, four = gather_pair(clock(own_two))
    clock.tick(two, four)
    six = gather_last(clock(two), clock(four))
    clock.tick(*six, down_ring[3])
    even_two = join(clock(own_two), two, four, *six)
    odd_two = swap(even_two, 1)
    down_weight = place_rows(finish([clock(part) for part in down_ring]), plane)
    clock.tick(even_two, mlp_weight)
    mlp_weight = join(clock(mlp_weight))

    def feed(normed):
        both = dot(normed, mlp_weight)
        gate, up_proj = both[:, :own_units], both[:, own_units:]
        return gate, up_proj, thin(gate * jax.nn.sigmoid(gate) * up_proj)

    even_gate, even_up, even_hidden = feed(clock(even_two))
    clock.tick(even_hidden, odd_two)
    odd_gate, odd_up, odd_hidden = feed(clock(odd_two))
    clock.tick(odd_hidden)
    out_odd = thin(dot(clock(odd_hidden), down_weight))
    out_peer = swap(out_odd, 1)
    out_even = thin(dot(after(even_hidden, out_odd), down_weight))
    clock.tick(out_even, out_peer)
    out_parts = (clock(out_even), out_peer)
    clock.tick(*send_rows(out_parts))
    out_arrived = cross(*(clock(part) for part in clock.past))
    down_sum = contract_rows(clock(even_hidden), even_above) + contract_rows(odd_hidden, odd_above)
    down_sum = thin(down_sum)
    clock.tick(down_sum)
    down_grad = planes_reduce(clock(down_sum)).astype(F32)

    def feed_back(above, gate, up_proj):
        sigmoid_gate = jax.nn.sigmoid(gate)
        hidden_grad = times_transposed(above, down_weight)
        gate_low = hidden_grad * up_proj * sigmoid_gate * (1.0 + gate * (1.0 - sigmoid_gate))
        return jnp.concatenate([thin(gate_low), thin(hidden_grad * gate * sigmoid_gate)], axis=1)

    odd_low = feed_back(clock(odd_above), odd_gate, odd_up)
    odd_part = thin(times_transposed(odd_low, mlp_weight))
    peer = swap(odd_part, 1)
    clock.tick(odd_part, *out_arrived)
    out_arrived = [clock(part) for part in out_arrived]
    out_last = cross(*pass_rows(out_parts, out_arrived))
    even_low = feed_back(clock(even_above), even_gate, even_up)
    parts = (thin(times_transposed(even_low, mlp_weight)), peer)
    clock.tick(*send_rows(parts), *out_last)
    arrived = cross(*clock.past[:2])
    (output,) = on_rows(
        output_kernel,
        (middle, *out_parts, *out_arrived, *[clock(part) for part in out_last]),
        (((count, model), BF16),),
        "output",
    )
    mlp_sum = contract_rows(clock(even_two), even_low)
    mlp_sum = thin(mlp_sum + contract_rows(clock(odd_two), odd_low))
    clock.tick(*arrived, mlp_sum, output, down_grad)
    mlp_total = planes_reduce(clock(mlp_sum))
    arrived = [clock(part) for part in arrived]
    last = cross(*pass_rows(parts, arrived))
    clock.tick(*last)
    last = [clock(part) for part in last]
    middle_grad, branch = on_rows(
        middle_back_kernel,
        (cotangent, gain_two, middle, scale_two, *parts, *arrived, *last),
        (((count, model), F32), ((count, model), BF16)),
        "middle_back",
    )

    clock.tick(branch)
    one = swap(clock(branch), 1)
    two, four = gather_pair(clock(branch))
    near_one, far_one = join(clock(near_one_even), near_one_odd), join(clock(far_one_even), far_one_odd)
    back_weight = jnp.concatenate(
        [
            clock(attn_weight)[:, :width],
            jnp.where(core == 0, attn_weight[:, width : width + HD], attn_weight[:, width + HD :]),
        ],
        axis=1,
    )
    clock.tick(one, two, four, near_one, far_one, back_weight)
    six = gather_last(clock(two), clock(four))
    three = swap(clock(two), 1)
    clock.tick(three)

    def attention_back(kept, *blocks):
        query_low, own, other = attend_back(kept, blocks, out_weight, tables, mine, heads)
        return query_low.reshape(-1, width), own.reshape(-1, HD), swap(other.reshape(-1, HD), 1)

    near_blocks = (clock(branch), two, one, three)
    near_query, near_own, near_other = attention_back(near_kept, *near_blocks)
    clock.tick(near_query, *six)
    far_even = join(clock(four), *six)
    far_odd = swap(far_even, 1)
    near_branch = join(*near_blocks)
    clock.tick(far_odd, near_branch, near_other)
    far_query, far_own, far_other = attention_back(far_kept, clock(far_even), far_odd)
    near_all = jnp.concatenate([near_query, thin(near_own + near_other)], axis=1)
    clock.tick(far_query, far_other, near_all)
    far_all = jnp.concatenate([clock(far_query), thin(far_own + far_other)], axis=1)
    far_branch = join(clock(far_even), far_odd)
    odd = parts_of(True, True, near_all, far_all, back_weight)
    peer = swap(odd, 1)
    even = parts_of(False, True, after(near_all, odd), far_all, back_weight)
    out_sum = contract_rows(after(near_mixed, even), near_branch) + contract_rows(far_mixed, far_branch)
    out_hop = onward(ring_start(out_sum, plane, planes))
    attn_sum = contract_rows(after(near_one, out_sum), near_all) + contract_rows(after(far_one, out_sum), far_all)
    clock.tick(even, peer, attn_sum)
    parts = (clock(even), peer)
    clock.tick(*send_rows(parts), mlp_total)
    arrived = cross(*clock.past[:2])
    mlp_back = exchange(clock(mlp_total).reshape(RANKS, local, 2 * own_units))
    attn_hop = onward(clock(ring_start(attn_sum, plane, planes)))
    clock.tick(attn_hop, out_hop)
    attn_hop = onward(ring_add(attn_sum, 1, clock(attn_hop), plane, planes))
    out_hop = onward(ring_add(out_sum, 1, clock(out_hop), plane, planes))
    clock.tick(*arrived)
    arrived = [clock(part) for part in arrived]
    last = cross(*pass_rows(parts, arrived))
    clock.tick(attn_hop, out_hop)
    attn_hop = onward(ring_add(attn_sum, 2, clock(attn_hop), plane, planes))
    out_hop = onward(ring_add(out_sum, 2, clock(out_hop), plane, planes))
    clock.tick(*last, mlp_back)
    mlp_back = clock(mlp_back)
    last = [clock(part) for part in last]
    (input_grad,) = on_rows(
        input_back_kernel,
        (middle_grad, gain_one, tokens, *parts, *arrived, *last),
        (((count, model), BF16),),
        "input_back",
    )
    clock.tick(attn_hop, out_hop, input_grad)
    for step in range(3, planes - 1):
        attn_hop = onward(ring_add(attn_sum, step, attn_hop, plane, planes))
        out_hop = onward(ring_add(out_sum, step, out_hop, plane, planes))
    out_total = ring_add(out_sum, planes - 1, clock(out_hop), plane, planes)
    attn_total = ring_add(attn_sum, planes - 1, clock(attn_hop), plane, planes)
    attn_back = exchange(thin(attn_total).reshape(RANKS, local, width + HD))
    out_grad = lax.ppermute(out_total, "dev", from_rank)

    gate_grad, up_grad, mlp_gain_sum = on_rows(
        functools.partial(mlp_back_kernel, units),
        (mlp_back, w_gate, w_up),
        ((w_gate.shape, F32), (w_up.shape, F32), ((local, 1), F32)),
        "mlp_back",
    )
    query_grad, key_grad, value_grad, attn_gain_sum = on_rows(
        attn_back_kernel,
        (attn_back, w_query, w_key, w_value),
        ((w_query.shape, F32), (w_key.shape, F32), (w_value.shape, F32), ((local, 1), F32)),
        "attn_back",
    )
    return (
        output,
        input_grad,
        attn_gain_sum[:, 0] / attn_gain,
        query_grad,
        key_grad,
        value_grad,
        out_grad,
        mlp_gain_sum[:, 0] / mlp_gain,
        gate_grad,
        up_grad,
        down_grad,
    )


def solution(mesh):
    row, vec = P("dev", None), P("dev")
    return jax.shard_map(
        per_device,
        mesh=mesh,
        in_specs=(row, vec, row, row, row, row, vec, row, row, row, row),
        out_specs=(row, row, vec, row, row, row, row, vec, row, row, row),
        check_vma=False,
    )
```

time: 846 us -> 662 us (0.78)
  Pallas kernels: 37.9 us -> 134 us
  local copies, waits for them, and re-layouts: 146 us -> 65.5 us
  waiting for transfers between devices: 295 us -> 220 us
  other arithmetic: 77.5 us -> 19.9 us
  starting transfers between devices: 149 us -> 92.6 us
  matrix products: 125 us -> 106 us
  between operations: 2.79 us -> 15.5 us
    pallas_call x2 -> x37, Pallas kernels: 37.9 us -> 134 us  [the longest x22 64.3 us: on_rows(): pl.pallas_call(function, out_shape=[jax.ShapeDtypeStruct(shape, dtype) fo...]
    ppermute x27 -> x15, waiting for transfers between devices: 151 us -> 75.9 us  [onward(): return lax.ppermute(block, 'dev', [(i, (i + RANKS) % n) for i in range(n)])]
    ppermute x80 -> x48, starting transfers between devices: 105 us -> 51.7 us  [swap(): return lax.ppermute(block, 'dev', [(i, i ^ bit) for i in range(n)])]
    reshape x19 -> x0, local copies, waits for them, and re-layouts: 34.4 us -> none  [the longest x4 11.1 us: in_order(): parts = parts.reshape(RANKS, local, planes, units).transpose(1, 2, 0, 3)]
    convert_element_type x26 -> x11, other arithmetic: 38.5 us -> 13.3 us  [the longest x9 10.9 us: thin(): return value.astype(BF16)]
    slice x33 -> x10, local copies, waits for them, and re-layouts: 27.7 us -> 4.98 us  [the longest x8 4.48 us: gather_last(): return (swap(two[:half], 4), swap(four[half:], 2))]
    ppermute x1, waiting for transfers between devices: 23.1 us -> 2.81 us  [per_device(): out_grad = lax.ppermute(out_total, 'dev', from_rank)]
    all_to_all x4, waiting for transfers between devices: 0.01 us -> 16.9 us  [exchange(): lax.all_to_all(blocks, 'dev', split_axis=0, concat_axis=0, tiled=True, ax...]
  transfers between devices with their start and end apart: 113 -> 75, of which waited for: 39 -> 27; matrix products, arithmetic and copies ran while one was open for 27% -> 18% of each run, Pallas kernels for 5% -> 19%
where the time goes in v2:
time: 662 us; the launch traced here: 653 us
  waiting for transfers between devices  220 us (33%)
  Pallas kernels  134 us (20%)
  matrix products  106 us (16%)
  starting transfers between devices  92.6 us (14%)
  local copies, waits for them, and re-layouts  65.5 us (10%)
  other arithmetic  19.9 us (3%)
  between operations  15.5 us (2%)
    ppermute x48, waiting for transfers between devices, swap(): return lax.ppermute(block, 'dev', [(i, i ^ bit) for i in range(n)])  114 us
    ppermute x15, waiting for transfers between devices, onward(): return lax.ppermute(block, 'dev', [(i, (i + RANKS) % n) for i in range(n)])  75.9 us
    pallas_call x22, Pallas kernels, on_rows(): pl.pallas_call(function, out_shape=[jax.ShapeDtypeStruct(shape, dtype) fo...  64.3 us
    unnamed x237, local copies, waits for them, and re-layouts  58 us
    pallas_call x4, Pallas kernels, attention_call(): pl.pallas_call(kernel, grid_spec=pltpu.PrefetchScalarGridSpec(num_scalar_...  53.9 us
    ppermute x48, starting transfers between devices, swap(): return lax.ppermute(block, 'dev', [(i, i ^ bit) for i in range(n)])  51.7 us
    dot_general x8, matrix products, contract_rows(): lax.dot_general(left, right, (((0,), (0,)), ((), ())), preferred_element_...  43.7 us
    dot_general x4, matrix products, times_transposed(): lax.dot_general(left, right, (((1,), (1,)), ((), ())), preferred_element_...  36.3 us
  transfers between devices with their start and end apart: 75, of which 27 were waited for; matrix products, arithmetic and copies ran while one was open for 18% of the time, Pallas kernels for 19%

profile of v2, /device:TPU:1, one launch (start us, length us, event | category | flops | bytes accessed | tf_op | source)
XLA Modules:
  0.0 653.3 jit_solution(2346941800158013671)
XLA Ops:
  10.6 5.2 all-to-all-start
  20.4 4.8 collective-permute-start.6
  39.7 9.4 %collective-permute-done.9.refs_1_ = bf16[512,384]{1,0:T(8,128)(2,1)S(1)} collective-permute-done((bf16[512,384]{1,0:T(8,128)(2,1)S(1)}, bf16[512,384]{1,0:T(8,128)(2,1)S(1)}, u32[]{:S(2)}, u32[]{:S(2)}) %collective-permute-start.9) | collective-permute-done | bytes 393248 | tf_op jit(solution)/shard_map/ppermute | solution.py:30
  51.4 12.4 %collective-permute-done.11.refs_1_ = bf16[64,2048]{1,0:T(8,128)(2,1)S(1)} collective-permute-done((bf16[64,2048]{1,0:T(8,128)(2,1)}, bf16[64,2048]{1,0:T(8,128)(2,1)S(1)}, u32[]{:S(2)}, u32[]{:S(2)}) %collective-permute-start.11) | collective-permute-done | bytes 262176 | tf_op jit(solution)/shard_map/ppermute | solution.py:30
  64.6 4.4 collective-permute-start.12
  72.7 17.3 %collective-permute-done.14.refs_2_ = bf16[64,2048]{1,0:T(8,128)(2,1)} collective-permute-done((bf16[64,2048]{1,0:T(8,128)(2,1)S(1)}, bf16[64,2048]{1,0:T(8,128)(2,1)}, u32[]{:S(2)}, u32[]{:S(2)}) %collective-permute-start.14) | collective-permute-done | bytes 262176 | tf_op jit(solution)/shard_map/ppermute | solution.py:30
  95.5 4.2 all-to-all-start.1
  107.1 11.4 %attend.2 = (bf16[1,4,256,256]{3,2,1,0:T(8,128)(2,1)S(1)}, bf16[1,256,1024]{2,1,0:T(8,128)(2,1)S(1)}, bf16[1,1024,128]{2,1,0:T(8,128)(2,1)S(1)}, f32[1,8,1024]{2,1,0:T(8,128)S(1)}) custom-call(s32[1]{0:T(128)} %bitcast.7.m_ref, bf16[512,2048]{1,0:T(8,128)(2,1)S(1)} %copy-done.17, bf16[512,2048]{1,0:T(8,128)(2,1)} %copy-done.35, ...), custom_call_target="tpu_custom_call" | custom-call | flops 1 | bytes 1 | tf_op jit(solution)/shard_map/attend/pallas_call | solution.py:512
  120.7 7.4 %collective-permute-done.18.refs_3_ = bf16[64,2048]{1,0:T(8,128)(2,1)S(1)} collective-permute-done((bf16[64,2048]{1,0:T(8,128)(2,1)}, bf16[64,2048]{1,0:T(8,128)(2,1)S(1)}, u32[]{:S(2)}, u32[]{:S(2)}) %collective-permute-start.18) | collective-permute-done | bytes 262176 | tf_op jit(solution)/shard_map/ppermute | solution.py:30
  129.4 11.9 %attend.3 = (bf16[1,4,256,256]{3,2,1,0:T(8,128)(2,1)S(1)}, bf16[1,256,1024]{2,1,0:T(8,128)(2,1)S(1)}, bf16[1,1024,128]{2,1,0:T(8,128)(2,1)S(1)}, f32[1,8,1024]{2,1,0:T(8,128)S(1)}) custom-call(s32[1]{0:T(128)} %bitcast.7.m_ref, bf16[512,2048]{1,0:T(8,128)(2,1)} %norm.3.refs_0_, bf16[512,2048]{1,0:T(8,128)(2,1)} %collective-permute-done.17.refs_1_, ...), custom_call_target="tpu_custom_call" | custom-call | flops 1 | bytes 1 | tf_op jit(solution)/shard_map/attend/pallas_call | solution.py:512
  141.4 6.8 %collective-permute-done.22.refs_2_ = bf16[176,2048]{1,0:T(8,128)(2,1)S(1)} collective-permute-done((bf16[176,2048]{1,0:T(8,128)(2,1)}, bf16[176,2048]{1,0:T(8,128)(2,1)S(1)}, u32[]{:S(2)}, u32[]{:S(2)}) %collective-permute-start.22) | collective-permute-done | bytes 720928 | tf_op jit(solution)/shard_map/ppermute | solution.py:30
  160.4 10.3 %collective-permute-done.25.refs_4_ = bf16[128,2048]{1,0:T(8,128)(2,1)S(1)} collective-permute-done((bf16[128,2048]{1,0:T(8,128)(2,1)S(1)}, bf16[128,2048]{1,0:T(8,128)(2,1)S(1)}, u32[]{:S(2)}, u32[]{:S(2)}) %collective-permute-start.25) | collective-permute-done | bytes 524320 | tf_op jit(solution)/shard_map/ppermute | solution.py:25
  178.2 23.6 %collective-permute-done.26.from_two.refs_2_ = bf16[256,2048]{1,0:T(8,128)(2,1)S(1)} collective-permute-done((bf16[256,2048]{1,0:T(8,128)(2,1)S(1)}, bf16[256,2048]{1,0:T(8,128)(2,1)S(1)}, u32[]{:S(2)}, u32[]{:S(2)}) %collective-permute-start.26) | collective-permute-done | bytes 1048608 | tf_op jit(solution)/shard_map/ppermute | solution.py:25
  206.6 10.4 %collective-permute-done.29.refs_4_ = bf16[128,2048]{1,0:T(8,128)(2,1)S(1)} collective-permute-done((bf16[128,2048]{1,0:T(8,128)(2,1)S(1)}, bf16[128,2048]{1,0:T(8,128)(2,1)S(1)}, u32[]{:S(2)}, u32[]{:S(2)}) %collective-permute-start.29) | collective-permute-done | bytes 524320 | tf_op jit(solution)/shard_map/ppermute | solution.py:25
  222.6 21.2 %collective-permute-done.32.refs_2_ = bf16[256,2048]{1,0:T(8,128)(2,1)S(1)} collective-permute-done((bf16[256,2048]{1,0:T(8,128)(2,1)S(1)}, bf16[256,2048]{1,0:T(8,128)(2,1)S(1)}, u32[]{:S(2)}, u32[]{:S(2)}) %collective-permute-start.32) | collective-permute-done | bytes 1048608 | tf_op jit(solution)/shard_map/ppermute | solution.py:25
  245.5 11.4 %collective-permute-done.35.refs_3_ = bf16[176,2048]{1,0:T(8,128)(2,1)S(1)} collective-permute-done((bf16[176,2048]{1,0:T(8,128)(2,1)S(1)}, bf16[176,2048]{1,0:T(8,128)(2,1)S(1)}, u32[]{:S(2)}, u32[]{:S(2)}) %collective-permute-start.35) | collective-permute-done | bytes 720928 | tf_op jit(solution)/shard_map/ppermute | solution.py:30
  263.9 10.5 %all-gather.2.cloned.1.call-done.refs_0_ = bf16[2048,1408]{1,0:T(8,128)(2,1)} async-done(((bf16[512,1408]{1,0:T(8,128)(2,1)}), bf16[2048,1408]{1,0:T(8,128)(2,1)}) %all-gather.2.cloned.1.call-update) | async-done | bytes 5767184 | tf_op jit(solution)/shard_map/all_gather | solution.py:50
  280.1 9.6 %fusion.14 = f32[1024,1408]{1,0:T(8,128)S(1)} fusion(bf16[1024,2048]{1,0:T(8,128)(2,1)} %join.9, bf16[2048,1408]{1,0:T(8,128)(2,1)S(1)} %join.10), kind=kOutput, calls=%fused_computation.65 | convolution fusion | flops 5905580032 | bytes 15728640 | tf_op jit(solution)/shard_map/dot_general | solution.py:338
  292.3 8.5 %fusion.15 = f32[1024,1408]{1,0:T(8,128)S(1)} fusion(bf16[1024,2048]{1,0:T(8,128)(2,1)} %collective-permute-done.36, bf16[2048,1408]{1,0:T(8,128)(2,1)S(1)} %join.10), kind=kOutput, calls=%fused_computation.66 | convolution fusion | flops 5905580032 | bytes 15728640 | tf_op jit(solution)/shard_map/dot_general | solution.py:338
  303.2 3.6 convolution_convert_fusion.3
  307.4 4.0 convolution_convert_fusion.2.even.refs_0_
  311.4 9.4 %fusion.16 = f32[704,2048]{1,0:T(8,128)} fusion(bf16[1024,704]{1,0:T(8,128)(2,1)S(1)} %multiply_convert_fusion.4, bf16[1024,2048]{1,0:T(8,128)(2,1)} %collective-permute-done.28), kind=kOutput, calls=%fused_computation.67 | convolution fusion | flops 2952790016 | bytes 11403264 | tf_op jit(solution)/shard_map/dot_general | solution.py:342
  326.4 6.5 add_convert_fusion.1
  332.8 9.2 %multiply_convert_fusion.3 = (bf16[1024,704]{1,0:T(8,128)(2,1)S(1)}, bf16[1024,704]{1,0:T(8,128)(2,1)S(1)}) fusion(f32[1024,1408]{1,0:T(8,128)} %copy-done.106, bf16[1024,2048]{1,0:T(8,128)(2,1)} %collective-permute-done.28, bf16[704,2048]{1,0:T(8,128)(2,1)} %copy-done.52), kind=kOutput, calls=%fused_computation.9 | convolution fusion | flops 2962161664 | bytes 15728640 | tf_op jit(solution)/shard_map/dot_general | solution.py:346
  342.1 8.3 %convolution_convert_fusion.1 = bf16[1024,2048]{1,0:T(8,128)(2,1)} fusion(bf16[2048,1408]{1,0:T(8,128)(2,1)S(1)} %bitcast.56, bf16[1024,704]{1,0:T(8,128)(2,1)S(1)} %get-tuple-element.302, bf16[1024,704]{1,0:T(8,128)(2,1)S(1)} %get-tuple-element.301), kind=kOutput, calls=%fused_computation.3 | convolution fusion | flops 5913444352 | bytes 12845056 | tf_op jit(solution)/shard_map/dot_general | solution.py:346
  351.2 9.8 %multiply_convert_fusion.1 = (bf16[1024,704]{1,0:T(8,128)(2,1)S(1)}, bf16[1024,704]{1,0:T(8,128)(2,1)S(1)}) fusion(f32[1024,1408]{1,0:T(8,128)} %copy-done.105, bf16[1024,2048]{1,0:T(8,128)(2,1)} %copy-done.48, bf16[704,2048]{1,0:T(8,128)(2,1)} %copy-done.52), kind=kOutput, calls=%fused_computation.7 | convolution fusion | flops 2962161664 | bytes 15728640 | tf_op jit(solution)/shard_map/dot_general | solution.py:346
  364.2 9.0 %convolution_convert_fusion.even.refs_0_ = bf16[1024,2048]{1,0:T(8,128)(2,1)S(1)} fusion(bf16[2048,1408]{1,0:T(8,128)(2,1)} %copy-done.38, bf16[1024,704]{1,0:T(8,128)(2,1)S(1)} %get-tuple-element.300, bf16[1024,704]{1,0:T(8,128)(2,1)S(1)} %get-tuple-element.299), kind=kOutput, calls=%fused_computation.2 | convolution fusion | flops 5913444352 | bytes 12845056 | tf_op jit(solution)/shard_map/dot_general | solution.py:346
  373.3 5.3 send_rows.6
  389.8 9.5 %fusion = f32[2048,1408]{1,0:T(8,128)S(1)} fusion(bf16[1024,2048]{1,0:T(8,128)(2,1)} %collective-permute-done.36, bf16[1024,704]{1,0:T(8,128)(2,1)} %copy-done.111, bf16[1024,704]{1,0:T(8,128)(2,1)S(1)} %copy-done.110), kind=kOutput, calls=%fused_computation.18 | convolution fusion | flops 5911347200 | bytes 18612224 | tf_op jit(solution)/shard_map/dot_general | solution.py:342
  399.3 12.5 %add_convert_fusion = bf16[2048,1408]{1,0:T(8,128)(2,1)} fusion(f32[2048,1408]{1,0:T(8,128)S(1)} %fusion, bf16[1024,2048]{1,0:T(8,128)(2,1)} %join.9, bf16[1024,704]{1,0:T(8,128)(2,1)S(1)} %copy-done.115, bf16[1024,704]{1,0:T(8,128)(2,1)S(1)} %copy-done.113), kind=kOutput, calls=%fused_computation | convolution fusion | flops 5917114368 | bytes 24379392 | tf_op jit(solution)/shard_map/dot_general | solution.py:342
  416.8 3.9 pass_rows.6
  421.0 12.3 %collective-permute-done.45.refs_4_ = bf16[128,2048]{1,0:T(8,128)(2,1)S(1)} collective-permute-done((bf16[128,2048]{1,0:T(8,128)(2,1)S(1)}, bf16[128,2048]{1,0:T(8,128)(2,1)S(1)}, u32[]{:S(2)}, u32[]{:S(2)}) %collective-permute-start.45) | collective-permute-done | bytes 524320 | tf_op jit(solution)/shard_map/ppermute | solution.py:25
  434.6 4.9 middle_back.1
  450.5 13.2 %collective-permute-done.49.refs_0_ = bf16[256,2048]{1,0:T(8,128)(2,1)} collective-permute-done((bf16[256,2048]{1,0:T(8,128)(2,1)}, bf16[256,2048]{1,0:T(8,128)(2,1)}, u32[]{:S(2)}, u32[]{:S(2)}) %collective-permute-start.49) | collective-permute-done | bytes 1048608 | tf_op jit(solution)/shard_map/ppermute | solution.py:25
  463.7 4.4 collective-permute-done.47.refs_1_
  475.1 15.8 %attend_back.2 = (bf16[1,4,256,256]{3,2,1,0:T(8,128)(2,1)S(1)}, f32[1,4,256,64]{3,2,1,0:T(8,128)S(1)}, f32[1,4,256,64]{3,2,1,0:T(8,128)S(1)}) custom-call(s32[1]{0:T(128)} %bitcast.7.m_ref, bf16[256,2048]{1,0:T(8,128)(2,1)} %get-tuple-element.251.refs_0_, bf16[256,2048]{1,0:T(8,128)(2,1)} %collective-permute-done.47.refs_1_, ...), custom_call_target="tpu_custom_call" | custom-call | flops 1 | bytes 1 | tf_op jit(solution)/shard_map/attend_back/pallas_call | solution.py:512
  499.0 14.8 %attend_back.3 = (bf16[1,4,256,256]{3,2,1,0:T(8,128)(2,1)S(1)}, f32[1,4,256,64]{3,2,1,0:T(8,128)S(1)}, f32[1,4,256,64]{3,2,1,0:T(8,128)S(1)}) custom-call(s32[1]{0:T(128)} %bitcast.7.m_ref, bf16[512,2048]{1,0:T(8,128)(2,1)} %copy-done.14, bf16[512,2048]{1,0:T(8,128)(2,1)} %copy-done.33, bf16[1,256,1024]{2,1,0:T(8,128)(2,1)S(1)} %copy-done.74, ...), custom_call_target="tpu_custom_call" | custom-call | flops 1 | bytes 1 | tf_op jit(solution)/shard_map/attend_back/pallas_call | solution.py:512
  516.2 4.7 odd_parts.3
  538.1 3.7 send_rows.7
  542.8 4.7 all-to-all-start.2
  547.6 11.2 %collective-permute-done.62 = bf16[64,2048]{1,0:T(8,128)(2,1)} collective-permute-done((bf16[64,2048]{1,0:T(8,128)(2,1)}, bf16[64,2048]{1,0:T(8,128)(2,1)}, u32[]{:S(2)}, u32[]{:S(2)}) %collective-permute-start.62) | collective-permute-done | bytes 262176 | tf_op jit(solution)/shard_map/ppermute | solution.py:30
  562.7 4.9 collective-permute-done.57.from_two.refs_2_
  575.4 4.5 collective-permute-start.59
  586.6 7.6 %collective-permute-done.59.refs_4_ = bf16[128,2048]{1,0:T(8,128)(2,1)} collective-permute-done((bf16[128,2048]{1,0:T(8,128)(2,1)}, bf16[128,2048]{1,0:T(8,128)(2,1)}, u32[]{:S(2)}, u32[]{:S(2)}) %collective-permute-start.59) | collective-permute-done | bytes 524320 | tf_op jit(solution)/shard_map/ppermute | solution.py:25
  599.3 5.3 input_back.1
  606.7 4.1 collective-permute-start.67
  613.0 6.5 all-to-all-start.3
  622.4 16.9 %all-to-all-done.3.parts = bf16[8,64,320]{2,1,0:T(8,128)(2,1)} async-done(((bf16[8,64,320]{2,1,0:T(8,128)(2,1)}), bf16[8,64,320]{2,1,0:T(8,128)(2,1)}, u32[]{:S(2)}, u32[]{:S(2)}) %all-to-all-start.3) | async-done | bytes 327712 | tf_op jit(solution)/shard_map/all_to_all | solution.py:39
  (444 shorter events, 206.4 us)
Async XLA Ops:
  10.6 25.4 %all-to-all-start = ((bf16[8,64,384]{2,1,0:T(8,128)(2,1)}), bf16[8,64,384]{2,1,0:T(8,128)(2,1)S(1)}, u32[]{:S(2)}, u32[]{:S(2)}) async-start(bf16[8,64,384]{2,1,0:T(8,128)(2,1)} %attn_parts.1), calls=%async_computation | async-start | bytes 786432 | tf_op jit(solution)/shard_map/all_to_all | solution.py:39
  36.1 27.6 %collective-permute-start.8 = (bf16[256,2048]{1,0:T(8,128)(2,1)S(1)}, bf16[256,2048]{1,0:T(8,128)(2,1)S(1)}, u32[]{:S(2)}, u32[]{:S(2)}) collective-permute-start(bf16[256,2048]{1,0:T(8,128)(2,1)S(1)} %copy-done.27), channel_id=1, source_target_pairs={{0,4},{1,5},{2,6},{3,7},{4,0},{5,1},{6,2},{7,3},{8,12},{9,13},{10,... | collective-permute-start | bytes 3145736 | tf_op jit(solution)/shard_map/ppermute | solution.py:25
  39.2 24.6 %collective-permute-start.7 = (bf16[256,2048]{1,0:T(8,128)(2,1)S(1)}, bf16[256,2048]{1,0:T(8,128)(2,1)S(1)}, u32[]{:S(2)}, u32[]{:S(2)}) collective-permute-start(bf16[256,2048]{1,0:T(8,128)(2,1)S(1)} %copy-done.27), channel_id=1, source_target_pairs={{0,2},{1,3},{2,0},{3,1},{4,6},{5,7},{6,4},{7,5},{8,10},{9,11},{10,... | collective-permute-start | bytes 3145736 | tf_op jit(solution)/shard_map/ppermute | solution.py:25
  64.6 26.1 %collective-permute-start.12 = (bf16[512,2048]{1,0:T(8,128)(2,1)S(1)}, bf16[512,2048]{1,0:T(8,128)(2,1)S(1)}, u32[]{:S(2)}, u32[]{:S(2)}) collective-permute-start(bf16[512,2048]{1,0:T(8,128)(2,1)S(1)} %norm.2.refs_0_), channel_id=1, source_target_pairs={{0,1},{1,0},{2,3},{3,2},{4,5},{5,4},{6,7},{7,6},{8,9},{9,8},{10,11... | collective-permute-start | bytes 6291464 | tf_op jit(solution)/shard_map/ppermute | solution.py:25
  70.5 20.2 %collective-permute-start.16 = (bf16[128,2048]{1,0:T(8,128)(2,1)S(1)}, bf16[128,2048]{1,0:T(8,128)(2,1)S(1)}, u32[]{:S(2)}, u32[]{:S(2)}) collective-permute-start(bf16[128,2048]{1,0:T(8,128)(2,1)S(1)} %slice.48), channel_id=1, source_target_pairs={{0,2},{1,3},{2,0},{3,1},{4,6},{5,7},{6,4},{7,5},{8,10},{9,11},{10,... | collective-permute-start | bytes 1572872 | tf_op jit(solution)/shard_map/ppermute | solution.py:25
  71.7 19.0 %collective-permute-start.15 = (bf16[128,2048]{1,0:T(8,128)(2,1)S(1)}, bf16[128,2048]{1,0:T(8,128)(2,1)S(1)}, u32[]{:S(2)}, u32[]{:S(2)}) collective-permute-start(bf16[128,2048]{1,0:T(8,128)(2,1)S(1)} %slice.47), channel_id=1, source_target_pairs={{0,4},{1,5},{2,6},{3,7},{4,0},{5,1},{6,2},{7,3},{8,12},{9,13},{10,... | collective-permute-start | bytes 1572872 | tf_op jit(solution)/shard_map/ppermute | solution.py:25
  72.2 17.8 %collective-permute-start.13 = (bf16[512,384]{1,0:T(8,128)(2,1)S(1)}, bf16[512,384]{1,0:T(8,128)(2,1)S(1)}, u32[]{:S(2)}, u32[]{:S(2)}) collective-permute-start(bf16[512,384]{1,0:T(8,128)(2,1)S(1)} %collective-permute-done.10.refs_2_), channel_id=1, source_target_pairs={{0,8},{1,9},{2,10},{3,11},{4,12},{5,13},{6,14},{7,15},{8,16},{9,17... | collective-permute-start | bytes 1179656 | tf_op jit(solution)/shard_map/ppermute | solution.py:30
  72.2 17.8 %collective-permute-start.14 = (bf16[64,2048]{1,0:T(8,128)(2,1)S(1)}, bf16[64,2048]{1,0:T(8,128)(2,1)}, u32[]{:S(2)}, u32[]{:S(2)}) collective-permute-start(bf16[64,2048]{1,0:T(8,128)(2,1)S(1)} %collective-permute-done.11.refs_1_), channel_id=1, source_target_pairs={{0,8},{1,9},{2,10},{3,11},{4,12},{5,13},{6,14},{7,15},{8,16},{9,17... | collective-permute-start | bytes 786440 | tf_op jit(solution)/shard_map/ppermute | solution.py:30
  94.3 34.5 %collective-permute-start.17 = (bf16[512,2048]{1,0:T(8,128)(2,1)}, bf16[512,2048]{1,0:T(8,128)(2,1)}, u32[]{:S(2)}, u32[]{:S(2)}) collective-permute-start(bf16[512,2048]{1,0:T(8,128)(2,1)} %norm.3.refs_0_), channel_id=1, source_target_pairs={{0,1},{1,0},{2,3},{3,2},{4,5},{5,4},{6,7},{7,6},{8,9},{9,8},{10,11... | collective-permute-start | bytes 6291464 | tf_op jit(solution)/shard_map/ppermute | solution.py:25
  95.5 33.3 %all-to-all-start.1 = ((bf16[8,64,1408]{2,1,0:T(8,128)(2,1)}), bf16[8,64,1408]{2,1,0:T(8,128)(2,1)}, u32[]{:S(2)}, u32[]{:S(2)}) async-start(bf16[8,64,1408]{2,1,0:T(8,128)(2,1)} %mlp_parts.1), calls=%async_computation.1 | async-start | bytes 2883584 | tf_op jit(solution)/shard_map/all_to_all | solution.py:39
  99.8 174.6 %all-gather.2.cloned.1.call-start = ((), (), s32[]{:S(2)}) async-start(), calls=%async_computation.6 | async-start | bytes 7208960 | tf_op jit(solution)/shard_map/all_gather | solution.py:50
  102.7 26.1 %collective-permute-start.19 = (bf16[176,2048]{1,0:T(8,128)(2,1)}, bf16[176,2048]{1,0:T(8,128)(2,1)}, u32[]{:S(2)}, u32[]{:S(2)}) collective-permute-start(bf16[176,2048]{1,0:T(8,128)(2,1)} %refs_0_.2), channel_id=1, source_target_pairs={{0,8},{1,9},{2,10},{3,11},{4,12},{5,13},{6,14},{7,15},{8,16},{9,17... | collective-permute-start | bytes 2162696 | tf_op jit(solution)/shard_map/ppermute | solution.py:30
  102.7 38.6 %collective-permute-start.21 = (bf16[256,2048]{1,0:T(8,128)(2,1)}, bf16[256,2048]{1,0:T(8,128)(2,1)}, u32[]{:S(2)}, u32[]{:S(2)}) collective-permute-start(bf16[256,2048]{1,0:T(8,128)(2,1)} %above.1), channel_id=1, source_target_pairs={{0,4},{1,5},{2,6},{3,7},{4,0},{5,1},{6,2},{7,3},{8,12},{9,13},{10,... | collective-permute-start | bytes 3145736 | tf_op jit(solution)/shard_map/ppermute | solution.py:25
  104.1 37.3 %collective-permute-start.20 = (bf16[256,2048]{1,0:T(8,128)(2,1)}, bf16[256,2048]{1,0:T(8,128)(2,1)}, u32[]{:S(2)}, u32[]{:S(2)}) collective-permute-start(bf16[256,2048]{1,0:T(8,128)(2,1)} %above.1), channel_id=1, source_target_pairs={{0,2},{1,3},{2,0},{3,1},{4,6},{5,7},{6,4},{7,5},{8,10},{9,11},{10,... | collective-permute-start | bytes 3145736 | tf_op jit(solution)/shard_map/ppermute | solution.py:25
  105.3 22.8 %collective-permute-start.18 = (bf16[64,2048]{1,0:T(8,128)(2,1)}, bf16[64,2048]{1,0:T(8,128)(2,1)S(1)}, u32[]{:S(2)}, u32[]{:S(2)}) collective-permute-start(bf16[64,2048]{1,0:T(8,128)(2,1)} %collective-permute-done.14.refs_2_), channel_id=1, source_target_pairs={{0,8},{1,9},{2,10},{3,11},{4,12},{5,13},{6,14},{7,15},{8,16},{9,17... | collective-permute-start | bytes 786440 | tf_op jit(solution)/shard_map/ppermute | solution.py:30
  128.8 19.4 %collective-permute-start.22 = (bf16[176,2048]{1,0:T(8,128)(2,1)}, bf16[176,2048]{1,0:T(8,128)(2,1)S(1)}, u32[]{:S(2)}, u32[]{:S(2)}) collective-permute-start(bf16[176,2048]{1,0:T(8,128)(2,1)} %collective-permute-done.19.refs_1_), channel_id=1, source_target_pairs={{0,8},{1,9},{2,10},{3,11},{4,12},{5,13},{6,14},{7,15},{8,16},{9,17... | collective-permute-start | bytes 2162696 | tf_op jit(solution)/shard_map/ppermute | solution.py:30
  152.8 18.7 %collective-permute-start.23 = (bf16[1024,2048]{1,0:T(8,128)(2,1)}, bf16[1024,2048]{1,0:T(8,128)(2,1)}, u32[]{:S(2)}, u32[]{:S(2)}) collective-permute-start(bf16[1024,2048]{1,0:T(8,128)(2,1)} %odd_parts.2), channel_id=1, source_target_pairs={{0,1},{1,0},{2,3},{3,2},{4,5},{5,4},{6,7},{7,6},{8,9},{9,8},{10,11... | collective-permute-start | bytes 12582920 | tf_op jit(solution)/shard_map/ppermute | solution.py:25
  154.6 257.3 %reduce-scatter.3.cloned.1.call-start = ((), (), s32[]{:S(2)}) async-start(), calls=%async_computation.7 | async-start | bytes 3604480 | tf_op jit(solution)/shard_map/reduce_scatter | solution.py:54
  175.9 26.0 %collective-permute-start.28 = (bf16[1024,2048]{1,0:T(8,128)(2,1)S(1)}, bf16[1024,2048]{1,0:T(8,128)(2,1)}, u32[]{:S(2)}, u32[]{:S(2)}) collective-permute-start(bf16[1024,2048]{1,0:T(8,128)(2,1)S(1)} %join.8), channel_id=1, source_target_pairs={{0,1},{1,0},{2,3},{3,2},{4,5},{5,4},{6,7},{7,6},{8,9},{9,8},{10,11... | collective-permute-start | bytes 12582920 | tf_op jit(solution)/shard_map/ppermute | solution.py:25
  177.0 24.8 %collective-permute-start.26 = (bf16[256,2048]{1,0:T(8,128)(2,1)S(1)}, bf16[256,2048]{1,0:T(8,128)(2,1)S(1)}, u32[]{:S(2)}, u32[]{:S(2)}) collective-permute-start(bf16[256,2048]{1,0:T(8,128)(2,1)S(1)} %get-tuple-element.192), channel_id=1, source_target_pairs={{0,2},{1,3},{2,0},{3,1},{4,6},{5,7},{6,4},{7,5},{8,10},{9,11},{10,... | collective-permute-start | bytes 3145736 | tf_op jit(solution)/shard_map/ppermute | solution.py:25
  177.4 24.5 %collective-permute-start.27 = (bf16[256,2048]{1,0:T(8,128)(2,1)S(1)}, bf16[256,2048]{1,0:T(8,128)(2,1)S(1)}, u32[]{:S(2)}, u32[]{:S(2)}) collective-permute-start(bf16[256,2048]{1,0:T(8,128)(2,1)S(1)} %get-tuple-element.193), channel_id=1, source_target_pairs={{0,4},{1,5},{2,6},{3,7},{4,0},{5,1},{6,2},{7,3},{8,12},{9,13},{10,... | collective-permute-start | bytes 3145736 | tf_op jit(solution)/shard_map/ppermute | solution.py:25
  221.2 22.6 %collective-permute-start.32 = (bf16[256,2048]{1,0:T(8,128)(2,1)S(1)}, bf16[256,2048]{1,0:T(8,128)(2,1)S(1)}, u32[]{:S(2)}, u32[]{:S(2)}) collective-permute-start(bf16[256,2048]{1,0:T(8,128)(2,1)S(1)} %get-tuple-element.207.refs_0_), channel_id=1, source_target_pairs={{0,4},{1,5},{2,6},{3,7},{4,0},{5,1},{6,2},{7,3},{8,12},{9,13},{10,... | collective-permute-start | bytes 3145736 | tf_op jit(solution)/shard_map/ppermute | solution.py:25
  222.2 22.3 %collective-permute-start.31 = (bf16[256,2048]{1,0:T(8,128)(2,1)S(1)}, bf16[256,2048]{1,0:T(8,128)(2,1)S(1)}, u32[]{:S(2)}, u32[]{:S(2)}) collective-permute-start(bf16[256,2048]{1,0:T(8,128)(2,1)S(1)} %get-tuple-element.207.refs_0_), channel_id=1, source_target_pairs={{0,2},{1,3},{2,0},{3,1},{4,6},{5,7},{6,4},{7,5},{8,10},{9,11},{10,... | collective-permute-start | bytes 3145736 | tf_op jit(solution)/shard_map/ppermute | solution.py:25
  222.6 34.3 %collective-permute-start.35 = (bf16[176,2048]{1,0:T(8,128)(2,1)S(1)}, bf16[176,2048]{1,0:T(8,128)(2,1)S(1)}, u32[]{:S(2)}, u32[]{:S(2)}) collective-permute-start(bf16[176,2048]{1,0:T(8,128)(2,1)S(1)} %copy-done.70), channel_id=1, source_target_pairs={{0,8},{1,9},{2,10},{3,11},{4,12},{5,13},{6,14},{7,15},{8,16},{9,17... | collective-permute-start | bytes 2162696 | tf_op jit(solution)/shard_map/ppermute | solution.py:30
  260.3 32.1 %collective-permute-start.36 = (bf16[1024,2048]{1,0:T(8,128)(2,1)}, bf16[1024,2048]{1,0:T(8,128)(2,1)}, u32[]{:S(2)}, u32[]{:S(2)}) collective-permute-start(bf16[1024,2048]{1,0:T(8,128)(2,1)} %join.9), channel_id=1, source_target_pairs={{0,1},{1,0},{2,3},{3,2},{4,5},{5,4},{6,7},{7,6},{8,9},{9,8},{10,11... | collective-permute-start | bytes 12582920 | tf_op jit(solution)/shard_map/ppermute | solution.py:25
  324.0 27.2 %collective-permute-start.38 = (bf16[256,2048]{1,0:T(8,128)(2,1)}, bf16[256,2048]{1,0:T(8,128)(2,1)}, u32[]{:S(2)}, u32[]{:S(2)}) collective-permute-start(bf16[256,2048]{1,0:T(8,128)(2,1)} %get-tuple-element.221), channel_id=1, source_target_pairs={{0,2},{1,3},{2,0},{3,1},{4,6},{5,7},{6,4},{7,5},{8,10},{9,11},{10,... | collective-permute-start | bytes 3145736 | tf_op jit(solution)/shard_map/ppermute | solution.py:25
  325.2 26.0 %collective-permute-start.39 = (bf16[256,2048]{1,0:T(8,128)(2,1)}, bf16[256,2048]{1,0:T(8,128)(2,1)}, u32[]{:S(2)}, u32[]{:S(2)}) collective-permute-start(bf16[256,2048]{1,0:T(8,128)(2,1)} %get-tuple-element.224), channel_id=1, source_target_pairs={{0,4},{1,5},{2,6},{3,7},{4,0},{5,1},{6,2},{7,3},{8,12},{9,13},{10,... | collective-permute-start | bytes 3145736 | tf_op jit(solution)/shard_map/ppermute | solution.py:25
  350.4 22.8 %collective-permute-start.41 = (bf16[1024,2048]{1,0:T(8,128)(2,1)}, bf16[1024,2048]{1,0:T(8,128)(2,1)}, u32[]{:S(2)}, u32[]{:S(2)}) collective-permute-start(bf16[1024,2048]{1,0:T(8,128)(2,1)} %convolution_convert_fusion.1), channel_id=1, source_target_pairs={{0,1},{1,0},{2,3},{3,2},{4,5},{5,4},{6,7},{7,6},{8,9},{9,8},{10,11... | collective-permute-start | bytes 12582920 | tf_op jit(solution)/shard_map/ppermute | solution.py:25
  351.1 190.8 %reduce-scatter.5.cloned.1.call-start = ((), (), s32[]{:S(2)}) async-start(), calls=%async_computation.8 | async-start | bytes 7208960 | tf_op jit(solution)/shard_map/reduce_scatter | solution.py:54
  364.1 17.3 %collective-permute-start.40 = (bf16[128,2048]{1,0:T(8,128)(2,1)S(1)}, bf16[128,2048]{1,0:T(8,128)(2,1)S(1)}, u32[]{:S(2)}, u32[]{:S(2)}) collective-permute-start(bf16[128,2048]{1,0:T(8,128)(2,1)S(1)} %get-tuple-element.227), channel_id=1, source_target_pairs={{0,2},{1,3},{2,0},{3,1},{4,6},{5,7},{6,4},{7,5},{8,10},{9,11},{10,... | collective-permute-start | bytes 1572872 | tf_op jit(solution)/shard_map/ppermute | solution.py:25
  364.1 18.0 %collective-permute-start.42 = (bf16[128,2048]{1,0:T(8,128)(2,1)S(1)}, bf16[128,2048]{1,0:T(8,128)(2,1)S(1)}, u32[]{:S(2)}, u32[]{:S(2)}) collective-permute-start(bf16[128,2048]{1,0:T(8,128)(2,1)S(1)} %get-tuple-element.231), channel_id=1, source_target_pairs={{0,4},{1,5},{2,6},{3,7},{4,0},{5,1},{6,2},{7,3},{8,12},{9,13},{10,... | collective-permute-start | bytes 1572872 | tf_op jit(solution)/shard_map/ppermute | solution.py:25
  378.5 35.7 %collective-permute-start.43 = (bf16[256,2048]{1,0:T(8,128)(2,1)}, bf16[256,2048]{1,0:T(8,128)(2,1)S(1)}, u32[]{:S(2)}, u32[]{:S(2)}) collective-permute-start(bf16[256,2048]{1,0:T(8,128)(2,1)} %get-tuple-element.229), channel_id=1, source_target_pairs={{0,2},{1,3},{2,0},{3,1},{4,6},{5,7},{6,4},{7,5},{8,10},{9,11},{10,... | collective-permute-start | bytes 3145736 | tf_op jit(solution)/shard_map/ppermute | solution.py:25
  379.9 34.3 %collective-permute-start.44 = (bf16[256,2048]{1,0:T(8,128)(2,1)}, bf16[256,2048]{1,0:T(8,128)(2,1)}, u32[]{:S(2)}, u32[]{:S(2)}) collective-permute-start(bf16[256,2048]{1,0:T(8,128)(2,1)} %get-tuple-element.230), channel_id=1, source_target_pairs={{0,4},{1,5},{2,6},{3,7},{4,0},{5,1},{6,2},{7,3},{8,12},{9,13},{10,... | collective-permute-start | bytes 3145736 | tf_op jit(solution)/shard_map/ppermute | solution.py:25
  440.8 22.9 %collective-permute-start.49 = (bf16[256,2048]{1,0:T(8,128)(2,1)}, bf16[256,2048]{1,0:T(8,128)(2,1)}, u32[]{:S(2)}, u32[]{:S(2)}) collective-permute-start(bf16[256,2048]{1,0:T(8,128)(2,1)} %get-tuple-element.251.refs_0_), channel_id=1, source_target_pairs={{0,4},{1,5},{2,6},{3,7},{4,0},{5,1},{6,2},{7,3},{8,12},{9,13},{10,... | collective-permute-start | bytes 3145736 | tf_op jit(solution)/shard_map/ppermute | solution.py:25
  440.8 22.9 %collective-permute-start.48 = (bf16[256,2048]{1,0:T(8,128)(2,1)}, bf16[256,2048]{1,0:T(8,128)(2,1)}, u32[]{:S(2)}, u32[]{:S(2)}) collective-permute-start(bf16[256,2048]{1,0:T(8,128)(2,1)} %get-tuple-element.251.refs_0_), channel_id=1, source_target_pairs={{0,1},{1,0},{2,3},{3,2},{4,5},{5,4},{6,7},{7,6},{8,9},{9,8},{10,11... | collective-permute-start | bytes 3145736 | tf_op jit(solution)/shard_map/ppermute | solution.py:25
  443.0 25.1 %collective-permute-start.47 = (bf16[256,2048]{1,0:T(8,128)(2,1)}, bf16[256,2048]{1,0:T(8,128)(2,1)}, u32[]{:S(2)}, u32[]{:S(2)}) collective-permute-start(bf16[256,2048]{1,0:T(8,128)(2,1)} %get-tuple-element.251.refs_0_), channel_id=1, source_target_pairs={{0,2},{1,3},{2,0},{3,1},{4,6},{5,7},{6,4},{7,5},{8,10},{9,11},{10,... | collective-permute-start | bytes 3145736 | tf_op jit(solution)/shard_map/ppermute | solution.py:25
  471.1 19.9 %collective-permute-start.53 = (bf16[128,2048]{1,0:T(8,128)(2,1)S(1)}, bf16[128,2048]{1,0:T(8,128)(2,1)S(1)}, u32[]{:S(2)}, u32[]{:S(2)}) collective-permute-start(bf16[128,2048]{1,0:T(8,128)(2,1)S(1)} %slice.61), channel_id=1, source_target_pairs={{0,2},{1,3},{2,0},{3,1},{4,6},{5,7},{6,4},{7,5},{8,10},{9,11},{10,... | collective-permute-start | bytes 1572872 | tf_op jit(solution)/shard_map/ppermute | solution.py:25
  472.6 18.4 %collective-permute-start.52 = (bf16[128,2048]{1,0:T(8,128)(2,1)S(1)}, bf16[128,2048]{1,0:T(8,128)(2,1)S(1)}, u32[]{:S(2)}, u32[]{:S(2)}) collective-permute-start(bf16[128,2048]{1,0:T(8,128)(2,1)S(1)} %slice.60), channel_id=1, source_target_pairs={{0,4},{1,5},{2,6},{3,7},{4,0},{5,1},{6,2},{7,3},{8,12},{9,13},{10,... | collective-permute-start | bytes 1572872 | tf_op jit(solution)/shard_map/ppermute | solution.py:25
  520.9 17.2 %collective-permute-start.56 = (bf16[1024,2048]{1,0:T(8,128)(2,1)}, bf16[1024,2048]{1,0:T(8,128)(2,1)}, u32[]{:S(2)}, u32[]{:S(2)}) collective-permute-start(bf16[1024,2048]{1,0:T(8,128)(2,1)} %odd_parts.3), channel_id=1, source_target_pairs={{0,1},{1,0},{2,3},{3,2},{4,5},{5,4},{6,7},{7,6},{8,9},{9,8},{10,11... | collective-permute-start | bytes 12582920 | tf_op jit(solution)/shard_map/ppermute | solution.py:25
  542.6 24.9 %collective-permute-start.57 = (bf16[256,2048]{1,0:T(8,128)(2,1)}, bf16[256,2048]{1,0:T(8,128)(2,1)S(1)}, u32[]{:S(2)}, u32[]{:S(2)}) collective-permute-start(bf16[256,2048]{1,0:T(8,128)(2,1)} %get-tuple-element.274), channel_id=1, source_target_pairs={{0,2},{1,3},{2,0},{3,1},{4,6},{5,7},{6,4},{7,5},{8,10},{9,11},{10,... | collective-permute-start | bytes 3145736 | tf_op jit(solution)/shard_map/ppermute | solution.py:25
  542.8 24.8 %collective-permute-start.58 = (bf16[256,2048]{1,0:T(8,128)(2,1)}, bf16[256,2048]{1,0:T(8,128)(2,1)S(1)}, u32[]{:S(2)}, u32[]{:S(2)}) collective-permute-start(bf16[256,2048]{1,0:T(8,128)(2,1)} %get-tuple-element.275), channel_id=1, source_target_pairs={{0,4},{1,5},{2,6},{3,7},{4,0},{5,1},{6,2},{7,3},{8,12},{9,13},{10,... | collective-permute-start | bytes 3145736 | tf_op jit(solution)/shard_map/ppermute | solution.py:25
  542.8 51.4 %all-to-all-start.2 = ((bf16[8,64,1408]{2,1,0:T(8,128)(2,1)}), bf16[8,64,1408]{2,1,0:T(8,128)(2,1)S(1)}, u32[]{:S(2)}, u32[]{:S(2)}) async-start(bf16[8,64,1408]{2,1,0:T(8,128)(2,1)} %bitcast.77), calls=%async_computation.4 | async-start | bytes 2883584 | tf_op jit(solution)/shard_map/all_to_all | solution.py:39
  560.8 19.1 %collective-permute-start.63 = (bf16[512,320]{0,1:T(8,128)(2,1)}, bf16[512,320]{0,1:T(8,128)(2,1)}, u32[]{:S(2)}, u32[]{:S(2)}) collective-permute-start(bf16[512,320]{0,1:T(8,128)(2,1)} %add_convert_fusion.4), channel_id=1, source_target_pairs={{0,8},{1,9},{2,10},{3,11},{4,12},{5,13},{6,14},{7,15},{8,16},{9,17... | collective-permute-start | bytes 983048 | tf_op jit(solution)/shard_map/ppermute | solution.py:30
  575.4 18.8 %collective-permute-start.59 = (bf16[128,2048]{1,0:T(8,128)(2,1)}, bf16[128,2048]{1,0:T(8,128)(2,1)}, u32[]{:S(2)}, u32[]{:S(2)}) collective-permute-start(bf16[128,2048]{1,0:T(8,128)(2,1)} %get-tuple-element.278), channel_id=1, source_target_pairs={{0,2},{1,3},{2,0},{3,1},{4,6},{5,7},{6,4},{7,5},{8,10},{9,11},{10,... | collective-permute-start | bytes 1572872 | tf_op jit(solution)/shard_map/ppermute | solution.py:25
  581.9 22.6 %collective-permute-start.65 = (bf16[512,320]{0,1:T(8,128)(2,1)}, bf16[512,320]{0,1:T(8,128)(2,1)}, u32[]{:S(2)}, u32[]{:S(2)}) collective-permute-start(bf16[512,320]{0,1:T(8,128)(2,1)} %add_convert_fusion.3), channel_id=1, source_target_pairs={{0,8},{1,9},{2,10},{3,11},{4,12},{5,13},{6,14},{7,15},{8,16},{9,17... | collective-permute-start | bytes 983048 | tf_op jit(solution)/shard_map/ppermute | solution.py:30
  583.8 20.8 %collective-permute-start.66 = (bf16[64,2048]{1,0:T(8,128)(2,1)}, bf16[64,2048]{1,0:T(8,128)(2,1)}, u32[]{:S(2)}, u32[]{:S(2)}) collective-permute-start(bf16[64,2048]{1,0:T(8,128)(2,1)} %add_convert_fusion.5), channel_id=1, source_target_pairs={{0,8},{1,9},{2,10},{3,11},{4,12},{5,13},{6,14},{7,15},{8,16},{9,17... | collective-permute-start | bytes 786440 | tf_op jit(solution)/shard_map/ppermute | solution.py:30
  606.7 38.0 %collective-permute-start.67 = (f32[64,2048]{1,0:T(8,128)}, f32[64,2048]{1,0:T(8,128)}, u32[]{:S(2)}, u32[]{:S(2)}) collective-permute-start(f32[64,2048]{1,0:T(8,128)} %convert_add_fusion), channel_id=1, source_target_pairs={{0,0},{8,1},{16,2},{24,3},{1,4},{9,5},{17,6},{25,7},{2,8},{10,9},{... | collective-permute-start | bytes 1572872 | tf_op jit(solution)/shard_map/ppermute | solution.py:815
  613.0 26.3 %all-to-all-start.3 = ((bf16[8,64,320]{2,1,0:T(8,128)(2,1)}), bf16[8,64,320]{2,1,0:T(8,128)(2,1)}, u32[]{:S(2)}, u32[]{:S(2)}) async-start(bf16[8,64,320]{2,1,0:T(8,128)(2,1)} %bitcast.76), calls=%async_computation.5 | async-start | bytes 786432 | tf_op jit(solution)/shard_map/all_to_all | solution.py:39
  (146 other events, 1959.5 us)
Sparse Core Ops, SparseCore 0:
  154.7 119.6 all-gather.1
  351.2 53.2 reduce-scatter.2
  414.4 100.0 reduce-scatter.4

commit v3 on v2

--- a/solution.py
+++ b/solution.py
@@ -118,52 +118,91 @@
     )(*ins)
 
 
-def send_kernel(even, peer, to_two, to_four):
-    rows = to_two.shape[0]
-    half = rows // 2
-
-    def summed(block, start):
-        span = slice(block * rows + start, block * rows + start + half)
-        return thin(wide(even[span]) + wide(peer[span]))
-
-    to_two[:half] = summed(1, 0)
-    to_two[half:] = summed(3, 0)
-    to_four[:half] = summed(2, half)
-    to_four[half:] = summed(3, half)
-
-
-def pass_kernel(even, peer, from_two, from_four, to_two, to_four):
-    half = to_two.shape[0]
-
-    def summed(block, start, arrived):
-        span = slice(block * 2 * half + start, block * 2 * half + start + half)
-        return thin(wide(even[span]) + wide(peer[span]) + wide(arrived[half:]))
-
-    to_four[...] = summed(2, 0, from_two)
-    to_two[...] = summed(1, half, from_four)
+def sliced_kernel(function, spans, whole, count, *refs):
+    distant, refs = refs[:whole], refs[whole:]
+    others, refs = refs[:count], refs[count:]
+    outs, held, done = refs[: -len(spans) - 1], refs[-len(spans) - 1 : -1], refs[-1]
+    copies = []
+    for i, (which, start, rows) in enumerate(spans):
+        source = distant[which].at[pl.ds(start, rows)]
+        copies.append(pltpu.make_async_copy(source, held[i], done.at[i]))
+        copies[-1].start()
+    for copy in copies:
+        copy.wait()
+    function(*others, *held, *outs)
+
+
+def on_spans(function, spans, others, outs, name, mebibytes=40):
+    arrays = []
+    for array, _, _ in spans:
+        if not any(array is known for known in arrays):
+            arrays.append(array)
+    which = lambda array: next(i for i, known in enumerate(arrays) if array is known)
+    places = tuple((which(array), start, rows) for array, start, rows in spans)
+    vmem = pl.BlockSpec(memory_space=pltpu.VMEM)
+    return pl.pallas_call(
+        functools.partial(sliced_kernel, function, places, len(arrays), len(others)),
+        in_specs=[ANY] * len(arrays) + [vmem] * len(others),
+        out_shape=[jax.ShapeDtypeStruct(shape, dtype) for shape, dtype in outs],
+        scratch_shapes=[pltpu.VMEM((rows, array.shape[1]), array.dtype) for array, _, rows in spans]
+        + [pltpu.SemaphoreType.DMA((len(spans),))],
+        compiler_params=pltpu.CompilerParams(vmem_limit_bytes=mebibytes * 2**20),
+        cost_estimate=WORK,
+        name=name,
+    )(*arrays, *others)
+
+
+def both(parts, start, rows):
+    return [(part, start, rows) for part in parts]
+
+
+def send_kernel(two_even, two_peer, four_even, four_peer, six_even, six_peer, to_two, to_four):
+    half = two_even.shape[0]
+    to_two[:half] = thin(wide(two_even[...]) + wide(two_peer[...]))
+    to_four[:half] = thin(wide(four_even[...]) + wide(four_peer[...]))
+    to_two[half:] = thin(wide(six_even[:half]) + wide(six_peer[:half]))
+    to_four[half:] = thin(wide(six_even[half:]) + wide(six_peer[half:]))
+
+
+def pass_kernel(four_even, four_peer, two_even, two_peer, from_two, from_four, to_two, to_four):
+    to_four[...] = thin(wide(four_even[...]) + wide(four_peer[...]) + wide(from_two[...]))
+    to_two[...] = thin(wide(two_even[...]) + wide(two_peer[...]) + wide(from_four[...]))
 
 
 def send_rows(parts):
     rows, cols = parts[0].shape
-    shape = ((rows // 4, cols), BF16)
-    return on_rows(send_kernel, parts, (shape, shape), "send_rows")
-
-
-def pass_rows(parts, arrived):
+    block, half = rows // 4, rows // 8
+    spans = both(parts, block, half) + both(parts, 2 * block + half, half)
+    spans += both(parts, 3 * block, block)
+    shape = ((block, cols), BF16)
+    return on_spans(send_kernel, spans, (), (shape, shape), "send_rows")
+
+
+def pass_rows(parts, arrived, mebibytes=40):
     rows, cols = parts[0].shape
-    shape = ((rows // 8, cols), BF16)
-    return on_rows(pass_kernel, (*parts, *arrived), (shape, shape), "pass_rows")
+    block, half = rows // 4, rows // 8
+    spans = both(parts, 2 * block, half) + both(parts, block + half, half)
+    spans += [(part, half, half) for part in arrived]
+    shape = ((half, cols), BF16)
+    return on_spans(pass_kernel, spans, (), (shape, shape), "pass_rows", mebibytes)
 
 
 def cross(to_two, to_four):
     return swap(to_two, 2), swap(to_four, 4)
+
+
+def own_spans(parts, arrived, last):
+    rows = parts[0].shape[0] // 4
+    half = rows // 2
+    first = [(part, 0, half) for part in arrived]
+    return both(parts, 0, rows) + first + [(part, 0, half) for part in last]
 
 
 def block_sum(even, peer, from_two, from_four, last_two, last_four):
     rows = last_two.shape[0]
     top, low = slice(0, rows), slice(rows, 2 * rows)
-    upper = wide(even[top]) + wide(peer[top]) + wide(from_two[top]) + wide(last_four[...])
-    lower = wide(even[low]) + wide(peer[low]) + wide(from_four[top]) + wide(last_two[...])
+    upper = wide(even[top]) + wide(peer[top]) + wide(from_two[...]) + wide(last_four[...])
+    lower = wide(even[low]) + wide(peer[low]) + wide(from_four[...]) + wide(last_two[...])
     return jnp.concatenate([upper, lower], axis=0)
 
 
@@ -385,15 +424,30 @@
         copy.wait()
 
 
+def heads_beside(stacked, heads):
+    return jnp.concatenate([stacked[h * HD : (h + 1) * HD] for h in range(heads)], axis=1)
+
+
+def heads_below(beside, heads):
+    rows = beside.shape[1] // heads
+    return jnp.concatenate([beside[:, h * rows : (h + 1) * rows] for h in range(heads)], axis=0)
+
+
+def causal(rows, heads):
+    key = lax.broadcasted_iota(jnp.int32, (rows, heads * rows), 0)
+    query = lax.broadcasted_iota(jnp.int32, (rows, heads * rows), 1)
+    return key <= query % rows
+
+
 def forward_kernel(heads, rows, count, m_ref, *refs):
     blocks, refs = refs[:count], refs[count:]
     weight_ref, cos_ref, sin_ref, mixed_ref, qt_ref, kv_ref, lse_ref, normed_ref, done = refs
     fetch(blocks, normed_ref, done)
     mine = m_ref[0]
     width = heads * HD
-    blocks = GROUP
     is_key = lax.broadcasted_iota(jnp.int32, (rows, 2 * HD), 1) < HD
-    for p in range(blocks):
+    ok = causal(rows, heads)
+    for p in range(GROUP):
         span = slice(p * rows, (p + 1) * rows)
         qkv = dot(normed_ref[spot_of(p, mine, rows), :], weight_ref[...])
         cosine, sine = cos_ref[span, :], sin_ref[span, :]
@@ -402,7 +456,7 @@
             part = qkv[:, start : start + 2 * HD]
             turned.append(part * cosine + partner(part) * sine)
         query = jnp.concatenate(turned, axis=1) * HD ** (-0.5)
-        qt_ref[0, :, span] = query.T.astype(BF16)
+        qt_ref[0, p] = heads_beside(query.T, heads).astype(BF16)
         part = qkv[:, width : width + 2 * HD]
         kv_ref[0, span, :] = jnp.where(
             is_key, part * cosine + partner(part) * sine, part
@@ -410,33 +464,25 @@
     kv = kv_ref[0]
     vt = kv.astype(F32).T.astype(BF16)[HD:, :]
     keys = kv[:, :HD]
-    ok = lax.broadcasted_iota(jnp.int32, (rows, rows), 0) <= lax.broadcasted_iota(
-        jnp.int32, (rows, rows), 1
-    )
-    for p in range(blocks):
+    for p in range(GROUP):
         span = slice(p * rows, (p + 1) * rows)
-        outs, tops = [], []
-        for h in range(heads):
-            query = qt_ref[0, h * HD : (h + 1) * HD, span]
-            last = jnp.where(ok, dot(keys[span], query), NEG)
-            top = jnp.max(last, axis=0, keepdims=True)
-            if p:
-                first = dot(keys[: p * rows], query)
-                top = jnp.maximum(top, jnp.max(first, axis=0, keepdims=True))
-            weight = jnp.exp(last - top)
-            total = jnp.sum(weight, axis=0, keepdims=True)
-            if p:
-                first = jnp.exp(first - top)
-                total = total + jnp.sum(first, axis=0, keepdims=True)
-            share = 1.0 / total
-            out = dot(vt[:, span], (weight * share).astype(BF16))
-            if p:
-                out = out + dot(vt[:, : p * rows], (first * share).astype(BF16))
-            outs.append(out)
-            tops.append(top + jnp.log(total))
-        mixed_ref[0, slot_of(p, mine)] = jnp.concatenate(outs, axis=0).T.astype(BF16)
-        tops += [tops[0]] * (8 - heads)
-        lse_ref[0, :, span] = jnp.concatenate(tops, axis=0)
+        query = qt_ref[0, p]
+        last = jnp.where(ok, dot(keys[span], query), NEG)
+        top = jnp.max(last, axis=0, keepdims=True)
+        if p:
+            first = dot(keys[: p * rows], query)
+            top = jnp.maximum(top, jnp.max(first, axis=0, keepdims=True))
+        last = jnp.exp(last - top)
+        total = jnp.sum(last, axis=0, keepdims=True)
+        if p:
+            first = jnp.exp(first - top)
+            total = total + jnp.sum(first, axis=0, keepdims=True)
+        share = 1.0 / total
+        out = dot(vt[:, span], (last * share).astype(BF16))
+        if p:
+            out = out + dot(vt[:, : p * rows], (first * share).astype(BF16))
+        mixed_ref[0, slot_of(p, mine)] = heads_below(out, heads).T.astype(BF16)
+        lse_ref[0, p] = top + jnp.log(total)
 
 
 def backward_kernel(heads, rows, count, m_ref, *refs):
@@ -446,44 +492,33 @@
     fetch(blocks, branch_ref, done)
     mine = m_ref[0]
     width = heads * HD
-    blocks = GROUP
     kv = kv_ref[0]
     kt = kv.astype(F32).T.astype(BF16)[:HD, :]
     keys = kv[:, :HD]
     values = pltpu.roll(kv.astype(F32), HD, 1).astype(BF16)[:, :HD]
-    ok = lax.broadcasted_iota(jnp.int32, (rows, rows), 0) <= lax.broadcasted_iota(
-        jnp.int32, (rows, rows), 1
-    )
-    for p in reversed(range(blocks)):
+    ok = causal(rows, heads)
+    for p in reversed(range(GROUP)):
         span = slice(p * rows, (p + 1) * rows)
         reach = (p + 1) * rows
         grad = thin(times_transposed(out_ref[...], branch_ref[spot_of(p, mine, rows), :]))
-        dqs = []
-        for h in range(heads):
-            query = qt_ref[0, h * HD : (h + 1) * HD, span]
-            above = grad[h * HD : (h + 1) * HD, :]
-            lse = lse_ref[0, h : h + 1, span]
-            scores = dot(keys[:reach], query)
-            if p:
-                scores = jnp.concatenate(
-                    [scores[: p * rows], jnp.where(ok, scores[p * rows :], NEG)], axis=0
-                )
-            else:
-                scores = jnp.where(ok, scores, NEG)
-            probs = jnp.exp(scores - lse)
-            probs_grad = dot(values[:reach], above)
-            delta = jnp.sum(probs * probs_grad, axis=0, keepdims=True)
-            score_low = (probs * (probs_grad - delta)).astype(BF16)
-            dk = times_transposed(score_low, query)
-            dv = times_transposed(probs.astype(BF16), above)
-            if p == blocks - 1 and h == 0:
-                dk_sum[...] = dk
-                dv_sum[...] = dv
-            else:
-                dk_sum[:reach, :] += dk
-                dv_sum[:reach, :] += dv
-            dqs.append(dot(kt[:, :reach], score_low))
-        dq = jnp.concatenate(dqs, axis=0).T * HD ** (-0.5)
+        above = heads_beside(grad, heads)
+        query = qt_ref[0, p]
+        scores = dot(keys[:reach], query)
+        last = jnp.where(ok, scores[p * rows :], NEG)
+        scores = jnp.concatenate([scores[: p * rows], last], axis=0) if p else last
+        probs = jnp.exp(scores - lse_ref[0, p])
+        probs_grad = dot(values[:reach], above)
+        delta = jnp.sum(probs * probs_grad, axis=0, keepdims=True)
+        score_low = (probs * (probs_grad - delta)).astype(BF16)
+        dk = times_transposed(score_low, query)
+        dv = times_transposed(probs.astype(BF16), above)
+        if p == GROUP - 1:
+            dk_sum[...] = dk
+            dv_sum[...] = dv
+        else:
+            dk_sum[:reach, :] += dk
+            dv_sum[:reach, :] += dv
+        dq = heads_below(dot(kt[:, :reach], score_low), heads).T * HD ** (-0.5)
         cosine, sine = cos_ref[span, :], sin_ref[span, :]
         turned = []
         for start in range(0, width, 2 * HD):
@@ -491,7 +526,7 @@
             turned.append(part * cosine - partner(part) * sine)
         dq_ref[0, slot_of(p, mine)] = jnp.concatenate(turned, axis=1).astype(BF16)
     is_key = lax.broadcasted_iota(jnp.int32, (rows, 2 * HD), 1) < HD
-    for p in range(blocks):
+    for p in range(GROUP):
         span = slice(p * rows, (p + 1) * rows)
         part = jnp.concatenate([dk_sum[span, :], dv_sum[span, :]], axis=1)
         cosine, sine = cos_ref[span, :], sin_ref[span, :]
@@ -534,9 +569,9 @@
     rows, width = length // GROUP, heads * HD
     shapes = (
         ((1, GROUP, rows, width), BF16),
-        ((1, width, length), BF16),
+        ((1, GROUP, HD, heads * rows), BF16),
         ((1, length, 2 * HD), BF16),
-        ((1, 8, length), F32),
+        ((1, GROUP, 1, heads * rows), F32),
     )
     kernel = functools.partial(forward_kernel, heads, rows, len(blocks))
     return attention_call(kernel, mine, blocks, (weight, *tables), shapes, [], "attend")
@@ -640,36 +675,33 @@
     clock.tick(attn_weight, far_even)
     out_ring.append(onward(clock(out_ring[2])))
     down_ring = [w_down, onward(clock(w_down))]
-    above_two, above_four = gather_pair(clock(cotangent))
 
     near_one_even, near_one_odd, far_one_even, far_one_odd = near_even, near_odd, far_even, far_odd
     near_mixed, *near_kept = attend((clock(near_even), near_odd), attn_weight, tables, mine, heads)
-    clock.tick(near_mixed, far_odd, out_ring[3], mlp_own, down_ring[1])
+    clock.tick(near_mixed, far_odd, mlp_own, down_ring[1])
+    above_two, above_four = gather_pair(clock(cotangent))
     down_ring.append(onward(clock(down_ring[1])))
     mlp_weight = planes_gather(clock(mlp_own))
     far_mixed, *far_kept = attend((clock(far_even), far_odd), attn_weight, tables, mine, heads)
     far_mixed, near_mixed = far_mixed.reshape(-1, width), near_mixed.reshape(-1, width)
-    clock.tick(far_mixed, above_two, above_four, down_ring[2])
-    down_ring.append(onward(clock(down_ring[2])))
-    above_six = gather_last(clock(above_two), clock(above_four))
+    clock.tick(far_mixed, out_ring[3])
     out_weight = place_rows(finish([clock(block) for block in out_ring]), plane)
     odd = parts_of(True, False, clock(near_mixed), far_mixed, out_weight)
     peer = swap(odd, 1)
     even = parts_of(False, False, after(near_mixed, odd), far_mixed, out_weight)
-    clock.tick(even, peer, *above_six)
+    clock.tick(even, peer)
     parts = (clock(even), peer)
     clock.tick(*send_rows(parts))
-    arrived = cross(*(clock(part) for part in clock.past))
-    even_above = join(clock(cotangent), above_two, above_four, *above_six)
-    odd_above = swap(even_above, 1)
-    clock.tick(*arrived, odd_above)
+    arrived = cross(*(clock(part) for part in clock.past[:2]))
+    clock.tick(*arrived, above_two, above_four)
     arrived = [clock(part) for part in arrived]
     last = cross(*pass_rows(parts, arrived))
-    clock.tick(*last)
+    clock.tick(*last, down_ring[2])
     last = [clock(part) for part in last]
-    middle, own_two, scale_two = on_rows(
+    middle, own_two, scale_two = on_spans(
         middle_kernel,
-        (tokens, gain_two, *parts, *arrived, *last),
+        own_spans(parts, arrived, last),
+        (tokens, gain_two),
         (((count, model), F32), ((count, model), BF16), ((count, 1), F32)),
         "middle",
     )
@@ -678,11 +710,13 @@
     two, four = gather_pair(clock(own_two))
     clock.tick(two, four)
     six = gather_last(clock(two), clock(four))
-    clock.tick(*six, down_ring[3])
+    clock.tick(*six)
     even_two = join(clock(own_two), two, four, *six)
     odd_two = swap(even_two, 1)
-    down_weight = place_rows(finish([clock(part) for part in down_ring]), plane)
-    clock.tick(even_two, mlp_weight)
+    clock.tick(even_two)
+    above_six = gather_last(clock(above_two), clock(above_four))
+    clock.tick(mlp_weight, down_ring[2])
+    down_ring.append(onward(clock(down_ring[2])))
     mlp_weight = join(clock(mlp_weight))
 
     def feed(normed):
@@ -692,19 +726,22 @@
 
     even_gate, even_up, even_hidden = feed(clock(even_two))
     clock.tick(even_hidden, odd_two)
+    even_above = join(clock(cotangent), above_two, above_four, *(clock(part) for part in above_six))
+    odd_above = swap(even_above, 1)
     odd_gate, odd_up, odd_hidden = feed(clock(odd_two))
-    clock.tick(odd_hidden)
-    out_odd = thin(dot(clock(odd_hidden), down_weight))
+    clock.tick(odd_hidden, down_ring[3])
+    down_weight = place_rows(finish([clock(part) for part in down_ring]), plane)
+    out_odd = thin(dot(odd_hidden, down_weight))
     out_peer = swap(out_odd, 1)
     out_even = thin(dot(after(even_hidden, out_odd), down_weight))
-    clock.tick(out_even, out_peer)
+    clock.tick(out_even, out_peer, odd_above)
     out_parts = (clock(out_even), out_peer)
     clock.tick(*send_rows(out_parts))
     out_arrived = cross(*(clock(part) for part in clock.past))
     down_sum = contract_rows(clock(even_hidden), even_above) + contract_rows(odd_hidden, odd_above)
     down_sum = thin(down_sum)
     clock.tick(down_sum)
-    down_grad = planes_reduce(clock(down_sum)).astype(F32)
+    down_total = planes_reduce(clock(down_sum))
 
     def feed_back(above, gate, up_proj):
         sigmoid_gate = jax.nn.sigmoid(gate)
@@ -715,32 +752,27 @@
     odd_low = feed_back(clock(odd_above), odd_gate, odd_up)
     odd_part = thin(times_transposed(odd_low, mlp_weight))
     peer = swap(odd_part, 1)
-    clock.tick(odd_part, *out_arrived)
-    out_arrived = [clock(part) for part in out_arrived]
-    out_last = cross(*pass_rows(out_parts, out_arrived))
+    clock.tick(odd_part)
     even_low = feed_back(clock(even_above), even_gate, even_up)
     parts = (thin(times_transposed(even_low, mlp_weight)), peer)
-    clock.tick(*send_rows(parts), *out_last)
+    clock.tick(*send_rows(parts), *out_arrived)
+    out_arrived = [clock(part) for part in out_arrived]
     arrived = cross(*clock.past[:2])
-    (output,) = on_rows(
-        output_kernel,
-        (middle, *out_parts, *out_arrived, *[clock(part) for part in out_last]),
-        (((count, model), BF16),),
-        "output",
-    )
     mlp_sum = contract_rows(clock(even_two), even_low)
-    mlp_sum = thin(mlp_sum + contract_rows(clock(odd_two), odd_low))
-    clock.tick(*arrived, mlp_sum, output, down_grad)
-    mlp_total = planes_reduce(clock(mlp_sum))
+    clock.tick(*arrived, mlp_sum)
     arrived = [clock(part) for part in arrived]
     last = cross(*pass_rows(parts, arrived))
-    clock.tick(*last)
+    mlp_sum = thin(mlp_sum + contract_rows(clock(odd_two), odd_low))
+    clock.tick(*last, mlp_sum, down_total)
+    mlp_total = planes_reduce(clock(mlp_sum))
     last = [clock(part) for part in last]
-    middle_grad, branch = on_rows(
+    middle_grad, branch = on_spans(
         middle_back_kernel,
-        (cotangent, gain_two, middle, scale_two, *parts, *arrived, *last),
+        own_spans(parts, arrived, last),
+        (cotangent, gain_two, middle, scale_two),
         (((count, model), F32), ((count, model), BF16)),
         "middle_back",
+        60,
     )
 
     clock.tick(branch)
@@ -770,49 +802,59 @@
     far_odd = swap(far_even, 1)
     near_branch = join(*near_blocks)
     clock.tick(far_odd, near_branch, near_other)
+    far_branch = join(clock(far_even), far_odd)
+    out_sum = contract_rows(clock(near_mixed), near_branch) + contract_rows(clock(far_mixed), far_branch)
+    out_sum = thin(out_sum)
+    clock.tick(out_sum, far_branch)
     far_query, far_own, far_other = attention_back(far_kept, clock(far_even), far_odd)
     near_all = jnp.concatenate([near_query, thin(near_own + near_other)], axis=1)
     clock.tick(far_query, far_other, near_all)
     far_all = jnp.concatenate([clock(far_query), thin(far_own + far_other)], axis=1)
-    far_branch = join(clock(far_even), far_odd)
     odd = parts_of(True, True, near_all, far_all, back_weight)
     peer = swap(odd, 1)
     even = parts_of(False, True, after(near_all, odd), far_all, back_weight)
-    out_sum = contract_rows(after(near_mixed, even), near_branch) + contract_rows(far_mixed, far_branch)
-    out_hop = onward(ring_start(out_sum, plane, planes))
-    attn_sum = contract_rows(after(near_one, out_sum), near_all) + contract_rows(after(far_one, out_sum), far_all)
+    out_last = cross(*pass_rows(out_parts, [after(part, even) for part in out_arrived], 60))
+    attn_sum = contract_rows(after(near_one, even), near_all) + contract_rows(after(far_one, even), far_all)
     clock.tick(even, peer, attn_sum)
     parts = (clock(even), peer)
-    clock.tick(*send_rows(parts), mlp_total)
+    clock.tick(*send_rows(parts), mlp_total, *out_last)
     arrived = cross(*clock.past[:2])
+    (output,) = on_spans(
+        output_kernel,
+        own_spans(out_parts, out_arrived, [clock(part) for part in out_last]),
+        (middle,),
+        (((count, model), BF16),),
+        "output",
+        60,
+    )
+    out_total = planes_reduce(clock(out_sum))
     mlp_back = exchange(clock(mlp_total).reshape(RANKS, local, 2 * own_units))
     attn_hop = onward(clock(ring_start(attn_sum, plane, planes)))
-    clock.tick(attn_hop, out_hop)
+    clock.tick(attn_hop)
     attn_hop = onward(ring_add(attn_sum, 1, clock(attn_hop), plane, planes))
-    out_hop = onward(ring_add(out_sum, 1, clock(out_hop), plane, planes))
-    clock.tick(*arrived)
+    clock.tick(*arrived, output)
     arrived = [clock(part) for part in arrived]
-    last = cross(*pass_rows(parts, arrived))
-    clock.tick(attn_hop, out_hop)
+    last = cross(*pass_rows(parts, arrived, 60))
+    clock.tick(attn_hop)
     attn_hop = onward(ring_add(attn_sum, 2, clock(attn_hop), plane, planes))
-    out_hop = onward(ring_add(out_sum, 2, clock(out_hop), plane, planes))
-    clock.tick(*last, mlp_back)
+    clock.tick(*last, mlp_back, out_total)
+    out_grad = lax.ppermute(clock(out_total), "dev", from_rank).astype(F32)
     mlp_back = clock(mlp_back)
     last = [clock(part) for part in last]
-    (input_grad,) = on_rows(
+    (input_grad,) = on_spans(
         input_back_kernel,
-        (middle_grad, gain_one, tokens, *parts, *arrived, *last),
+        own_spans(parts, arrived, last),
+        (middle_grad, gain_one, tokens),
         (((count, model), BF16),),
         "input_back",
-    )
-    clock.tick(attn_hop, out_hop, input_grad)
+        60,
+    )
+    clock.tick(attn_hop, input_grad)
+    down_grad = clock(down_total).astype(F32)
     for step in range(3, planes - 1):
         attn_hop = onward(ring_add(attn_sum, step, attn_hop, plane, planes))
-        out_hop = onward(ring_add(out_sum, step, out_hop, plane, planes))
-    out_total = ring_add(out_sum, planes - 1, clock(out_hop), plane, planes)
     attn_total = ring_add(attn_sum, planes - 1, clock(attn_hop), plane, planes)
     attn_back = exchange(thin(attn_total).reshape(RANKS, local, width + HD))
-    out_grad = lax.ppermute(out_total, "dev", from_rank)
 
     gate_grad, up_grad, mlp_gain_sum = on_rows(
         functools.partial(mlp_back_kernel, units),

time: 662 us -> 622 us (0.940)
  local copies, waits for them, and re-layouts: 65.5 us -> 44.4 us
  Pallas kernels: 134 us -> 118 us
  matrix products: 106 us -> 113 us
    pallas_call x22 -> x10, Pallas kernels: 64.3 us -> 20 us  [on_rows(): pl.pallas_call(function, out_shape=[jax.ShapeDtypeStruct(shape, dtype) fo...]
    pallas_call x0 -> x12, Pallas kernels: none -> 41.1 us  [on_spans(): pl.pallas_call(functools.partial(sliced_kernel, function, places, len(arr...]
    ppermute x48, waiting for transfers between devices: 114 us -> 135 us  [swap(): return lax.ppermute(block, 'dev', [(i, i ^ bit) for i in range(n)])]
    unnamed x237 -> x214, local copies, waits for them, and re-layouts: 58 us -> 38.5 us
    all_to_all x4, waiting for transfers between devices: 16.9 us -> 0.01 us  [exchange(): lax.all_to_all(blocks, 'dev', split_axis=0, concat_axis=0, tiled=True, ax...]
    ppermute x15 -> x12, waiting for transfers between devices: 75.9 us -> 59.4 us  [onward(): return lax.ppermute(block, 'dev', [(i, (i + RANKS) % n) for i in range(n)])]
    pallas_call x4, Pallas kernels: 53.9 us -> 42.1 us  [attention_call(): pl.pallas_call(kernel, grid_spec=pltpu.PrefetchScalarGridSpec(num_scalar_...]
    ppermute x1, waiting for transfers between devices: 2.81 us -> 13.9 us  [per_device(): out_grad = lax.ppermute(clock(out_total), 'dev', from_rank).astype(F32)]
  transfers between devices with their start and end apart: 75 -> 73, of which waited for: 27 -> 36; matrix products, arithmetic and copies ran while one was open for 18% -> 17% of each run, Pallas kernels for 19% -> 18%
where the time goes in v3:
time: 622 us; the launch traced here: 613 us
  waiting for transfers between devices  217 us (35%)
  Pallas kernels  118 us (19%)
  matrix products  113 us (18%)
  starting transfers between devices  87.2 us (14%)
  local copies, waits for them, and re-layouts  44.4 us (7%)
  other arithmetic  17.4 us (3%)
  between operations  15.5 us (2%)
    ppermute x48, waiting for transfers between devices, swap(): return lax.ppermute(block, 'dev', [(i, i ^ bit) for i in range(n)])  135 us
    ppermute x12, waiting for transfers between devices, onward(): return lax.ppermute(block, 'dev', [(i, (i + RANKS) % n) for i in range(n)])  59.4 us
    ppermute x48, starting transfers between devices, swap(): return lax.ppermute(block, 'dev', [(i, i ^ bit) for i in range(n)])  49.4 us
    dot_general x8, matrix products, contract_rows(): lax.dot_general(left, right, (((0,), (0,)), ((), ())), preferred_element_...  47.6 us
    pallas_call x4, Pallas kernels, attention_call(): pl.pallas_call(kernel, grid_spec=pltpu.PrefetchScalarGridSpec(num_scalar_...  42.1 us
    pallas_call x12, Pallas kernels, on_spans(): pl.pallas_call(functools.partial(sliced_kernel, function, places, len(arr...  41.1 us
    dot_general x4, matrix products, times_transposed(): lax.dot_general(left, right, (((1,), (1,)), ((), ())), preferred_element_...  39.2 us
    unnamed x214, local copies, waits for them, and re-layouts  38.5 us
  transfers between devices with their start and end apart: 73, of which 36 were waited for; matrix products, arithmetic and copies ran while one was open for 17% of the time, Pallas kernels for 18%

profile of v3, /device:TPU:1, one launch (start us, length us, event | category | flops | bytes accessed | tf_op | source)
XLA Modules:
  0.0 613.3 jit_solution(6705221265887086130)
XLA Ops:
  10.6 5.2 all-to-all-start
  16.5 3.4 collective-permute-start.2
  20.4 4.8 collective-permute-start.6
  40.5 8.6 %collective-permute-done.9.refs_1_ = bf16[512,384]{1,0:T(8,128)(2,1)S(1)} collective-permute-done((bf16[512,384]{1,0:T(8,128)(2,1)S(1)}, bf16[512,384]{1,0:T(8,128)(2,1)S(1)}, u32[]{:S(2)}, u32[]{:S(2)}) %collective-permute-start.9) | collective-permute-done | bytes 393248 | tf_op jit(solution)/shard_map/ppermute | solution.py:30
  51.4 12.4 %collective-permute-done.11.refs_1_ = bf16[64,2048]{1,0:T(8,128)(2,1)S(1)} collective-permute-done((bf16[64,2048]{1,0:T(8,128)(2,1)}, bf16[64,2048]{1,0:T(8,128)(2,1)S(1)}, u32[]{:S(2)}, u32[]{:S(2)}) %collective-permute-start.11) | collective-permute-done | bytes 262176 | tf_op jit(solution)/shard_map/ppermute | solution.py:30
  64.6 4.4 collective-permute-start.12
  72.6 17.3 %collective-permute-done.14.refs_2_ = bf16[64,2048]{1,0:T(8,128)(2,1)} collective-permute-done((bf16[64,2048]{1,0:T(8,128)(2,1)S(1)}, bf16[64,2048]{1,0:T(8,128)(2,1)}, u32[]{:S(2)}, u32[]{:S(2)}) %collective-permute-start.14) | collective-permute-done | bytes 262176 | tf_op jit(solution)/shard_map/ppermute | solution.py:30
  95.4 4.2 all-to-all-start.1
  106.3 8.7 %attend.2 = (bf16[1,4,256,256]{3,2,1,0:T(8,128)(2,1)S(1)}, bf16[1,4,64,1024]{3,2,1,0:T(8,128)(2,1)S(1)}, bf16[1,1024,128]{2,1,0:T(8,128)(2,1)S(1)}, f32[1,4,1,1024]{3,2,1,0:T(1,128)S(1)}) custom-call(s32[1]{0:T(128)} %bitcast.m_ref, bf16[512,2048]{1,0:T(8,128)(2,1)S(1)} %copy-done.9, bf16[512,2048]{1,0:T(8,128)(2,1)} %copy-done.24, ...), custom_call_target="tpu_custom_call" | custom-call | flops 1 | bytes 1 | tf_op jit(solution)/shard_map/attend/pallas_call | solution.py:547
  117.3 7.1 %collective-permute-done.18.refs_1_ = bf16[176,2048]{1,0:T(8,128)(2,1)} collective-permute-done((bf16[176,2048]{1,0:T(8,128)(2,1)}, bf16[176,2048]{1,0:T(8,128)(2,1)}, u32[]{:S(2)}, u32[]{:S(2)}) %collective-permute-start.18) | collective-permute-done | bytes 720928 | tf_op jit(solution)/shard_map/ppermute | solution.py:30
  124.5 9.0 %attend.3 = (bf16[1,4,256,256]{3,2,1,0:T(8,128)(2,1)S(1)}, bf16[1,4,64,1024]{3,2,1,0:T(8,128)(2,1)S(1)}, bf16[1,1024,128]{2,1,0:T(8,128)(2,1)S(1)}, f32[1,4,1,1024]{3,2,1,0:T(1,128)S(1)}) custom-call(s32[1]{0:T(128)} %bitcast.m_ref, bf16[512,2048]{1,0:T(8,128)(2,1)} %norm.3.refs_0_, bf16[512,2048]{1,0:T(8,128)(2,1)} %collective-permute-done.17.refs_1_, ...), custom_call_target="tpu_custom_call" | custom-call | flops 1 | bytes 1 | tf_op jit(solution)/shard_map/attend/pallas_call | solution.py:547
  152.0 13.2 %collective-permute-done.24.refs_2_ = bf16[256,2048]{1,0:T(8,128)(2,1)S(1)} collective-permute-done((bf16[256,2048]{1,0:T(8,128)(2,1)}, bf16[256,2048]{1,0:T(8,128)(2,1)S(1)}, u32[]{:S(2)}, u32[]{:S(2)}) %collective-permute-start.24) | collective-permute-done | bytes 1048608 | tf_op jit(solution)/shard_map/ppermute | solution.py:25
  166.3 22.5 %collective-permute-done.21.refs_2_ = bf16[256,2048]{1,0:T(8,128)(2,1)S(1)} collective-permute-done((bf16[256,2048]{1,0:T(8,128)(2,1)S(1)}, bf16[256,2048]{1,0:T(8,128)(2,1)S(1)}, u32[]{:S(2)}, u32[]{:S(2)}) %collective-permute-start.21) | collective-permute-done | bytes 1048608 | tf_op jit(solution)/shard_map/ppermute | solution.py:25
  192.0 11.0 %collective-permute-done.25.refs_4_ = bf16[128,2048]{1,0:T(8,128)(2,1)S(1)} collective-permute-done((bf16[128,2048]{1,0:T(8,128)(2,1)S(1)}, bf16[128,2048]{1,0:T(8,128)(2,1)S(1)}, u32[]{:S(2)}, u32[]{:S(2)}) %collective-permute-start.25) | collective-permute-done | bytes 524320 | tf_op jit(solution)/shard_map/ppermute | solution.py:25
  208.6 21.8 %collective-permute-done.29.refs_2_ = bf16[256,2048]{1,0:T(8,128)(2,1)S(1)} collective-permute-done((bf16[256,2048]{1,0:T(8,128)(2,1)S(1)}, bf16[256,2048]{1,0:T(8,128)(2,1)S(1)}, u32[]{:S(2)}, u32[]{:S(2)}) %collective-permute-start.29) | collective-permute-done | bytes 1048608 | tf_op jit(solution)/shard_map/ppermute | solution.py:25
  232.1 9.0 %collective-permute-done.31.refs_4_ = bf16[128,2048]{1,0:T(8,128)(2,1)S(1)} collective-permute-done((bf16[128,2048]{1,0:T(8,128)(2,1)S(1)}, bf16[128,2048]{1,0:T(8,128)(2,1)S(1)}, u32[]{:S(2)}, u32[]{:S(2)}) %collective-permute-start.31) | collective-permute-done | bytes 524320 | tf_op jit(solution)/shard_map/ppermute | solution.py:25
  244.1 4.1 collective-permute-start.32
  251.7 8.6 %all-gather.2.cloned.1.call-done.refs_0_ = bf16[2048,1408]{1,0:T(8,128)(2,1)} async-done(((bf16[512,1408]{1,0:T(8,128)(2,1)}), bf16[2048,1408]{1,0:T(8,128)(2,1)}) %all-gather.2.cloned.1.call-update) | async-done | bytes 5767184 | tf_op jit(solution)/shard_map/all_gather | solution.py:50
  263.5 10.0 %fusion.15 = f32[1024,1408]{1,0:T(8,128)S(1)} fusion(bf16[1024,2048]{1,0:T(8,128)(2,1)} %join.8, bf16[2048,1408]{1,0:T(8,128)(2,1)S(1)} %join.9), kind=kOutput, calls=%fused_computation.62 | convolution fusion | flops 5905580032 | bytes 15728640 | tf_op jit(solution)/shard_map/dot_general | solution.py:377
  279.7 9.4 %fusion.16 = f32[1024,1408]{1,0:T(8,128)S(1)} fusion(bf16[1024,2048]{1,0:T(8,128)(2,1)} %collective-permute-done.32, bf16[2048,1408]{1,0:T(8,128)(2,1)S(1)} %join.9), kind=kOutput, calls=%fused_computation.63 | convolution fusion | flops 5905580032 | bytes 15728640 | tf_op jit(solution)/shard_map/dot_general | solution.py:377
  294.9 3.6 convolution_convert_fusion.3
  299.2 3.6 convolution_convert_fusion.2.refs_0_
  308.0 5.4 fusion.17
  313.4 5.1 add_convert_fusion.1
  318.5 9.1 %multiply_convert_fusion.3 = (bf16[1024,704]{1,0:T(8,128)(2,1)S(1)}, bf16[1024,704]{1,0:T(8,128)(2,1)S(1)}) fusion(f32[1024,1408]{1,0:T(8,128)} %copy-done.91, bf16[1024,2048]{1,0:T(8,128)(2,1)} %collective-permute-done.37, bf16[704,2048]{1,0:T(8,128)(2,1)} %copy-done.38), kind=kOutput, calls=%fused_computation.9 | convolution fusion | flops 2962161664 | bytes 15728640 | tf_op jit(solution)/shard_map/dot_general | solution.py:385
  327.6 12.1 %convolution_convert_fusion.1 = bf16[1024,2048]{1,0:T(8,128)(2,1)} fusion(bf16[2048,1408]{1,0:T(8,128)(2,1)} %copy-done.29, bf16[1024,704]{1,0:T(8,128)(2,1)S(1)} %get-tuple-element.306, bf16[1024,704]{1,0:T(8,128)(2,1)S(1)} %get-tuple-element.305), kind=kOutput, calls=%fused_computation.3 | convolution fusion | flops 5913444352 | bytes 12845056 | tf_op jit(solution)/shard_map/dot_general | solution.py:385
  342.6 9.1 %multiply_convert_fusion.1 = (bf16[1024,704]{1,0:T(8,128)(2,1)S(1)}, bf16[1024,704]{1,0:T(8,128)(2,1)S(1)}) fusion(f32[1024,1408]{1,0:T(8,128)} %copy-done.90, bf16[1024,2048]{1,0:T(8,128)(2,1)} %copy-done.37, bf16[704,2048]{1,0:T(8,128)(2,1)} %copy-done.38), kind=kOutput, calls=%fused_computation.7 | convolution fusion | flops 2962161664 | bytes 15728640 | tf_op jit(solution)/shard_map/dot_general | solution.py:385
  351.7 8.9 %convolution_convert_fusion.refs_0_ = bf16[1024,2048]{1,0:T(8,128)(2,1)S(1)} fusion(bf16[2048,1408]{1,0:T(8,128)(2,1)} %copy-done.29, bf16[1024,704]{1,0:T(8,128)(2,1)S(1)} %get-tuple-element.304, bf16[1024,704]{1,0:T(8,128)(2,1)S(1)} %get-tuple-element.303), kind=kOutput, calls=%fused_computation.2 | convolution fusion | flops 5913444352 | bytes 12845056 | tf_op jit(solution)/shard_map/dot_general | solution.py:385
  360.6 3.6 send_rows.6
  366.0 12.0 %fusion.1 = f32[2048,1408]{1,0:T(8,128)} fusion(bf16[1024,2048]{1,0:T(8,128)(2,1)} %join.8, bf16[1024,704]{1,0:T(8,128)(2,1)S(1)} %get-tuple-element.304, bf16[1024,704]{1,0:T(8,128)(2,1)S(1)} %get-tuple-element.303), kind=kOutput, calls=%fused_computation.19 | convolution fusion | flops 5911347200 | bytes 18612224 | tf_op jit(solution)/shard_map/dot_general | solution.py:381
  378.1 10.0 %collective-permute-done.41.refs_2_ = bf16[256,2048]{1,0:T(8,128)(2,1)S(1)} collective-permute-done((bf16[256,2048]{1,0:T(8,128)(2,1)S(1)}, bf16[256,2048]{1,0:T(8,128)(2,1)S(1)}, u32[]{:S(2)}, u32[]{:S(2)}) %collective-permute-start.41) | collective-permute-done | bytes 1048608 | tf_op jit(solution)/shard_map/ppermute | solution.py:25
  392.2 14.0 %add_convert_fusion = bf16[2048,1408]{1,0:T(8,128)(2,1)} fusion(f32[2048,1408]{1,0:T(8,128)} %fusion.1, bf16[1024,2048]{1,0:T(8,128)(2,1)} %collective-permute-done.32, bf16[1024,704]{1,0:T(8,128)(2,1)S(1)} %copy-done.106, bf16[1024,704]{1,0:T(8,128)(2,1)S(1)} %copy-done.104), kind=kOutput, calls=%fused_computation | convolution fusion | flops 5917114368 | bytes 24379392 | tf_op jit(solution)/shard_map/dot_general | solution.py:381
  406.5 7.0 %middle_back.1 = (f32[256,2048]{1,0:T(8,128)}, bf16[256,2048]{1,0:T(8,128)(2,1)}) custom-call(bf16[1024,2048]{1,0:T(8,128)(2,1)} %copy-done.4, bf16[1024,2048]{1,0:T(8,128)(2,1)} %collective-permute-done.39.refs_1_, bf16[256,2048]{1,0:T(8,128)(2,1)} %copy-done.32, bf16[256,2048]{1,0:T(8,128)(2,1)} %copy-done.33, ...), custom_call_target="tpu_custom_call" | custom-call | flops 1 | bytes 1 | tf_op jit(solution)/shard_map/middle_back/pallas_call | solution.py:143
  423.9 12.2 %collective-permute-done.47.refs_0_ = bf16[256,2048]{1,0:T(8,128)(2,1)} collective-permute-done((bf16[256,2048]{1,0:T(8,128)(2,1)}, bf16[256,2048]{1,0:T(8,128)(2,1)}, u32[]{:S(2)}, u32[]{:S(2)}) %collective-permute-start.47) | collective-permute-done | bytes 1048608 | tf_op jit(solution)/shard_map/ppermute | solution.py:25
  436.1 6.1 %collective-permute-done.45.refs_1_ = bf16[256,2048]{1,0:T(8,128)(2,1)S(1)} collective-permute-done((bf16[256,2048]{1,0:T(8,128)(2,1)}, bf16[256,2048]{1,0:T(8,128)(2,1)S(1)}, u32[]{:S(2)}, u32[]{:S(2)}) %collective-permute-start.45) | collective-permute-done | bytes 1048608 | tf_op jit(solution)/shard_map/ppermute | solution.py:25
  446.2 12.5 %attend_back.2 = (bf16[1,4,256,256]{3,2,1,0:T(8,128)(2,1)S(1)}, f32[1,4,256,64]{3,2,1,0:T(8,128)S(1)}, f32[1,4,256,64]{3,2,1,0:T(8,128)S(1)}) custom-call(s32[1]{0:T(128)} %bitcast.m_ref, bf16[256,2048]{1,0:T(8,128)(2,1)S(1)} %copy-done.31, bf16[256,2048]{1,0:T(8,128)(2,1)S(1)} %collective-permute-done.45.refs_1_, ...), custom_call_target="tpu_custom_call" | custom-call | flops 1 | bytes 1 | tf_op jit(solution)/shard_map/attend_back/pallas_call | solution.py:547
  473.4 11.9 %attend_back.3 = (bf16[1,4,256,256]{3,2,1,0:T(8,128)(2,1)S(1)}, f32[1,4,256,64]{3,2,1,0:T(8,128)S(1)}, f32[1,4,256,64]{3,2,1,0:T(8,128)S(1)}) custom-call(s32[1]{0:T(128)} %bitcast.m_ref, bf16[512,2048]{1,0:T(8,128)(2,1)} %copy-done.7, bf16[512,2048]{1,0:T(8,128)(2,1)} %copy-done.23, bf16[1,4,64,1024]{3,2,1,0:T(8,128)(2,1)S(1)} %copy-done.65, ...), custom_call_target="tpu_custom_call" | custom-call | flops 1 | bytes 1 | tf_op jit(solution)/shard_map/attend_back/pallas_call | solution.py:547
  487.4 4.5 odd_parts.3
  501.9 4.3 fusion.13
  518.7 5.6 all-to-all-start.2
  524.3 6.3 %collective-permute-done.61 = bf16[512,320]{0,1:T(8,128)(2,1)} collective-permute-done((bf16[512,320]{0,1:T(8,128)(2,1)}, bf16[512,320]{0,1:T(8,128)(2,1)}, u32[]{:S(2)}, u32[]{:S(2)}) %collective-permute-start.61) | collective-permute-done | bytes 327712 | tf_op jit(solution)/shard_map/ppermute | solution.py:30
  532.6 5.3 output.1
  543.1 7.6 %collective-permute-done.62 = bf16[512,320]{0,1:T(8,128)(2,1)} collective-permute-done((bf16[512,320]{0,1:T(8,128)(2,1)}, bf16[512,320]{0,1:T(8,128)(2,1)}, u32[]{:S(2)}, u32[]{:S(2)}) %collective-permute-start.62) | collective-permute-done | bytes 327712 | tf_op jit(solution)/shard_map/ppermute | solution.py:30
  552.8 12.2 %collective-permute-done.59.refs_4_ = bf16[128,2048]{1,0:T(8,128)(2,1)S(1)} collective-permute-done((bf16[128,2048]{1,0:T(8,128)(2,1)}, bf16[128,2048]{1,0:T(8,128)(2,1)S(1)}, u32[]{:S(2)}, u32[]{:S(2)}) %collective-permute-start.59) | collective-permute-done | bytes 524320 | tf_op jit(solution)/shard_map/ppermute | solution.py:25
  566.0 6.8 %input_back.1 = bf16[256,2048]{1,0:T(8,128)(2,1)} custom-call(bf16[1024,2048]{1,0:T(8,128)(2,1)} %copy-done, bf16[1024,2048]{1,0:T(8,128)(2,1)} %collective-permute-done.55.refs_1_, bf16[256,2048]{1,0:T(8,128)(2,1)} %collective-permute-done.57.refs_2_, bf16[256,2048]{1,0:T(8,128)(2,1)} %collective-permute-done.58.refs_3_, bf16[128,2048]{1,0:T(8,128)(2,1)} %copy-done.97, ...), custom_call_target="tpu_custom_call" | custom-call | flops 1 | bytes 1 | tf_op jit(solution)/shard_map/input_back/pallas_call | solution.py:143
  575.1 5.6 all-to-all-start.3
  580.7 3.7 collective-permute-start.64
  588.5 13.9 %collective-permute-done.64 = bf16[64,2048]{1,0:T(8,128)(2,1)} collective-permute-done((bf16[64,2048]{1,0:T(8,128)(2,1)}, bf16[64,2048]{1,0:T(8,128)(2,1)}, u32[]{:S(2)}, u32[]{:S(2)}) %collective-permute-start.64) | collective-permute-done | bytes 262176 | tf_op jit(solution)/shard_map/ppermute | solution.py:841
  (413 shorter events, 181.0 us)
Async XLA Ops:
  10.6 25.4 %all-to-all-start = ((bf16[8,64,384]{2,1,0:T(8,128)(2,1)}), bf16[8,64,384]{2,1,0:T(8,128)(2,1)S(1)}, u32[]{:S(2)}, u32[]{:S(2)}) async-start(bf16[8,64,384]{2,1,0:T(8,128)(2,1)} %attn_parts.1), calls=%async_computation | async-start | bytes 786432 | tf_op jit(solution)/shard_map/all_to_all | solution.py:39
  20.4 15.7 %collective-permute-start.6 = (bf16[64,2048]{1,0:T(8,128)(2,1)}, bf16[64,2048]{1,0:T(8,128)(2,1)}, u32[]{:S(2)}, u32[]{:S(2)}) collective-permute-start(bf16[64,2048]{1,0:T(8,128)(2,1)} %param.16), channel_id=1, source_target_pairs={{0,0},{1,8},{2,16},{3,24},{4,1},{5,9},{6,17},{7,25},{8,2},{9,10},{... | collective-permute-start | bytes 786440 | tf_op jit(solution)/shard_map/ppermute | solution.py:648
  36.1 27.7 %collective-permute-start.8 = (bf16[256,2048]{1,0:T(8,128)(2,1)S(1)}, bf16[256,2048]{1,0:T(8,128)(2,1)S(1)}, u32[]{:S(2)}, u32[]{:S(2)}) collective-permute-start(bf16[256,2048]{1,0:T(8,128)(2,1)S(1)} %copy-done.20), channel_id=1, source_target_pairs={{0,4},{1,5},{2,6},{3,7},{4,0},{5,1},{6,2},{7,3},{8,12},{9,13},{10,... | collective-permute-start | bytes 3145736 | tf_op jit(solution)/shard_map/ppermute | solution.py:25
  39.2 24.6 %collective-permute-start.7 = (bf16[256,2048]{1,0:T(8,128)(2,1)S(1)}, bf16[256,2048]{1,0:T(8,128)(2,1)S(1)}, u32[]{:S(2)}, u32[]{:S(2)}) collective-permute-start(bf16[256,2048]{1,0:T(8,128)(2,1)S(1)} %copy-done.20), channel_id=1, source_target_pairs={{0,2},{1,3},{2,0},{3,1},{4,6},{5,7},{6,4},{7,5},{8,10},{9,11},{10,... | collective-permute-start | bytes 3145736 | tf_op jit(solution)/shard_map/ppermute | solution.py:25
  64.6 26.1 %collective-permute-start.12 = (bf16[512,2048]{1,0:T(8,128)(2,1)S(1)}, bf16[512,2048]{1,0:T(8,128)(2,1)S(1)}, u32[]{:S(2)}, u32[]{:S(2)}) collective-permute-start(bf16[512,2048]{1,0:T(8,128)(2,1)S(1)} %norm.2.refs_0_), channel_id=1, source_target_pairs={{0,1},{1,0},{2,3},{3,2},{4,5},{5,4},{6,7},{7,6},{8,9},{9,8},{10,11... | collective-permute-start | bytes 6291464 | tf_op jit(solution)/shard_map/ppermute | solution.py:25
  70.4 20.2 %collective-permute-start.16 = (bf16[128,2048]{1,0:T(8,128)(2,1)S(1)}, bf16[128,2048]{1,0:T(8,128)(2,1)S(1)}, u32[]{:S(2)}, u32[]{:S(2)}) collective-permute-start(bf16[128,2048]{1,0:T(8,128)(2,1)S(1)} %slice.48), channel_id=1, source_target_pairs={{0,2},{1,3},{2,0},{3,1},{4,6},{5,7},{6,4},{7,5},{8,10},{9,11},{10,... | collective-permute-start | bytes 1572872 | tf_op jit(solution)/shard_map/ppermute | solution.py:25
  71.7 19.0 %collective-permute-start.15 = (bf16[128,2048]{1,0:T(8,128)(2,1)S(1)}, bf16[128,2048]{1,0:T(8,128)(2,1)S(1)}, u32[]{:S(2)}, u32[]{:S(2)}) collective-permute-start(bf16[128,2048]{1,0:T(8,128)(2,1)S(1)} %slice.47), channel_id=1, source_target_pairs={{0,4},{1,5},{2,6},{3,7},{4,0},{5,1},{6,2},{7,3},{8,12},{9,13},{10,... | collective-permute-start | bytes 1572872 | tf_op jit(solution)/shard_map/ppermute | solution.py:25
  72.1 17.8 %collective-permute-start.13 = (bf16[512,384]{1,0:T(8,128)(2,1)S(1)}, bf16[512,384]{1,0:T(8,128)(2,1)S(1)}, u32[]{:S(2)}, u32[]{:S(2)}) collective-permute-start(bf16[512,384]{1,0:T(8,128)(2,1)S(1)} %collective-permute-done.10.refs_2_), channel_id=1, source_target_pairs={{0,8},{1,9},{2,10},{3,11},{4,12},{5,13},{6,14},{7,15},{8,16},{9,17... | collective-permute-start | bytes 1179656 | tf_op jit(solution)/shard_map/ppermute | solution.py:30
  72.2 17.8 %collective-permute-start.14 = (bf16[64,2048]{1,0:T(8,128)(2,1)S(1)}, bf16[64,2048]{1,0:T(8,128)(2,1)}, u32[]{:S(2)}, u32[]{:S(2)}) collective-permute-start(bf16[64,2048]{1,0:T(8,128)(2,1)S(1)} %collective-permute-done.11.refs_1_), channel_id=1, source_target_pairs={{0,8},{1,9},{2,10},{3,11},{4,12},{5,13},{6,14},{7,15},{8,16},{9,17... | collective-permute-start | bytes 786440 | tf_op jit(solution)/shard_map/ppermute | solution.py:30
  94.2 30.2 %collective-permute-start.17 = (bf16[512,2048]{1,0:T(8,128)(2,1)}, bf16[512,2048]{1,0:T(8,128)(2,1)}, u32[]{:S(2)}, u32[]{:S(2)}) collective-permute-start(bf16[512,2048]{1,0:T(8,128)(2,1)} %norm.3.refs_0_), channel_id=1, source_target_pairs={{0,1},{1,0},{2,3},{3,2},{4,5},{5,4},{6,7},{7,6},{8,9},{9,8},{10,11... | collective-permute-start | bytes 6291464 | tf_op jit(solution)/shard_map/ppermute | solution.py:25
  95.4 29.0 %all-to-all-start.1 = ((bf16[8,64,1408]{2,1,0:T(8,128)(2,1)}), bf16[8,64,1408]{2,1,0:T(8,128)(2,1)}, u32[]{:S(2)}, u32[]{:S(2)}) async-start(bf16[8,64,1408]{2,1,0:T(8,128)(2,1)} %mlp_parts.1), calls=%async_computation.1 | async-start | bytes 2883584 | tf_op jit(solution)/shard_map/all_to_all | solution.py:39
  99.7 160.6 %all-gather.2.cloned.1.call-start = ((), (), s32[]{:S(2)}) async-start(), calls=%async_computation.7 | async-start | bytes 7208960 | tf_op jit(solution)/shard_map/all_gather | solution.py:50
  104.5 19.9 %collective-permute-start.18 = (bf16[176,2048]{1,0:T(8,128)(2,1)}, bf16[176,2048]{1,0:T(8,128)(2,1)}, u32[]{:S(2)}, u32[]{:S(2)}) collective-permute-start(bf16[176,2048]{1,0:T(8,128)(2,1)} %refs_0_.1), channel_id=1, source_target_pairs={{0,8},{1,9},{2,10},{3,11},{4,12},{5,13},{6,14},{7,15},{8,16},{9,17... | collective-permute-start | bytes 2162696 | tf_op jit(solution)/shard_map/ppermute | solution.py:30
  104.6 28.9 %collective-permute-start.19 = (bf16[64,2048]{1,0:T(8,128)(2,1)}, bf16[64,2048]{1,0:T(8,128)(2,1)}, u32[]{:S(2)}, u32[]{:S(2)}) collective-permute-start(bf16[64,2048]{1,0:T(8,128)(2,1)} %collective-permute-done.14.refs_2_), channel_id=1, source_target_pairs={{0,8},{1,9},{2,10},{3,11},{4,12},{5,13},{6,14},{7,15},{8,16},{9,17... | collective-permute-start | bytes 786440 | tf_op jit(solution)/shard_map/ppermute | solution.py:30
  139.8 266.5 %reduce-scatter.4.cloned.1.call-start = ((), (), s32[]{:S(2)}) async-start(), calls=%async_computation.8 | async-start | bytes 3604480 | tf_op jit(solution)/shard_map/reduce_scatter | solution.py:54
  139.8 25.4 %collective-permute-start.24 = (bf16[256,2048]{1,0:T(8,128)(2,1)}, bf16[256,2048]{1,0:T(8,128)(2,1)S(1)}, u32[]{:S(2)}, u32[]{:S(2)}) collective-permute-start(bf16[256,2048]{1,0:T(8,128)(2,1)} %refs_6_.3), channel_id=1, source_target_pairs={{0,4},{1,5},{2,6},{3,7},{4,0},{5,1},{6,2},{7,3},{8,12},{9,13},{10,... | collective-permute-start | bytes 3145736 | tf_op jit(solution)/shard_map/ppermute | solution.py:25
  141.5 24.8 %collective-permute-start.23 = (bf16[256,2048]{1,0:T(8,128)(2,1)}, bf16[256,2048]{1,0:T(8,128)(2,1)S(1)}, u32[]{:S(2)}, u32[]{:S(2)}) collective-permute-start(bf16[256,2048]{1,0:T(8,128)(2,1)} %refs_6_.3), channel_id=1, source_target_pairs={{0,2},{1,3},{2,0},{3,1},{4,6},{5,7},{6,4},{7,5},{8,10},{9,11},{10,... | collective-permute-start | bytes 3145736 | tf_op jit(solution)/shard_map/ppermute | solution.py:25
  149.1 39.6 %collective-permute-start.21 = (bf16[256,2048]{1,0:T(8,128)(2,1)S(1)}, bf16[256,2048]{1,0:T(8,128)(2,1)S(1)}, u32[]{:S(2)}, u32[]{:S(2)}) collective-permute-start(bf16[256,2048]{1,0:T(8,128)(2,1)S(1)} %get-tuple-element.190), channel_id=1, source_target_pairs={{0,2},{1,3},{2,0},{3,1},{4,6},{5,7},{6,4},{7,5},{8,10},{9,11},{10,... | collective-permute-start | bytes 3145736 | tf_op jit(solution)/shard_map/ppermute | solution.py:25
  150.8 38.0 %collective-permute-start.22 = (bf16[256,2048]{1,0:T(8,128)(2,1)S(1)}, bf16[256,2048]{1,0:T(8,128)(2,1)S(1)}, u32[]{:S(2)}, u32[]{:S(2)}) collective-permute-start(bf16[256,2048]{1,0:T(8,128)(2,1)S(1)} %get-tuple-element.191), channel_id=1, source_target_pairs={{0,4},{1,5},{2,6},{3,7},{4,0},{5,1},{6,2},{7,3},{8,12},{9,13},{10,... | collective-permute-start | bytes 3145736 | tf_op jit(solution)/shard_map/ppermute | solution.py:25
  152.0 40.0 %collective-permute-start.27 = (bf16[176,2048]{1,0:T(8,128)(2,1)}, bf16[176,2048]{1,0:T(8,128)(2,1)S(1)}, u32[]{:S(2)}, u32[]{:S(2)}) collective-permute-start(bf16[176,2048]{1,0:T(8,128)(2,1)} %collective-permute-done.18.refs_1_), channel_id=1, source_target_pairs={{0,8},{1,9},{2,10},{3,11},{4,12},{5,13},{6,14},{7,15},{8,16},{9,17... | collective-permute-start | bytes 2162696 | tf_op jit(solution)/shard_map/ppermute | solution.py:30
  207.8 22.7 %collective-permute-start.29 = (bf16[256,2048]{1,0:T(8,128)(2,1)S(1)}, bf16[256,2048]{1,0:T(8,128)(2,1)S(1)}, u32[]{:S(2)}, u32[]{:S(2)}) collective-permute-start(bf16[256,2048]{1,0:T(8,128)(2,1)S(1)} %get-tuple-element.204.refs_0_), channel_id=1, source_target_pairs={{0,4},{1,5},{2,6},{3,7},{4,0},{5,1},{6,2},{7,3},{8,12},{9,13},{10,... | collective-permute-start | bytes 3145736 | tf_op jit(solution)/shard_map/ppermute | solution.py:25
  208.1 22.4 %collective-permute-start.28 = (bf16[256,2048]{1,0:T(8,128)(2,1)S(1)}, bf16[256,2048]{1,0:T(8,128)(2,1)S(1)}, u32[]{:S(2)}, u32[]{:S(2)}) collective-permute-start(bf16[256,2048]{1,0:T(8,128)(2,1)S(1)} %get-tuple-element.204.refs_0_), channel_id=1, source_target_pairs={{0,2},{1,3},{2,0},{3,1},{4,6},{5,7},{6,4},{7,5},{8,10},{9,11},{10,... | collective-permute-start | bytes 3145736 | tf_op jit(solution)/shard_map/ppermute | solution.py:25
  244.1 33.0 %collective-permute-start.32 = (bf16[1024,2048]{1,0:T(8,128)(2,1)}, bf16[1024,2048]{1,0:T(8,128)(2,1)}, u32[]{:S(2)}, u32[]{:S(2)}) collective-permute-start(bf16[1024,2048]{1,0:T(8,128)(2,1)} %join.8), channel_id=1, source_target_pairs={{0,1},{1,0},{2,3},{3,2},{4,5},{5,4},{6,7},{7,6},{8,9},{9,8},{10,11... | collective-permute-start | bytes 12582920 | tf_op jit(solution)/shard_map/ppermute | solution.py:25
  249.8 27.2 %collective-permute-start.36 = (bf16[128,2048]{1,0:T(8,128)(2,1)}, bf16[128,2048]{1,0:T(8,128)(2,1)}, u32[]{:S(2)}, u32[]{:S(2)}) collective-permute-start(bf16[128,2048]{1,0:T(8,128)(2,1)} %slice.56), channel_id=1, source_target_pairs={{0,2},{1,3},{2,0},{3,1},{4,6},{5,7},{6,4},{7,5},{8,10},{9,11},{10,... | collective-permute-start | bytes 1572872 | tf_op jit(solution)/shard_map/ppermute | solution.py:25
  250.6 26.4 %collective-permute-start.35 = (bf16[128,2048]{1,0:T(8,128)(2,1)}, bf16[128,2048]{1,0:T(8,128)(2,1)}, u32[]{:S(2)}, u32[]{:S(2)}) collective-permute-start(bf16[128,2048]{1,0:T(8,128)(2,1)} %slice.55), channel_id=1, source_target_pairs={{0,4},{1,5},{2,6},{3,7},{4,0},{5,1},{6,2},{7,3},{8,12},{9,13},{10,... | collective-permute-start | bytes 1572872 | tf_op jit(solution)/shard_map/ppermute | solution.py:25
  260.3 31.2 %collective-permute-start.33 = (bf16[176,2048]{1,0:T(8,128)(2,1)}, bf16[176,2048]{1,0:T(8,128)(2,1)S(1)}, u32[]{:S(2)}, u32[]{:S(2)}) collective-permute-start(bf16[176,2048]{1,0:T(8,128)(2,1)} %copy-done.60), channel_id=1, source_target_pairs={{0,8},{1,9},{2,10},{3,11},{4,12},{5,13},{6,14},{7,15},{8,16},{9,17... | collective-permute-start | bytes 2162696 | tf_op jit(solution)/shard_map/ppermute | solution.py:30
  279.2 23.6 %collective-permute-start.37 = (bf16[1024,2048]{1,0:T(8,128)(2,1)S(1)}, bf16[1024,2048]{1,0:T(8,128)(2,1)}, u32[]{:S(2)}, u32[]{:S(2)}) collective-permute-start(bf16[1024,2048]{1,0:T(8,128)(2,1)S(1)} %join.10), channel_id=1, source_target_pairs={{0,1},{1,0},{2,3},{3,2},{4,5},{5,4},{6,7},{7,6},{8,9},{9,8},{10,11... | collective-permute-start | bytes 12582920 | tf_op jit(solution)/shard_map/ppermute | solution.py:25
  339.7 20.9 %collective-permute-start.39 = (bf16[1024,2048]{1,0:T(8,128)(2,1)}, bf16[1024,2048]{1,0:T(8,128)(2,1)}, u32[]{:S(2)}, u32[]{:S(2)}) collective-permute-start(bf16[1024,2048]{1,0:T(8,128)(2,1)} %convolution_convert_fusion.1), channel_id=1, source_target_pairs={{0,1},{1,0},{2,3},{3,2},{4,5},{5,4},{6,7},{7,6},{8,9},{9,8},{10,11... | collective-permute-start | bytes 12582920 | tf_op jit(solution)/shard_map/ppermute | solution.py:25
  340.1 174.4 %reduce-scatter.6.cloned.1.call-start = ((), (), s32[]{:S(2)}) async-start(), calls=%async_computation.9 | async-start | bytes 7208960 | tf_op jit(solution)/shard_map/reduce_scatter | solution.py:54
  340.2 25.0 %collective-permute-start.38 = (bf16[256,2048]{1,0:T(8,128)(2,1)}, bf16[256,2048]{1,0:T(8,128)(2,1)S(1)}, u32[]{:S(2)}, u32[]{:S(2)}) collective-permute-start(bf16[256,2048]{1,0:T(8,128)(2,1)} %copy-done.89), channel_id=1, source_target_pairs={{0,2},{1,3},{2,0},{3,1},{4,6},{5,7},{6,4},{7,5},{8,10},{9,11},{10,... | collective-permute-start | bytes 3145736 | tf_op jit(solution)/shard_map/ppermute | solution.py:25
  341.5 24.5 %collective-permute-start.40 = (bf16[256,2048]{1,0:T(8,128)(2,1)S(1)}, bf16[256,2048]{1,0:T(8,128)(2,1)S(1)}, u32[]{:S(2)}, u32[]{:S(2)}) collective-permute-start(bf16[256,2048]{1,0:T(8,128)(2,1)S(1)} %get-tuple-element.229), channel_id=1, source_target_pairs={{0,4},{1,5},{2,6},{3,7},{4,0},{5,1},{6,2},{7,3},{8,12},{9,13},{10,... | collective-permute-start | bytes 3145736 | tf_op jit(solution)/shard_map/ppermute | solution.py:25
  364.2 23.8 %collective-permute-start.41 = (bf16[256,2048]{1,0:T(8,128)(2,1)S(1)}, bf16[256,2048]{1,0:T(8,128)(2,1)S(1)}, u32[]{:S(2)}, u32[]{:S(2)}) collective-permute-start(bf16[256,2048]{1,0:T(8,128)(2,1)S(1)} %get-tuple-element.227), channel_id=1, source_target_pairs={{0,2},{1,3},{2,0},{3,1},{4,6},{5,7},{6,4},{7,5},{8,10},{9,11},{10,... | collective-permute-start | bytes 3145736 | tf_op jit(solution)/shard_map/ppermute | solution.py:25
  364.7 23.9 %collective-permute-start.42 = (bf16[256,2048]{1,0:T(8,128)(2,1)S(1)}, bf16[256,2048]{1,0:T(8,128)(2,1)S(1)}, u32[]{:S(2)}, u32[]{:S(2)}) collective-permute-start(bf16[256,2048]{1,0:T(8,128)(2,1)S(1)} %get-tuple-element.228), channel_id=1, source_target_pairs={{0,4},{1,5},{2,6},{3,7},{4,0},{5,1},{6,2},{7,3},{8,12},{9,13},{10,... | collective-permute-start | bytes 3145736 | tf_op jit(solution)/shard_map/ppermute | solution.py:25
  390.6 15.6 %collective-permute-start.43 = (bf16[128,2048]{1,0:T(8,128)(2,1)S(1)}, bf16[128,2048]{1,0:T(8,128)(2,1)}, u32[]{:S(2)}, u32[]{:S(2)}) collective-permute-start(bf16[128,2048]{1,0:T(8,128)(2,1)S(1)} %get-tuple-element.235), channel_id=1, source_target_pairs={{0,2},{1,3},{2,0},{3,1},{4,6},{5,7},{6,4},{7,5},{8,10},{9,11},{10,... | collective-permute-start | bytes 1572872 | tf_op jit(solution)/shard_map/ppermute | solution.py:25
  406.2 158.8 %reduce-scatter.8.cloned.1.call-start = ((), (), s32[]{:S(2)}) async-start(), calls=%async_computation.10 | async-start | bytes 1310720 | tf_op jit(solution)/shard_map/reduce_scatter | solution.py:54
  413.6 22.5 %collective-permute-start.47 = (bf16[256,2048]{1,0:T(8,128)(2,1)}, bf16[256,2048]{1,0:T(8,128)(2,1)}, u32[]{:S(2)}, u32[]{:S(2)}) collective-permute-start(bf16[256,2048]{1,0:T(8,128)(2,1)} %get-tuple-element.249.refs_0_), channel_id=1, source_target_pairs={{0,4},{1,5},{2,6},{3,7},{4,0},{5,1},{6,2},{7,3},{8,12},{9,13},{10,... | collective-permute-start | bytes 3145736 | tf_op jit(solution)/shard_map/ppermute | solution.py:25
  414.3 21.8 %collective-permute-start.46 = (bf16[256,2048]{1,0:T(8,128)(2,1)}, bf16[256,2048]{1,0:T(8,128)(2,1)}, u32[]{:S(2)}, u32[]{:S(2)}) collective-permute-start(bf16[256,2048]{1,0:T(8,128)(2,1)} %get-tuple-element.249.refs_0_), channel_id=1, source_target_pairs={{0,1},{1,0},{2,3},{3,2},{4,5},{5,4},{6,7},{7,6},{8,9},{9,8},{10,11... | collective-permute-start | bytes 3145736 | tf_op jit(solution)/shard_map/ppermute | solution.py:25
  417.1 25.1 %collective-permute-start.45 = (bf16[256,2048]{1,0:T(8,128)(2,1)}, bf16[256,2048]{1,0:T(8,128)(2,1)S(1)}, u32[]{:S(2)}, u32[]{:S(2)}) collective-permute-start(bf16[256,2048]{1,0:T(8,128)(2,1)} %get-tuple-element.249.refs_0_), channel_id=1, source_target_pairs={{0,2},{1,3},{2,0},{3,1},{4,6},{5,7},{6,4},{7,5},{8,10},{9,11},{10,... | collective-permute-start | bytes 3145736 | tf_op jit(solution)/shard_map/ppermute | solution.py:25
  491.9 17.4 %collective-permute-start.55 = (bf16[1024,2048]{1,0:T(8,128)(2,1)}, bf16[1024,2048]{1,0:T(8,128)(2,1)}, u32[]{:S(2)}, u32[]{:S(2)}) collective-permute-start(bf16[1024,2048]{1,0:T(8,128)(2,1)} %odd_parts.3), channel_id=1, source_target_pairs={{0,1},{1,0},{2,3},{3,2},{4,5},{5,4},{6,7},{7,6},{8,9},{9,8},{10,11... | collective-permute-start | bytes 12582920 | tf_op jit(solution)/shard_map/ppermute | solution.py:25
  514.6 23.8 %collective-permute-start.57 = (bf16[256,2048]{1,0:T(8,128)(2,1)}, bf16[256,2048]{1,0:T(8,128)(2,1)}, u32[]{:S(2)}, u32[]{:S(2)}) collective-permute-start(bf16[256,2048]{1,0:T(8,128)(2,1)} %get-tuple-element.276), channel_id=1, source_target_pairs={{0,2},{1,3},{2,0},{3,1},{4,6},{5,7},{6,4},{7,5},{8,10},{9,11},{10,... | collective-permute-start | bytes 3145736 | tf_op jit(solution)/shard_map/ppermute | solution.py:25
  515.0 23.4 %collective-permute-start.58 = (bf16[256,2048]{1,0:T(8,128)(2,1)S(1)}, bf16[256,2048]{1,0:T(8,128)(2,1)}, u32[]{:S(2)}, u32[]{:S(2)}) collective-permute-start(bf16[256,2048]{1,0:T(8,128)(2,1)S(1)} %get-tuple-element.277), channel_id=1, source_target_pairs={{0,4},{1,5},{2,6},{3,7},{4,0},{5,1},{6,2},{7,3},{8,12},{9,13},{10,... | collective-permute-start | bytes 3145736 | tf_op jit(solution)/shard_map/ppermute | solution.py:25
  518.7 46.4 %all-to-all-start.2 = ((bf16[8,64,1408]{2,1,0:T(8,128)(2,1)}), bf16[8,64,1408]{2,1,0:T(8,128)(2,1)S(1)}, u32[]{:S(2)}, u32[]{:S(2)}) async-start(bf16[8,64,1408]{2,1,0:T(8,128)(2,1)} %bitcast.75), calls=%async_computation.4 | async-start | bytes 2883584 | tf_op jit(solution)/shard_map/all_to_all | solution.py:39
  532.6 18.2 %collective-permute-start.62 = (bf16[512,320]{0,1:T(8,128)(2,1)}, bf16[512,320]{0,1:T(8,128)(2,1)}, u32[]{:S(2)}, u32[]{:S(2)}) collective-permute-start(bf16[512,320]{0,1:T(8,128)(2,1)} %add_convert_fusion.4), channel_id=1, source_target_pairs={{0,8},{1,9},{2,10},{3,11},{4,12},{5,13},{6,14},{7,15},{8,16},{9,17... | collective-permute-start | bytes 983048 | tf_op jit(solution)/shard_map/ppermute | solution.py:30
  541.5 23.5 %collective-permute-start.59 = (bf16[128,2048]{1,0:T(8,128)(2,1)}, bf16[128,2048]{1,0:T(8,128)(2,1)S(1)}, u32[]{:S(2)}, u32[]{:S(2)}) collective-permute-start(bf16[128,2048]{1,0:T(8,128)(2,1)} %get-tuple-element.284), channel_id=1, source_target_pairs={{0,2},{1,3},{2,0},{3,1},{4,6},{5,7},{6,4},{7,5},{8,10},{9,11},{10,... | collective-permute-start | bytes 1572872 | tf_op jit(solution)/shard_map/ppermute | solution.py:25
  542.6 22.5 %collective-permute-start.60 = (bf16[128,2048]{1,0:T(8,128)(2,1)}, bf16[128,2048]{1,0:T(8,128)(2,1)S(1)}, u32[]{:S(2)}, u32[]{:S(2)}) collective-permute-start(bf16[128,2048]{1,0:T(8,128)(2,1)} %get-tuple-element.285), channel_id=1, source_target_pairs={{0,4},{1,5},{2,6},{3,7},{4,0},{5,1},{6,2},{7,3},{8,12},{9,13},{10,... | collective-permute-start | bytes 1572872 | tf_op jit(solution)/shard_map/ppermute | solution.py:25
  552.8 20.0 %collective-permute-start.63 = (bf16[512,320]{0,1:T(8,128)(2,1)}, bf16[512,320]{0,1:T(8,128)(2,1)}, u32[]{:S(2)}, u32[]{:S(2)}) collective-permute-start(bf16[512,320]{0,1:T(8,128)(2,1)} %add_convert_fusion.3), channel_id=1, source_target_pairs={{0,8},{1,9},{2,10},{3,11},{4,12},{5,13},{6,14},{7,15},{8,16},{9,17... | collective-permute-start | bytes 983048 | tf_op jit(solution)/shard_map/ppermute | solution.py:30
  575.1 29.1 %all-to-all-start.3 = ((bf16[8,64,320]{2,1,0:T(8,128)(2,1)}), bf16[8,64,320]{2,1,0:T(8,128)(2,1)S(1)}, u32[]{:S(2)}, u32[]{:S(2)}) async-start(bf16[8,64,320]{2,1,0:T(8,128)(2,1)} %bitcast.74), calls=%async_computation.6 | async-start | bytes 786432 | tf_op jit(solution)/shard_map/all_to_all | solution.py:39
  580.7 21.7 %collective-permute-start.64 = (bf16[64,2048]{1,0:T(8,128)(2,1)}, bf16[64,2048]{1,0:T(8,128)(2,1)}, u32[]{:S(2)}, u32[]{:S(2)}) collective-permute-start(bf16[64,2048]{1,0:T(8,128)(2,1)} %reduce-scatter.8.cloned.1.call-done), channel_id=1, source_target_pairs={{0,0},{8,1},{16,2},{24,3},{1,4},{9,5},{17,6},{25,7},{2,8},{10,9},{... | collective-permute-start | bytes 786440 | tf_op jit(solution)/shard_map/ppermute | solution.py:841
  (132 other events, 1477.2 us)
Sparse Core Ops, SparseCore 0:
  139.9 120.3 all-gather.1
  340.3 56.8 reduce-scatter.3
  406.4 104.4 reduce-scatter.5
  514.7 37.1 reduce-scatter.7

commit v4 on v3

--- a/solution.py
+++ b/solution.py
@@ -16,7 +16,7 @@
 F32 = jnp.float32
 ANY = pl.BlockSpec(memory_space=pl.ANY)
 SCALAR = pl.BlockSpec(memory_space=pltpu.SMEM)
-WORK = pl.CostEstimate(flops=1, bytes_accessed=1, transcendentals=0)
+WORK = pl.CostEstimate(flops=2 * 10**9, bytes_accessed=1, transcendentals=0)
 BF16 = jnp.bfloat16
 
 
@@ -819,42 +819,43 @@
     parts = (clock(even), peer)
     clock.tick(*send_rows(parts), mlp_total, *out_last)
     arrived = cross(*clock.past[:2])
-    (output,) = on_spans(
-        output_kernel,
-        own_spans(out_parts, out_arrived, [clock(part) for part in out_last]),
-        (middle,),
-        (((count, model), BF16),),
-        "output",
-        60,
-    )
+    out_last = [clock(part) for part in out_last]
     out_total = planes_reduce(clock(out_sum))
     mlp_back = exchange(clock(mlp_total).reshape(RANKS, local, 2 * own_units))
     attn_hop = onward(clock(ring_start(attn_sum, plane, planes)))
     clock.tick(attn_hop)
     attn_hop = onward(ring_add(attn_sum, 1, clock(attn_hop), plane, planes))
-    clock.tick(*arrived, output)
+    clock.tick(*arrived)
     arrived = [clock(part) for part in arrived]
     last = cross(*pass_rows(parts, arrived, 60))
+    (output,) = on_spans(
+        output_kernel,
+        own_spans(out_parts, out_arrived, out_last),
+        (clock(middle),),
+        (((count, model), BF16),),
+        "output",
+        60,
+    )
     clock.tick(attn_hop)
     attn_hop = onward(ring_add(attn_sum, 2, clock(attn_hop), plane, planes))
-    clock.tick(*last, mlp_back, out_total)
-    out_grad = lax.ppermute(clock(out_total), "dev", from_rank).astype(F32)
+    for step in range(3, planes - 1):
+        attn_hop = onward(ring_add(attn_sum, step, attn_hop, plane, planes))
+    clock.tick(*last, mlp_back, out_total, output, attn_hop)
     mlp_back = clock(mlp_back)
     last = [clock(part) for part in last]
+    attn_total = thin(ring_add(attn_sum, planes - 1, clock(attn_hop), plane, planes))
+    attn_back = exchange(attn_total.reshape(RANKS, local, width + HD))
     (input_grad,) = on_spans(
         input_back_kernel,
         own_spans(parts, arrived, last),
-        (middle_grad, gain_one, tokens),
+        (after(middle_grad, attn_total), gain_one, tokens),
         (((count, model), BF16),),
         "input_back",
         60,
     )
-    clock.tick(attn_hop, input_grad)
+    out_grad = lax.ppermute(after(out_total, attn_total), "dev", from_rank).astype(F32)
+    clock.tick(input_grad)
     down_grad = clock(down_total).astype(F32)
-    for step in range(3, planes - 1):
-        attn_hop = onward(ring_add(attn_sum, step, attn_hop, plane, planes))
-    attn_total = ring_add(attn_sum, planes - 1, clock(attn_hop), plane, planes)
-    attn_back = exchange(thin(attn_total).reshape(RANKS, local, width + HD))
 
     gate_grad, up_grad, mlp_gain_sum = on_rows(
         functools.partial(mlp_back_kernel, units),

time: 622 us -> 599 us (0.963)
  waiting for transfers between devices: 217 us -> 199 us
    ppermute x1, waiting for transfers between devices: 13.9 us -> 0.01 us  [per_device(): lax.ppermute(after(out_total, attn_total), 'dev', from_rank).astype(F32)]
    ppermute x12, waiting for transfers between devices: 59.4 us -> 50.9 us  [onward(): return lax.ppermute(block, 'dev', [(i, (i + RANKS) % n) for i in range(n)])]
    unnamed x214 -> x218, local copies, waits for them, and re-layouts: 38.5 us -> 38 us
  transfers between devices with their start and end apart: 73 -> 73, of which waited for: 36 -> 33; matrix products, arithmetic and copies ran while one was open for 17% -> 17% of each run, Pallas kernels for 18% -> 18%
where the time goes in v4:
time: 599 us; the launch traced here: 592 us
  waiting for transfers between devices  199 us (33%)
  Pallas kernels  117 us (20%)
  matrix products  110 us (18%)
  starting transfers between devices  90.8 us (15%)
  local copies, waits for them, and re-layouts  42.7 us (7%)
  other arithmetic  17.3 us (3%)
  between operations  15.6 us (3%)
    ppermute x48, waiting for transfers between devices, swap(): return lax.ppermute(block, 'dev', [(i, i ^ bit) for i in range(n)])  138 us
    ppermute x12, waiting for transfers between devices, onward(): return lax.ppermute(block, 'dev', [(i, (i + RANKS) % n) for i in range(n)])  50.9 us
    dot_general x8, matrix products, contract_rows(): lax.dot_general(left, right, (((0,), (0,)), ((), ())), preferred_element_...  47.2 us
    ppermute x48, starting transfers between devices, swap(): return lax.ppermute(block, 'dev', [(i, i ^ bit) for i in range(n)])  47 us
    pallas_call x4, Pallas kernels, attention_call(): pl.pallas_call(kernel, grid_spec=pltpu.PrefetchScalarGridSpec(num_scalar_...  42.3 us
    pallas_call x12, Pallas kernels, on_spans(): pl.pallas_call(functools.partial(sliced_kernel, function, places, len(arr...  40.8 us
    unnamed x218, local copies, waits for them, and re-layouts  38 us
    dot_general x4, matrix products, times_transposed(): lax.dot_general(left, right, (((1,), (1,)), ((), ())), preferred_element_...  35.8 us
  transfers between devices with their start and end apart: 73, of which 33 were waited for; matrix products, arithmetic and copies ran while one was open for 17% of the time, Pallas kernels for 18%

profile of v4, /device:TPU:1, one launch (start us, length us, event | category | flops | bytes accessed | tf_op | source)
XLA Modules:
  0.0 591.5 jit_solution(9380170025070392283)
XLA Ops:
  10.6 5.2 all-to-all-start
  15.8 3.4 collective-permute-start.2
  19.7 4.8 collective-permute-start.6
  35.0 3.4 collective-permute-start.8
  39.3 9.1 %collective-permute-done.9.refs_1_ = bf16[512,384]{1,0:T(8,128)(2,1)S(1)} collective-permute-done((bf16[512,384]{1,0:T(8,128)(2,1)S(1)}, bf16[512,384]{1,0:T(8,128)(2,1)S(1)}, u32[]{:S(2)}, u32[]{:S(2)}) %collective-permute-start.9) | collective-permute-done | bytes 393248 | tf_op jit(solution)/shard_map/ppermute | solution.py:30
  51.7 11.4 %collective-permute-done.11.refs_1_ = bf16[64,2048]{1,0:T(8,128)(2,1)S(1)} collective-permute-done((bf16[64,2048]{1,0:T(8,128)(2,1)}, bf16[64,2048]{1,0:T(8,128)(2,1)S(1)}, u32[]{:S(2)}, u32[]{:S(2)}) %collective-permute-start.11) | collective-permute-done | bytes 262176 | tf_op jit(solution)/shard_map/ppermute | solution.py:30
  63.9 4.3 collective-permute-start.12
  71.9 17.5 %collective-permute-done.14.refs_2_ = bf16[64,2048]{1,0:T(8,128)(2,1)} collective-permute-done((bf16[64,2048]{1,0:T(8,128)(2,1)S(1)}, bf16[64,2048]{1,0:T(8,128)(2,1)}, u32[]{:S(2)}, u32[]{:S(2)}) %collective-permute-start.14) | collective-permute-done | bytes 262176 | tf_op jit(solution)/shard_map/ppermute | solution.py:30
  93.1 4.2 all-to-all-start.1
  104.4 8.5 %attend.2 = (bf16[1,4,256,256]{3,2,1,0:T(8,128)(2,1)S(1)}, bf16[1,4,64,1024]{3,2,1,0:T(8,128)(2,1)S(1)}, bf16[1,1024,128]{2,1,0:T(8,128)(2,1)S(1)}, f32[1,4,1,1024]{3,2,1,0:T(1,128)S(1)}) custom-call(s32[1]{0:T(128)} %bitcast.m_ref, bf16[512,2048]{1,0:T(8,128)(2,1)S(1)} %copy-done.23, bf16[512,2048]{1,0:T(8,128)(2,1)} %collective-permute-done.12.refs_1_, ...), custom_call_target="tpu_custom_call" | custom-call | flops 2000000000 | bytes 1 | tf_op jit(solution)/shard_map/attend/pallas_call | solution.py:547
  115.2 5.8 collective-permute-done.18.refs_1_
  122.8 9.3 %attend.3 = (bf16[1,4,256,256]{3,2,1,0:T(8,128)(2,1)S(1)}, bf16[1,4,64,1024]{3,2,1,0:T(8,128)(2,1)S(1)}, bf16[1,1024,128]{2,1,0:T(8,128)(2,1)S(1)}, f32[1,4,1,1024]{3,2,1,0:T(1,128)S(1)}) custom-call(s32[1]{0:T(128)} %bitcast.m_ref, bf16[512,2048]{1,0:T(8,128)(2,1)} %norm.3.refs_0_, bf16[512,2048]{1,0:T(8,128)(2,1)} %collective-permute-done.17.refs_1_, ...), custom_call_target="tpu_custom_call" | custom-call | flops 2000000000 | bytes 1 | tf_op jit(solution)/shard_map/attend/pallas_call | solution.py:547
  150.6 13.0 %collective-permute-done.24.refs_2_ = bf16[256,2048]{1,0:T(8,128)(2,1)S(1)} collective-permute-done((bf16[256,2048]{1,0:T(8,128)(2,1)S(1)}, bf16[256,2048]{1,0:T(8,128)(2,1)S(1)}, u32[]{:S(2)}, u32[]{:S(2)}) %collective-permute-start.24) | collective-permute-done | bytes 1048608 | tf_op jit(solution)/shard_map/ppermute | solution.py:25
  164.7 22.5 %collective-permute-done.21.refs_2_ = bf16[256,2048]{1,0:T(8,128)(2,1)S(1)} collective-permute-done((bf16[256,2048]{1,0:T(8,128)(2,1)S(1)}, bf16[256,2048]{1,0:T(8,128)(2,1)S(1)}, u32[]{:S(2)}, u32[]{:S(2)}) %collective-permute-start.21) | collective-permute-done | bytes 1048608 | tf_op jit(solution)/shard_map/ppermute | solution.py:25
  190.4 11.0 %collective-permute-done.25.refs_4_ = bf16[128,2048]{1,0:T(8,128)(2,1)S(1)} collective-permute-done((bf16[128,2048]{1,0:T(8,128)(2,1)S(1)}, bf16[128,2048]{1,0:T(8,128)(2,1)S(1)}, u32[]{:S(2)}, u32[]{:S(2)}) %collective-permute-start.25) | collective-permute-done | bytes 524320 | tf_op jit(solution)/shard_map/ppermute | solution.py:25
  206.5 21.8 %collective-permute-done.29.refs_2_ = bf16[256,2048]{1,0:T(8,128)(2,1)S(1)} collective-permute-done((bf16[256,2048]{1,0:T(8,128)(2,1)S(1)}, bf16[256,2048]{1,0:T(8,128)(2,1)S(1)}, u32[]{:S(2)}, u32[]{:S(2)}) %collective-permute-start.29) | collective-permute-done | bytes 1048608 | tf_op jit(solution)/shard_map/ppermute | solution.py:25
  229.9 8.9 %collective-permute-done.31.refs_4_ = bf16[128,2048]{1,0:T(8,128)(2,1)S(1)} collective-permute-done((bf16[128,2048]{1,0:T(8,128)(2,1)S(1)}, bf16[128,2048]{1,0:T(8,128)(2,1)S(1)}, u32[]{:S(2)}, u32[]{:S(2)}) %collective-permute-start.31) | collective-permute-done | bytes 524320 | tf_op jit(solution)/shard_map/ppermute | solution.py:25
  242.0 4.1 collective-permute-start.32
  249.5 9.3 %all-gather.2.cloned.1.call-done.refs_0_ = bf16[2048,1408]{1,0:T(8,128)(2,1)} async-done(((bf16[512,1408]{1,0:T(8,128)(2,1)}), bf16[2048,1408]{1,0:T(8,128)(2,1)}) %all-gather.2.cloned.1.call-update) | async-done | bytes 5767184 | tf_op jit(solution)/shard_map/all_gather | solution.py:50
  262.1 10.0 %fusion.15 = f32[1024,1408]{1,0:T(8,128)S(1)} fusion(bf16[1024,2048]{1,0:T(8,128)(2,1)} %join.8, bf16[2048,1408]{1,0:T(8,128)(2,1)S(1)} %join.9), kind=kOutput, calls=%fused_computation.62 | convolution fusion | flops 5905580032 | bytes 15728640 | tf_op jit(solution)/shard_map/dot_general | solution.py:377
  277.1 9.4 %fusion.16 = f32[1024,1408]{1,0:T(8,128)S(1)} fusion(bf16[1024,2048]{1,0:T(8,128)(2,1)} %collective-permute-done.32, bf16[2048,1408]{1,0:T(8,128)(2,1)S(1)} %join.9), kind=kOutput, calls=%fused_computation.63 | convolution fusion | flops 5905580032 | bytes 15728640 | tf_op jit(solution)/shard_map/dot_general | solution.py:377
  290.7 3.6 convolution_convert_fusion.3
  294.9 3.6 convolution_convert_fusion.2.refs_0_
  303.7 5.4 fusion.17
  309.1 4.9 add_convert_fusion.1
  314.1 9.2 %multiply_convert_fusion.3 = (bf16[1024,704]{1,0:T(8,128)(2,1)S(1)}, bf16[1024,704]{1,0:T(8,128)(2,1)S(1)}) fusion(f32[1024,1408]{1,0:T(8,128)} %copy-done.87, bf16[1024,2048]{1,0:T(8,128)(2,1)} %collective-permute-done.37, bf16[704,2048]{1,0:T(8,128)(2,1)} %copy-done.85), kind=kOutput, calls=%fused_computation.9 | convolution fusion | flops 2962161664 | bytes 15728640 | tf_op jit(solution)/shard_map/dot_general | solution.py:385
  323.4 8.3 %convolution_convert_fusion.1 = bf16[1024,2048]{1,0:T(8,128)(2,1)} fusion(bf16[2048,1408]{1,0:T(8,128)(2,1)S(1)} %bitcast.56, bf16[1024,704]{1,0:T(8,128)(2,1)S(1)} %get-tuple-element.310, bf16[1024,704]{1,0:T(8,128)(2,1)S(1)} %get-tuple-element.309), kind=kOutput, calls=%fused_computation.3 | convolution fusion | flops 5913444352 | bytes 12845056 | tf_op jit(solution)/shard_map/dot_general | solution.py:385
  334.5 9.1 %multiply_convert_fusion.1 = (bf16[1024,704]{1,0:T(8,128)(2,1)S(1)}, bf16[1024,704]{1,0:T(8,128)(2,1)S(1)}) fusion(f32[1024,1408]{1,0:T(8,128)} %copy-done.86, bf16[1024,2048]{1,0:T(8,128)(2,1)} %copy-done.14, bf16[704,2048]{1,0:T(8,128)(2,1)} %copy-done.85), kind=kOutput, calls=%fused_computation.7 | convolution fusion | flops 2962161664 | bytes 15728640 | tf_op jit(solution)/shard_map/dot_general | solution.py:385
  343.6 9.2 %convolution_convert_fusion.refs_0_ = bf16[1024,2048]{1,0:T(8,128)(2,1)S(1)} fusion(bf16[2048,1408]{1,0:T(8,128)(2,1)} %copy-done.9, bf16[1024,704]{1,0:T(8,128)(2,1)S(1)} %get-tuple-element.308, bf16[1024,704]{1,0:T(8,128)(2,1)S(1)} %get-tuple-element.307), kind=kOutput, calls=%fused_computation.2 | convolution fusion | flops 5913444352 | bytes 12845056 | tf_op jit(solution)/shard_map/dot_general | solution.py:385
  352.8 3.6 send_rows.6
  357.7 12.1 %fusion.1 = f32[2048,1408]{1,0:T(8,128)} fusion(bf16[1024,2048]{1,0:T(8,128)(2,1)} %join.8, bf16[1024,704]{1,0:T(8,128)(2,1)S(1)} %get-tuple-element.308, bf16[1024,704]{1,0:T(8,128)(2,1)S(1)} %get-tuple-element.307), kind=kOutput, calls=%fused_computation.19 | convolution fusion | flops 5911347200 | bytes 18612224 | tf_op jit(solution)/shard_map/dot_general | solution.py:381
  369.8 10.4 %collective-permute-done.41.refs_2_ = bf16[256,2048]{1,0:T(8,128)(2,1)S(1)} collective-permute-done((bf16[256,2048]{1,0:T(8,128)(2,1)S(1)}, bf16[256,2048]{1,0:T(8,128)(2,1)S(1)}, u32[]{:S(2)}, u32[]{:S(2)}) %collective-permute-start.41) | collective-permute-done | bytes 1048608 | tf_op jit(solution)/shard_map/ppermute | solution.py:25
  384.1 14.0 %add_convert_fusion = bf16[2048,1408]{1,0:T(8,128)(2,1)} fusion(f32[2048,1408]{1,0:T(8,128)} %fusion.1, bf16[1024,2048]{1,0:T(8,128)(2,1)} %collective-permute-done.32, bf16[1024,704]{1,0:T(8,128)(2,1)S(1)} %copy-done.106, bf16[1024,704]{1,0:T(8,128)(2,1)S(1)} %copy-done.104), kind=kOutput, calls=%fused_computation | convolution fusion | flops 5917114368 | bytes 24379392 | tf_op jit(solution)/shard_map/dot_general | solution.py:381
  399.1 7.2 %middle_back.1 = (f32[256,2048]{1,0:T(8,128)}, bf16[256,2048]{1,0:T(8,128)(2,1)}) custom-call(bf16[1024,2048]{1,0:T(8,128)(2,1)} %copy-done.4, bf16[1024,2048]{1,0:T(8,128)(2,1)} %collective-permute-done.39.refs_1_, bf16[256,2048]{1,0:T(8,128)(2,1)} %copy-done.11, bf16[256,2048]{1,0:T(8,128)(2,1)} %copy-done.12, bf16[128,2048]{1,0:T(8,128)(2,1)} %copy-done.94, ...), custom_call_target="tpu_custom_call" | custom-call | flops 2000000000 | bytes 1 | tf_op jit(solution)/shard_map/middle_back/pallas_call | solution.py:143
  420.3 8.5 %collective-permute-done.47.refs_0_ = bf16[256,2048]{1,0:T(8,128)(2,1)S(1)} collective-permute-done((bf16[256,2048]{1,0:T(8,128)(2,1)}, bf16[256,2048]{1,0:T(8,128)(2,1)S(1)}, u32[]{:S(2)}, u32[]{:S(2)}) %collective-permute-start.47) | collective-permute-done | bytes 1048608 | tf_op jit(solution)/shard_map/ppermute | solution.py:25
  428.8 6.7 %collective-permute-done.45.refs_1_ = bf16[256,2048]{1,0:T(8,128)(2,1)S(1)} collective-permute-done((bf16[256,2048]{1,0:T(8,128)(2,1)}, bf16[256,2048]{1,0:T(8,128)(2,1)S(1)}, u32[]{:S(2)}, u32[]{:S(2)}) %collective-permute-start.45) | collective-permute-done | bytes 1048608 | tf_op jit(solution)/shard_map/ppermute | solution.py:25
  439.5 12.5 %attend_back.2 = (bf16[1,4,256,256]{3,2,1,0:T(8,128)(2,1)S(1)}, f32[1,4,256,64]{3,2,1,0:T(8,128)S(1)}, f32[1,4,256,64]{3,2,1,0:T(8,128)S(1)}) custom-call(s32[1]{0:T(128)} %bitcast.m_ref, bf16[256,2048]{1,0:T(8,128)(2,1)S(1)} %copy-done.28, bf16[256,2048]{1,0:T(8,128)(2,1)S(1)} %collective-permute-done.45.refs_1_, bf16[256,2048]{1,0:T(8,128)(2,1)} %copy-done.29, ...), custom_call_target="tpu_custom_call" | custom-call | flops 2000000000 | bytes 1 | tf_op jit(solution)/shard_map/attend_back/pallas_call | solution.py:547
  464.2 11.9 %attend_back.3 = (bf16[1,4,256,256]{3,2,1,0:T(8,128)(2,1)S(1)}, f32[1,4,256,64]{3,2,1,0:T(8,128)S(1)}, f32[1,4,256,64]{3,2,1,0:T(8,128)S(1)}) custom-call(s32[1]{0:T(128)} %bitcast.m_ref, bf16[512,2048]{1,0:T(8,128)(2,1)} %copy-done.25, bf16[512,2048]{1,0:T(8,128)(2,1)} %copy-done.26, bf16[1,4,64,1024]{3,2,1,0:T(8,128)(2,1)S(1)} %copy-done.78, ...), custom_call_target="tpu_custom_call" | custom-call | flops 2000000000 | bytes 1 | tf_op jit(solution)/shard_map/attend_back/pallas_call | solution.py:547
  478.2 4.7 odd_parts.3
  491.9 4.0 fusion.13
  509.1 5.6 all-to-all-start.2
  514.7 3.8 collective-permute-done.61
  522.1 6.1 %collective-permute-done.57.refs_2_ = bf16[256,2048]{1,0:T(8,128)(2,1)} collective-permute-done((bf16[256,2048]{1,0:T(8,128)(2,1)S(1)}, bf16[256,2048]{1,0:T(8,128)(2,1)}, u32[]{:S(2)}, u32[]{:S(2)}) %collective-permute-start.57) | collective-permute-done | bytes 1048608 | tf_op jit(solution)/shard_map/ppermute | solution.py:25
  539.4 5.5 output.1
  544.9 10.0 %collective-permute-done.59.refs_4_ = bf16[128,2048]{1,0:T(8,128)(2,1)} collective-permute-done((bf16[128,2048]{1,0:T(8,128)(2,1)}, bf16[128,2048]{1,0:T(8,128)(2,1)}, u32[]{:S(2)}, u32[]{:S(2)}) %collective-permute-start.59) | collective-permute-done | bytes 524320 | tf_op jit(solution)/shard_map/ppermute | solution.py:25
  558.5 4.6 collective-permute-start.64
  563.1 7.3 %all-to-all-start.3 = ((bf16[8,64,320]{2,1,0:T(8,128)(2,1)}), bf16[8,64,320]{2,1,0:T(8,128)(2,1)S(1)}, u32[]{:S(2)}, u32[]{:S(2)}) async-start(bf16[8,64,320]{2,1,0:T(8,128)(2,1)} %bitcast.76), calls=%async_computation.6 | async-start | bytes 786432 | tf_op jit(solution)/shard_map/all_to_all | solution.py:39
  572.7 6.9 %input_back.1 = bf16[256,2048]{1,0:T(8,128)(2,1)} custom-call(bf16[1024,2048]{1,0:T(8,128)(2,1)} %copy-done.2, bf16[1024,2048]{1,0:T(8,128)(2,1)} %collective-permute-done.55.refs_1_, bf16[256,2048]{1,0:T(8,128)(2,1)} %collective-permute-done.57.refs_2_, bf16[256,2048]{1,0:T(8,128)(2,1)} %collective-permute-done.58.refs_3_, ...), custom_call_target="tpu_custom_call" | custom-call | flops 2000000000 | bytes 1 | tf_op jit(solution)/shard_map/input_back/pallas_call | solution.py:143
  (419 shorter events, 180.1 us)
Async XLA Ops:
  10.6 24.4 %all-to-all-start = ((bf16[8,64,384]{2,1,0:T(8,128)(2,1)}), bf16[8,64,384]{2,1,0:T(8,128)(2,1)S(1)}, u32[]{:S(2)}, u32[]{:S(2)}) async-start(bf16[8,64,384]{2,1,0:T(8,128)(2,1)} %attn_parts.1), calls=%async_computation | async-start | bytes 786432 | tf_op jit(solution)/shard_map/all_to_all | solution.py:39
  35.0 28.1 %collective-permute-start.8 = (bf16[256,2048]{1,0:T(8,128)(2,1)S(1)}, bf16[256,2048]{1,0:T(8,128)(2,1)S(1)}, u32[]{:S(2)}, u32[]{:S(2)}) collective-permute-start(bf16[256,2048]{1,0:T(8,128)(2,1)S(1)} %copy-done.15), channel_id=1, source_target_pairs={{0,4},{1,5},{2,6},{3,7},{4,0},{5,1},{6,2},{7,3},{8,12},{9,13},{10,... | collective-permute-start | bytes 3145736 | tf_op jit(solution)/shard_map/ppermute | solution.py:25
  38.4 24.7 %collective-permute-start.7 = (bf16[256,2048]{1,0:T(8,128)(2,1)S(1)}, bf16[256,2048]{1,0:T(8,128)(2,1)S(1)}, u32[]{:S(2)}, u32[]{:S(2)}) collective-permute-start(bf16[256,2048]{1,0:T(8,128)(2,1)S(1)} %copy-done.15), channel_id=1, source_target_pairs={{0,2},{1,3},{2,0},{3,1},{4,6},{5,7},{6,4},{7,5},{8,10},{9,11},{10,... | collective-permute-start | bytes 3145736 | tf_op jit(solution)/shard_map/ppermute | solution.py:25
  63.9 25.5 %collective-permute-start.12 = (bf16[512,2048]{1,0:T(8,128)(2,1)S(1)}, bf16[512,2048]{1,0:T(8,128)(2,1)}, u32[]{:S(2)}, u32[]{:S(2)}) collective-permute-start(bf16[512,2048]{1,0:T(8,128)(2,1)S(1)} %norm.2.refs_0_), channel_id=1, source_target_pairs={{0,1},{1,0},{2,3},{3,2},{4,5},{5,4},{6,7},{7,6},{8,9},{9,8},{10,11... | collective-permute-start | bytes 6291464 | tf_op jit(solution)/shard_map/ppermute | solution.py:25
  69.7 19.8 %collective-permute-start.16 = (bf16[128,2048]{1,0:T(8,128)(2,1)S(1)}, bf16[128,2048]{1,0:T(8,128)(2,1)S(1)}, u32[]{:S(2)}, u32[]{:S(2)}) collective-permute-start(bf16[128,2048]{1,0:T(8,128)(2,1)S(1)} %slice.48), channel_id=1, source_target_pairs={{0,2},{1,3},{2,0},{3,1},{4,6},{5,7},{6,4},{7,5},{8,10},{9,11},{10,... | collective-permute-start | bytes 1572872 | tf_op jit(solution)/shard_map/ppermute | solution.py:25
  70.8 18.6 %collective-permute-start.15 = (bf16[128,2048]{1,0:T(8,128)(2,1)S(1)}, bf16[128,2048]{1,0:T(8,128)(2,1)S(1)}, u32[]{:S(2)}, u32[]{:S(2)}) collective-permute-start(bf16[128,2048]{1,0:T(8,128)(2,1)S(1)} %slice.47), channel_id=1, source_target_pairs={{0,4},{1,5},{2,6},{3,7},{4,0},{5,1},{6,2},{7,3},{8,12},{9,13},{10,... | collective-permute-start | bytes 1572872 | tf_op jit(solution)/shard_map/ppermute | solution.py:25
  71.8 17.6 %collective-permute-start.13 = (bf16[512,384]{1,0:T(8,128)(2,1)S(1)}, bf16[512,384]{1,0:T(8,128)(2,1)S(1)}, u32[]{:S(2)}, u32[]{:S(2)}) collective-permute-start(bf16[512,384]{1,0:T(8,128)(2,1)S(1)} %collective-permute-done.10.refs_2_), channel_id=1, source_target_pairs={{0,8},{1,9},{2,10},{3,11},{4,12},{5,13},{6,14},{7,15},{8,16},{9,17... | collective-permute-start | bytes 1179656 | tf_op jit(solution)/shard_map/ppermute | solution.py:30
  71.8 17.6 %collective-permute-start.14 = (bf16[64,2048]{1,0:T(8,128)(2,1)S(1)}, bf16[64,2048]{1,0:T(8,128)(2,1)}, u32[]{:S(2)}, u32[]{:S(2)}) collective-permute-start(bf16[64,2048]{1,0:T(8,128)(2,1)S(1)} %collective-permute-done.11.refs_1_), channel_id=1, source_target_pairs={{0,8},{1,9},{2,10},{3,11},{4,12},{5,13},{6,14},{7,15},{8,16},{9,17... | collective-permute-start | bytes 786440 | tf_op jit(solution)/shard_map/ppermute | solution.py:30
  91.6 29.4 %collective-permute-start.17 = (bf16[512,2048]{1,0:T(8,128)(2,1)}, bf16[512,2048]{1,0:T(8,128)(2,1)}, u32[]{:S(2)}, u32[]{:S(2)}) collective-permute-start(bf16[512,2048]{1,0:T(8,128)(2,1)} %norm.3.refs_0_), channel_id=1, source_target_pairs={{0,1},{1,0},{2,3},{3,2},{4,5},{5,4},{6,7},{7,6},{8,9},{9,8},{10,11... | collective-permute-start | bytes 6291464 | tf_op jit(solution)/shard_map/ppermute | solution.py:25
  93.1 28.0 %all-to-all-start.1 = ((bf16[8,64,1408]{2,1,0:T(8,128)(2,1)}), bf16[8,64,1408]{2,1,0:T(8,128)(2,1)}, u32[]{:S(2)}, u32[]{:S(2)}) async-start(bf16[8,64,1408]{2,1,0:T(8,128)(2,1)} %mlp_parts.1), calls=%async_computation.1 | async-start | bytes 2883584 | tf_op jit(solution)/shard_map/all_to_all | solution.py:39
  97.3 161.5 %all-gather.2.cloned.1.call-start = ((), (), s32[]{:S(2)}) async-start(), calls=%async_computation.7 | async-start | bytes 7208960 | tf_op jit(solution)/shard_map/all_gather | solution.py:50
  101.3 19.7 %collective-permute-start.18 = (bf16[176,2048]{1,0:T(8,128)(2,1)}, bf16[176,2048]{1,0:T(8,128)(2,1)S(1)}, u32[]{:S(2)}, u32[]{:S(2)}) collective-permute-start(bf16[176,2048]{1,0:T(8,128)(2,1)} %refs_0_.1), channel_id=1, source_target_pairs={{0,8},{1,9},{2,10},{3,11},{4,12},{5,13},{6,14},{7,15},{8,16},{9,17... | collective-permute-start | bytes 2162696 | tf_op jit(solution)/shard_map/ppermute | solution.py:30
  101.3 30.8 %collective-permute-start.19 = (bf16[64,2048]{1,0:T(8,128)(2,1)}, bf16[64,2048]{1,0:T(8,128)(2,1)S(1)}, u32[]{:S(2)}, u32[]{:S(2)}) collective-permute-start(bf16[64,2048]{1,0:T(8,128)(2,1)} %collective-permute-done.14.refs_2_), channel_id=1, source_target_pairs={{0,8},{1,9},{2,10},{3,11},{4,12},{5,13},{6,14},{7,15},{8,16},{9,17... | collective-permute-start | bytes 786440 | tf_op jit(solution)/shard_map/ppermute | solution.py:30
  138.4 259.7 %reduce-scatter.4.cloned.1.call-start = ((), (), s32[]{:S(2)}) async-start(), calls=%async_computation.8 | async-start | bytes 3604480 | tf_op jit(solution)/shard_map/reduce_scatter | solution.py:54
  138.4 25.2 %collective-permute-start.24 = (bf16[256,2048]{1,0:T(8,128)(2,1)S(1)}, bf16[256,2048]{1,0:T(8,128)(2,1)S(1)}, u32[]{:S(2)}, u32[]{:S(2)}) collective-permute-start(bf16[256,2048]{1,0:T(8,128)(2,1)S(1)} %copy-done.10), channel_id=1, source_target_pairs={{0,4},{1,5},{2,6},{3,7},{4,0},{5,1},{6,2},{7,3},{8,12},{9,13},{10,... | collective-permute-start | bytes 3145736 | tf_op jit(solution)/shard_map/ppermute | solution.py:25
  140.1 24.6 %collective-permute-start.23 = (bf16[256,2048]{1,0:T(8,128)(2,1)S(1)}, bf16[256,2048]{1,0:T(8,128)(2,1)S(1)}, u32[]{:S(2)}, u32[]{:S(2)}) collective-permute-start(bf16[256,2048]{1,0:T(8,128)(2,1)S(1)} %copy-done.10), channel_id=1, source_target_pairs={{0,2},{1,3},{2,0},{3,1},{4,6},{5,7},{6,4},{7,5},{8,10},{9,11},{10,... | collective-permute-start | bytes 3145736 | tf_op jit(solution)/shard_map/ppermute | solution.py:25
  148.4 38.8 %collective-permute-start.21 = (bf16[256,2048]{1,0:T(8,128)(2,1)S(1)}, bf16[256,2048]{1,0:T(8,128)(2,1)S(1)}, u32[]{:S(2)}, u32[]{:S(2)}) collective-permute-start(bf16[256,2048]{1,0:T(8,128)(2,1)S(1)} %get-tuple-element.192), channel_id=1, source_target_pairs={{0,2},{1,3},{2,0},{3,1},{4,6},{5,7},{6,4},{7,5},{8,10},{9,11},{10,... | collective-permute-start | bytes 3145736 | tf_op jit(solution)/shard_map/ppermute | solution.py:25
  149.4 37.8 %collective-permute-start.22 = (bf16[256,2048]{1,0:T(8,128)(2,1)S(1)}, bf16[256,2048]{1,0:T(8,128)(2,1)S(1)}, u32[]{:S(2)}, u32[]{:S(2)}) collective-permute-start(bf16[256,2048]{1,0:T(8,128)(2,1)S(1)} %get-tuple-element.193), channel_id=1, source_target_pairs={{0,4},{1,5},{2,6},{3,7},{4,0},{5,1},{6,2},{7,3},{8,12},{9,13},{10,... | collective-permute-start | bytes 3145736 | tf_op jit(solution)/shard_map/ppermute | solution.py:25
  150.6 39.8 %collective-permute-start.27 = (bf16[176,2048]{1,0:T(8,128)(2,1)S(1)}, bf16[176,2048]{1,0:T(8,128)(2,1)S(1)}, u32[]{:S(2)}, u32[]{:S(2)}) collective-permute-start(bf16[176,2048]{1,0:T(8,128)(2,1)S(1)} %copy-done.49), channel_id=1, source_target_pairs={{0,8},{1,9},{2,10},{3,11},{4,12},{5,13},{6,14},{7,15},{8,16},{9,17... | collective-permute-start | bytes 2162696 | tf_op jit(solution)/shard_map/ppermute | solution.py:30
  205.6 22.7 %collective-permute-start.29 = (bf16[256,2048]{1,0:T(8,128)(2,1)S(1)}, bf16[256,2048]{1,0:T(8,128)(2,1)S(1)}, u32[]{:S(2)}, u32[]{:S(2)}) collective-permute-start(bf16[256,2048]{1,0:T(8,128)(2,1)S(1)} %get-tuple-element.206.refs_0_), channel_id=1, source_target_pairs={{0,4},{1,5},{2,6},{3,7},{4,0},{5,1},{6,2},{7,3},{8,12},{9,13},{10,... | collective-permute-start | bytes 3145736 | tf_op jit(solution)/shard_map/ppermute | solution.py:25
  205.9 22.4 %collective-permute-start.28 = (bf16[256,2048]{1,0:T(8,128)(2,1)S(1)}, bf16[256,2048]{1,0:T(8,128)(2,1)S(1)}, u32[]{:S(2)}, u32[]{:S(2)}) collective-permute-start(bf16[256,2048]{1,0:T(8,128)(2,1)S(1)} %get-tuple-element.206.refs_0_), channel_id=1, source_target_pairs={{0,2},{1,3},{2,0},{3,1},{4,6},{5,7},{6,4},{7,5},{8,10},{9,11},{10,... | collective-permute-start | bytes 3145736 | tf_op jit(solution)/shard_map/ppermute | solution.py:25
  242.0 33.1 %collective-permute-start.32 = (bf16[1024,2048]{1,0:T(8,128)(2,1)}, bf16[1024,2048]{1,0:T(8,128)(2,1)}, u32[]{:S(2)}, u32[]{:S(2)}) collective-permute-start(bf16[1024,2048]{1,0:T(8,128)(2,1)} %join.8), channel_id=1, source_target_pairs={{0,1},{1,0},{2,3},{3,2},{4,5},{5,4},{6,7},{7,6},{8,9},{9,8},{10,11... | collective-permute-start | bytes 12582920 | tf_op jit(solution)/shard_map/ppermute | solution.py:25
  247.8 27.3 %collective-permute-start.36 = (bf16[128,2048]{1,0:T(8,128)(2,1)}, bf16[128,2048]{1,0:T(8,128)(2,1)}, u32[]{:S(2)}, u32[]{:S(2)}) collective-permute-start(bf16[128,2048]{1,0:T(8,128)(2,1)} %slice.56), channel_id=1, source_target_pairs={{0,2},{1,3},{2,0},{3,1},{4,6},{5,7},{6,4},{7,5},{8,10},{9,11},{10,... | collective-permute-start | bytes 1572872 | tf_op jit(solution)/shard_map/ppermute | solution.py:25
  248.4 26.7 %collective-permute-start.35 = (bf16[128,2048]{1,0:T(8,128)(2,1)}, bf16[128,2048]{1,0:T(8,128)(2,1)}, u32[]{:S(2)}, u32[]{:S(2)}) collective-permute-start(bf16[128,2048]{1,0:T(8,128)(2,1)} %slice.55), channel_id=1, source_target_pairs={{0,4},{1,5},{2,6},{3,7},{4,0},{5,1},{6,2},{7,3},{8,12},{9,13},{10,... | collective-permute-start | bytes 1572872 | tf_op jit(solution)/shard_map/ppermute | solution.py:25
  258.9 30.1 %collective-permute-start.33 = (bf16[176,2048]{1,0:T(8,128)(2,1)}, bf16[176,2048]{1,0:T(8,128)(2,1)S(1)}, u32[]{:S(2)}, u32[]{:S(2)}) collective-permute-start(bf16[176,2048]{1,0:T(8,128)(2,1)} %copy-done.51), channel_id=1, source_target_pairs={{0,8},{1,9},{2,10},{3,11},{4,12},{5,13},{6,14},{7,15},{8,16},{9,17... | collective-permute-start | bytes 2162696 | tf_op jit(solution)/shard_map/ppermute | solution.py:30
  276.6 22.0 %collective-permute-start.37 = (bf16[1024,2048]{1,0:T(8,128)(2,1)S(1)}, bf16[1024,2048]{1,0:T(8,128)(2,1)}, u32[]{:S(2)}, u32[]{:S(2)}) collective-permute-start(bf16[1024,2048]{1,0:T(8,128)(2,1)S(1)} %join.10), channel_id=1, source_target_pairs={{0,1},{1,0},{2,3},{3,2},{4,5},{5,4},{6,7},{7,6},{8,9},{9,8},{10,11... | collective-permute-start | bytes 12582920 | tf_op jit(solution)/shard_map/ppermute | solution.py:25
  331.7 21.1 %collective-permute-start.39 = (bf16[1024,2048]{1,0:T(8,128)(2,1)}, bf16[1024,2048]{1,0:T(8,128)(2,1)}, u32[]{:S(2)}, u32[]{:S(2)}) collective-permute-start(bf16[1024,2048]{1,0:T(8,128)(2,1)} %convolution_convert_fusion.1), channel_id=1, source_target_pairs={{0,1},{1,0},{2,3},{3,2},{4,5},{5,4},{6,7},{7,6},{8,9},{9,8},{10,11... | collective-permute-start | bytes 12582920 | tf_op jit(solution)/shard_map/ppermute | solution.py:25
  332.1 172.4 %reduce-scatter.6.cloned.1.call-start = ((), (), s32[]{:S(2)}) async-start(), calls=%async_computation.9 | async-start | bytes 7208960 | tf_op jit(solution)/shard_map/reduce_scatter | solution.py:54
  332.1 25.0 %collective-permute-start.38 = (bf16[256,2048]{1,0:T(8,128)(2,1)}, bf16[256,2048]{1,0:T(8,128)(2,1)S(1)}, u32[]{:S(2)}, u32[]{:S(2)}) collective-permute-start(bf16[256,2048]{1,0:T(8,128)(2,1)} %copy-done.43), channel_id=1, source_target_pairs={{0,2},{1,3},{2,0},{3,1},{4,6},{5,7},{6,4},{7,5},{8,10},{9,11},{10,... | collective-permute-start | bytes 3145736 | tf_op jit(solution)/shard_map/ppermute | solution.py:25
  333.3 24.4 %collective-permute-start.40 = (bf16[256,2048]{1,0:T(8,128)(2,1)S(1)}, bf16[256,2048]{1,0:T(8,128)(2,1)S(1)}, u32[]{:S(2)}, u32[]{:S(2)}) collective-permute-start(bf16[256,2048]{1,0:T(8,128)(2,1)S(1)} %get-tuple-element.231), channel_id=1, source_target_pairs={{0,4},{1,5},{2,6},{3,7},{4,0},{5,1},{6,2},{7,3},{8,12},{9,13},{10,... | collective-permute-start | bytes 3145736 | tf_op jit(solution)/shard_map/ppermute | solution.py:25
  356.4 23.8 %collective-permute-start.41 = (bf16[256,2048]{1,0:T(8,128)(2,1)S(1)}, bf16[256,2048]{1,0:T(8,128)(2,1)S(1)}, u32[]{:S(2)}, u32[]{:S(2)}) collective-permute-start(bf16[256,2048]{1,0:T(8,128)(2,1)S(1)} %get-tuple-element.229), channel_id=1, source_target_pairs={{0,2},{1,3},{2,0},{3,1},{4,6},{5,7},{6,4},{7,5},{8,10},{9,11},{10,... | collective-permute-start | bytes 3145736 | tf_op jit(solution)/shard_map/ppermute | solution.py:25
  356.7 23.7 %collective-permute-start.42 = (bf16[256,2048]{1,0:T(8,128)(2,1)S(1)}, bf16[256,2048]{1,0:T(8,128)(2,1)S(1)}, u32[]{:S(2)}, u32[]{:S(2)}) collective-permute-start(bf16[256,2048]{1,0:T(8,128)(2,1)S(1)} %get-tuple-element.230), channel_id=1, source_target_pairs={{0,4},{1,5},{2,6},{3,7},{4,0},{5,1},{6,2},{7,3},{8,12},{9,13},{10,... | collective-permute-start | bytes 3145736 | tf_op jit(solution)/shard_map/ppermute | solution.py:25
  398.1 158.2 %reduce-scatter.8.cloned.1.call-start = ((), (), s32[]{:S(2)}) async-start(), calls=%async_computation.10 | async-start | bytes 1310720 | tf_op jit(solution)/shard_map/reduce_scatter | solution.py:54
  406.2 22.6 %collective-permute-start.47 = (bf16[256,2048]{1,0:T(8,128)(2,1)}, bf16[256,2048]{1,0:T(8,128)(2,1)S(1)}, u32[]{:S(2)}, u32[]{:S(2)}) collective-permute-start(bf16[256,2048]{1,0:T(8,128)(2,1)} %get-tuple-element.251.refs_0_), channel_id=1, source_target_pairs={{0,4},{1,5},{2,6},{3,7},{4,0},{5,1},{6,2},{7,3},{8,12},{9,13},{10,... | collective-permute-start | bytes 3145736 | tf_op jit(solution)/shard_map/ppermute | solution.py:25
  407.2 21.6 %collective-permute-start.46 = (bf16[256,2048]{1,0:T(8,128)(2,1)}, bf16[256,2048]{1,0:T(8,128)(2,1)S(1)}, u32[]{:S(2)}, u32[]{:S(2)}) collective-permute-start(bf16[256,2048]{1,0:T(8,128)(2,1)} %get-tuple-element.251.refs_0_), channel_id=1, source_target_pairs={{0,1},{1,0},{2,3},{3,2},{4,5},{5,4},{6,7},{7,6},{8,9},{9,8},{10,11... | collective-permute-start | bytes 3145736 | tf_op jit(solution)/shard_map/ppermute | solution.py:25
  410.4 25.1 %collective-permute-start.45 = (bf16[256,2048]{1,0:T(8,128)(2,1)}, bf16[256,2048]{1,0:T(8,128)(2,1)S(1)}, u32[]{:S(2)}, u32[]{:S(2)}) collective-permute-start(bf16[256,2048]{1,0:T(8,128)(2,1)} %get-tuple-element.251.refs_0_), channel_id=1, source_target_pairs={{0,2},{1,3},{2,0},{3,1},{4,6},{5,7},{6,4},{7,5},{8,10},{9,11},{10,... | collective-permute-start | bytes 3145736 | tf_op jit(solution)/shard_map/ppermute | solution.py:25
  436.3 16.5 %collective-permute-start.51 = (bf16[128,2048]{1,0:T(8,128)(2,1)S(1)}, bf16[128,2048]{1,0:T(8,128)(2,1)S(1)}, u32[]{:S(2)}, u32[]{:S(2)}) collective-permute-start(bf16[128,2048]{1,0:T(8,128)(2,1)S(1)} %slice.61), channel_id=1, source_target_pairs={{0,2},{1,3},{2,0},{3,1},{4,6},{5,7},{6,4},{7,5},{8,10},{9,11},{10,... | collective-permute-start | bytes 1572872 | tf_op jit(solution)/shard_map/ppermute | solution.py:25
  436.4 16.5 %collective-permute-start.50 = (bf16[128,2048]{1,0:T(8,128)(2,1)S(1)}, bf16[128,2048]{1,0:T(8,128)(2,1)S(1)}, u32[]{:S(2)}, u32[]{:S(2)}) collective-permute-start(bf16[128,2048]{1,0:T(8,128)(2,1)S(1)} %slice.60), channel_id=1, source_target_pairs={{0,4},{1,5},{2,6},{3,7},{4,0},{5,1},{6,2},{7,3},{8,12},{9,13},{10,... | collective-permute-start | bytes 1572872 | tf_op jit(solution)/shard_map/ppermute | solution.py:25
  482.9 16.3 %collective-permute-start.55 = (bf16[1024,2048]{1,0:T(8,128)(2,1)}, bf16[1024,2048]{1,0:T(8,128)(2,1)}, u32[]{:S(2)}, u32[]{:S(2)}) collective-permute-start(bf16[1024,2048]{1,0:T(8,128)(2,1)} %odd_parts.3), channel_id=1, source_target_pairs={{0,1},{1,0},{2,3},{3,2},{4,5},{5,4},{6,7},{7,6},{8,9},{9,8},{10,11... | collective-permute-start | bytes 12582920 | tf_op jit(solution)/shard_map/ppermute | solution.py:25
  504.5 23.7 %collective-permute-start.57 = (bf16[256,2048]{1,0:T(8,128)(2,1)S(1)}, bf16[256,2048]{1,0:T(8,128)(2,1)}, u32[]{:S(2)}, u32[]{:S(2)}) collective-permute-start(bf16[256,2048]{1,0:T(8,128)(2,1)S(1)} %get-tuple-element.278), channel_id=1, source_target_pairs={{0,2},{1,3},{2,0},{3,1},{4,6},{5,7},{6,4},{7,5},{8,10},{9,11},{10,... | collective-permute-start | bytes 3145736 | tf_op jit(solution)/shard_map/ppermute | solution.py:25
  505.7 23.2 %collective-permute-start.58 = (bf16[256,2048]{1,0:T(8,128)(2,1)S(1)}, bf16[256,2048]{1,0:T(8,128)(2,1)}, u32[]{:S(2)}, u32[]{:S(2)}) collective-permute-start(bf16[256,2048]{1,0:T(8,128)(2,1)S(1)} %get-tuple-element.279), channel_id=1, source_target_pairs={{0,4},{1,5},{2,6},{3,7},{4,0},{5,1},{6,2},{7,3},{8,12},{9,13},{10,... | collective-permute-start | bytes 3145736 | tf_op jit(solution)/shard_map/ppermute | solution.py:25
  509.1 46.5 %all-to-all-start.2 = ((bf16[8,64,1408]{2,1,0:T(8,128)(2,1)}), bf16[8,64,1408]{2,1,0:T(8,128)(2,1)S(1)}, u32[]{:S(2)}, u32[]{:S(2)}) async-start(bf16[8,64,1408]{2,1,0:T(8,128)(2,1)} %bitcast.77), calls=%async_computation.4 | async-start | bytes 2883584 | tf_op jit(solution)/shard_map/all_to_all | solution.py:39
  520.5 16.1 %collective-permute-start.62 = (bf16[512,320]{0,1:T(8,128)(2,1)}, bf16[512,320]{0,1:T(8,128)(2,1)}, u32[]{:S(2)}, u32[]{:S(2)}) collective-permute-start(bf16[512,320]{0,1:T(8,128)(2,1)} %add_convert_fusion.4), channel_id=1, source_target_pairs={{0,8},{1,9},{2,10},{3,11},{4,12},{5,13},{6,14},{7,15},{8,16},{9,17... | collective-permute-start | bytes 983048 | tf_op jit(solution)/shard_map/ppermute | solution.py:30
  531.9 22.9 %collective-permute-start.59 = (bf16[128,2048]{1,0:T(8,128)(2,1)}, bf16[128,2048]{1,0:T(8,128)(2,1)}, u32[]{:S(2)}, u32[]{:S(2)}) collective-permute-start(bf16[128,2048]{1,0:T(8,128)(2,1)} %get-tuple-element.287), channel_id=1, source_target_pairs={{0,2},{1,3},{2,0},{3,1},{4,6},{5,7},{6,4},{7,5},{8,10},{9,11},{10,... | collective-permute-start | bytes 1572872 | tf_op jit(solution)/shard_map/ppermute | solution.py:25
  532.6 23.0 %collective-permute-start.60 = (bf16[128,2048]{1,0:T(8,128)(2,1)}, bf16[128,2048]{1,0:T(8,128)(2,1)}, u32[]{:S(2)}, u32[]{:S(2)}) collective-permute-start(bf16[128,2048]{1,0:T(8,128)(2,1)} %get-tuple-element.288), channel_id=1, source_target_pairs={{0,4},{1,5},{2,6},{3,7},{4,0},{5,1},{6,2},{7,3},{8,12},{9,13},{10,... | collective-permute-start | bytes 1572872 | tf_op jit(solution)/shard_map/ppermute | solution.py:25
  538.6 17.0 %collective-permute-start.63 = (bf16[512,320]{0,1:T(8,128)(2,1)}, bf16[512,320]{0,1:T(8,128)(2,1)S(1)}, u32[]{:S(2)}, u32[]{:S(2)}) collective-permute-start(bf16[512,320]{0,1:T(8,128)(2,1)} %add_convert_fusion.3), channel_id=1, source_target_pairs={{0,8},{1,9},{2,10},{3,11},{4,12},{5,13},{6,14},{7,15},{8,16},{9,17... | collective-permute-start | bytes 983048 | tf_op jit(solution)/shard_map/ppermute | solution.py:30
  558.5 23.0 %collective-permute-start.64 = (bf16[64,2048]{1,0:T(8,128)(2,1)}, bf16[64,2048]{1,0:T(8,128)(2,1)}, u32[]{:S(2)}, u32[]{:S(2)}) collective-permute-start(bf16[64,2048]{1,0:T(8,128)(2,1)} %reduce-scatter.8.cloned.1.call-done), channel_id=1, source_target_pairs={{0,0},{8,1},{16,2},{24,3},{1,4},{9,5},{17,6},{25,7},{2,8},{10,9},{... | collective-permute-start | bytes 786440 | tf_op jit(solution)/shard_map/ppermute | solution.py:856
  563.1 20.1 %all-to-all-start.3 = ((bf16[8,64,320]{2,1,0:T(8,128)(2,1)}), bf16[8,64,320]{2,1,0:T(8,128)(2,1)S(1)}, u32[]{:S(2)}, u32[]{:S(2)}) async-start(bf16[8,64,320]{2,1,0:T(8,128)(2,1)} %bitcast.76), calls=%async_computation.6 | async-start | bytes 786432 | tf_op jit(solution)/shard_map/all_to_all | solution.py:39
  (135 other events, 1434.5 us)
Sparse Core Ops, SparseCore 0:
  138.5 120.3 all-gather.1
  332.2 56.8 reduce-scatter.3
  398.2 104.6 reduce-scatter.5
  505.7 35.6 reduce-scatter.7

commit v5 on v4

--- a/solution.py
+++ b/solution.py
@@ -16,7 +16,8 @@
 F32 = jnp.float32
 ANY = pl.BlockSpec(memory_space=pl.ANY)
 SCALAR = pl.BlockSpec(memory_space=pltpu.SMEM)
-WORK = pl.CostEstimate(flops=2 * 10**9, bytes_accessed=1, transcendentals=0)
+WORK = pl.CostEstimate(flops=2400000000, bytes_accessed=1, transcendentals=0)
+ATTENTION_WORK = pl.CostEstimate(flops=2000000000, bytes_accessed=1, transcendentals=0)
 BF16 = jnp.bfloat16
 
 
@@ -559,7 +560,7 @@
         ),
         out_shape=[jax.ShapeDtypeStruct(shape, dtype) for shape, dtype in shapes],
         compiler_params=pltpu.CompilerParams(vmem_limit_bytes=48 * 2**20),
-        cost_estimate=WORK,
+        cost_estimate=ATTENTION_WORK,
         name=name,
     )(mine, *blocks, *others)
 

time: 599 us -> 597 us (level)
  waiting for transfers between devices: 199 us -> 206 us
    unnamed x218 -> x210, local copies, waits for them, and re-layouts: 38 us -> 35.6 us
  transfers between devices with their start and end apart: 73 -> 73, of which waited for: 33 -> 34; matrix products, arithmetic and copies ran while one was open for 17% -> 17% of each run, Pallas kernels for 18% -> 18%
where the time goes in v5:
time: 597 us; the launch traced here: 591 us
  waiting for transfers between devices  206 us (35%)
  Pallas kernels  115 us (19%)
  matrix products  109 us (18%)
  starting transfers between devices  88.2 us (15%)
  local copies, waits for them, and re-layouts  40.3 us (7%)
  other arithmetic  16.6 us (3%)
  between operations  15.5 us (3%)
    ppermute x48, waiting for transfers between devices, swap(): return lax.ppermute(block, 'dev', [(i, i ^ bit) for i in range(n)])  139 us
    ppermute x12, waiting for transfers between devices, onward(): return lax.ppermute(block, 'dev', [(i, (i + RANKS) % n) for i in range(n)])  56.8 us
    ppermute x48, starting transfers between devices, swap(): return lax.ppermute(block, 'dev', [(i, i ^ bit) for i in range(n)])  46.9 us
    dot_general x8, matrix products, contract_rows(): lax.dot_general(left, right, (((0,), (0,)), ((), ())), preferred_element_...  46.8 us
    pallas_call x4, Pallas kernels, attention_call(): pl.pallas_call(kernel, grid_spec=pltpu.PrefetchScalarGridSpec(num_scalar_...  42.3 us
    pallas_call x12, Pallas kernels, on_spans(): pl.pallas_call(functools.partial(sliced_kernel, function, places, len(arr...  40.6 us
    dot_general x4, matrix products, times_transposed(): lax.dot_general(left, right, (((1,), (1,)), ((), ())), preferred_element_...  35.8 us
    unnamed x210, local copies, waits for them, and re-layouts  35.6 us
  transfers between devices with their start and end apart: 73, of which 34 were waited for; matrix products, arithmetic and copies ran while one was open for 17% of the time, Pallas kernels for 18%

profile of v5, /device:TPU:1, one launch (start us, length us, event | category | flops | bytes accessed | tf_op | source)
XLA Modules:
  0.0 590.7 jit_solution(15769493019913191408)
XLA Ops:
  10.6 5.2 all-to-all-start
  19.7 4.8 collective-permute-start.6
  34.7 3.9 collective-permute-start.8
  39.1 9.4 %collective-permute-done.9.refs_1_ = bf16[512,384]{1,0:T(8,128)(2,1)S(1)} collective-permute-done((bf16[512,384]{1,0:T(8,128)(2,1)S(1)}, bf16[512,384]{1,0:T(8,128)(2,1)S(1)}, u32[]{:S(2)}, u32[]{:S(2)}) %collective-permute-start.9) | collective-permute-done | bytes 393248 | tf_op jit(solution)/shard_map/ppermute | solution.py:31
  51.2 11.9 %collective-permute-done.11.refs_1_ = bf16[64,2048]{1,0:T(8,128)(2,1)S(1)} collective-permute-done((bf16[64,2048]{1,0:T(8,128)(2,1)}, bf16[64,2048]{1,0:T(8,128)(2,1)S(1)}, u32[]{:S(2)}, u32[]{:S(2)}) %collective-permute-start.11) | collective-permute-done | bytes 262176 | tf_op jit(solution)/shard_map/ppermute | solution.py:31
  64.0 4.4 collective-permute-start.12
  72.1 17.3 %collective-permute-done.14.refs_2_ = bf16[64,2048]{1,0:T(8,128)(2,1)S(1)} collective-permute-done((bf16[64,2048]{1,0:T(8,128)(2,1)S(1)}, bf16[64,2048]{1,0:T(8,128)(2,1)S(1)}, u32[]{:S(2)}, u32[]{:S(2)}) %collective-permute-start.14) | collective-permute-done | bytes 262176 | tf_op jit(solution)/shard_map/ppermute | solution.py:31
  92.7 4.2 all-to-all-start.1
  104.0 8.5 %attend.2 = (bf16[1,4,256,256]{3,2,1,0:T(8,128)(2,1)S(1)}, bf16[1,4,64,1024]{3,2,1,0:T(8,128)(2,1)S(1)}, bf16[1,1024,128]{2,1,0:T(8,128)(2,1)S(1)}, f32[1,4,1,1024]{3,2,1,0:T(1,128)S(1)}) custom-call(s32[1]{0:T(128)} %bitcast.m_ref, bf16[512,2048]{1,0:T(8,128)(2,1)S(1)} %copy-done.32, bf16[512,2048]{1,0:T(8,128)(2,1)} %collective-permute-done.12.refs_1_, ...), custom_call_target="tpu_custom_call" | custom-call | flops 2000000000 | bytes 1 | tf_op jit(solution)/shard_map/attend/pallas_call | solution.py:548
  114.8 5.9 collective-permute-done.18.refs_1_
  121.8 9.3 %attend.3 = (bf16[1,4,256,256]{3,2,1,0:T(8,128)(2,1)S(1)}, bf16[1,4,64,1024]{3,2,1,0:T(8,128)(2,1)S(1)}, bf16[1,1024,128]{2,1,0:T(8,128)(2,1)S(1)}, f32[1,4,1,1024]{3,2,1,0:T(1,128)S(1)}) custom-call(s32[1]{0:T(128)} %bitcast.m_ref, bf16[512,2048]{1,0:T(8,128)(2,1)} %norm.3.refs_0_, bf16[512,2048]{1,0:T(8,128)(2,1)} %collective-permute-done.17.refs_1_, ...), custom_call_target="tpu_custom_call" | custom-call | flops 2000000000 | bytes 1 | tf_op jit(solution)/shard_map/attend/pallas_call | solution.py:548
  149.6 13.0 %collective-permute-done.24.refs_2_ = bf16[256,2048]{1,0:T(8,128)(2,1)S(1)} collective-permute-done((bf16[256,2048]{1,0:T(8,128)(2,1)S(1)}, bf16[256,2048]{1,0:T(8,128)(2,1)S(1)}, u32[]{:S(2)}, u32[]{:S(2)}) %collective-permute-start.24) | collective-permute-done | bytes 1048608 | tf_op jit(solution)/shard_map/ppermute | solution.py:26
  163.7 22.5 %collective-permute-done.21.refs_2_ = bf16[256,2048]{1,0:T(8,128)(2,1)S(1)} collective-permute-done((bf16[256,2048]{1,0:T(8,128)(2,1)S(1)}, bf16[256,2048]{1,0:T(8,128)(2,1)S(1)}, u32[]{:S(2)}, u32[]{:S(2)}) %collective-permute-start.21) | collective-permute-done | bytes 1048608 | tf_op jit(solution)/shard_map/ppermute | solution.py:26
  189.5 11.0 %collective-permute-done.25.refs_4_ = bf16[128,2048]{1,0:T(8,128)(2,1)S(1)} collective-permute-done((bf16[128,2048]{1,0:T(8,128)(2,1)S(1)}, bf16[128,2048]{1,0:T(8,128)(2,1)S(1)}, u32[]{:S(2)}, u32[]{:S(2)}) %collective-permute-start.25) | collective-permute-done | bytes 524320 | tf_op jit(solution)/shard_map/ppermute | solution.py:26
  204.9 21.8 %collective-permute-done.29.refs_2_ = bf16[256,2048]{1,0:T(8,128)(2,1)S(1)} collective-permute-done((bf16[256,2048]{1,0:T(8,128)(2,1)S(1)}, bf16[256,2048]{1,0:T(8,128)(2,1)S(1)}, u32[]{:S(2)}, u32[]{:S(2)}) %collective-permute-start.29) | collective-permute-done | bytes 1048608 | tf_op jit(solution)/shard_map/ppermute | solution.py:26
  228.3 9.1 %collective-permute-done.31.refs_4_ = bf16[128,2048]{1,0:T(8,128)(2,1)S(1)} collective-permute-done((bf16[128,2048]{1,0:T(8,128)(2,1)S(1)}, bf16[128,2048]{1,0:T(8,128)(2,1)S(1)}, u32[]{:S(2)}, u32[]{:S(2)}) %collective-permute-start.31) | collective-permute-done | bytes 524320 | tf_op jit(solution)/shard_map/ppermute | solution.py:26
  240.4 4.1 collective-permute-start.32
  247.9 10.0 %all-gather.2.cloned.1.call-done.refs_0_ = bf16[2048,1408]{1,0:T(8,128)(2,1)} async-done(((bf16[512,1408]{1,0:T(8,128)(2,1)}), bf16[2048,1408]{1,0:T(8,128)(2,1)}) %all-gather.2.cloned.1.call-update) | async-done | bytes 5767184 | tf_op jit(solution)/shard_map/all_gather | solution.py:51
  261.1 10.0 %fusion.15 = f32[1024,1408]{1,0:T(8,128)S(1)} fusion(bf16[1024,2048]{1,0:T(8,128)(2,1)} %join.8, bf16[2048,1408]{1,0:T(8,128)(2,1)S(1)} %join.9), kind=kOutput, calls=%fused_computation.62 | convolution fusion | flops 5905580032 | bytes 15728640 | tf_op jit(solution)/shard_map/dot_general | solution.py:378
  275.2 9.4 %fusion.16 = f32[1024,1408]{1,0:T(8,128)S(1)} fusion(bf16[1024,2048]{1,0:T(8,128)(2,1)} %collective-permute-done.32, bf16[2048,1408]{1,0:T(8,128)(2,1)S(1)} %join.9), kind=kOutput, calls=%fused_computation.63 | convolution fusion | flops 5905580032 | bytes 15728640 | tf_op jit(solution)/shard_map/dot_general | solution.py:378
  288.5 3.6 convolution_convert_fusion.3
  292.7 3.6 convolution_convert_fusion.2.refs_0_
  302.4 5.0 fusion.17
  307.5 4.9 add_convert_fusion.1
  312.4 9.2 %multiply_convert_fusion.3 = (bf16[1024,704]{1,0:T(8,128)(2,1)S(1)}, bf16[1024,704]{1,0:T(8,128)(2,1)S(1)}) fusion(f32[1024,1408]{1,0:T(8,128)} %copy-done.84, bf16[1024,2048]{1,0:T(8,128)(2,1)} %collective-permute-done.37, bf16[704,2048]{1,0:T(8,128)(2,1)} %copy-done.82), kind=kOutput, calls=%fused_computation.9 | convolution fusion | flops 2962161664 | bytes 15728640 | tf_op jit(solution)/shard_map/dot_general | solution.py:386
  321.7 8.3 %convolution_convert_fusion.1 = bf16[1024,2048]{1,0:T(8,128)(2,1)} fusion(bf16[2048,1408]{1,0:T(8,128)(2,1)S(1)} %bitcast.56, bf16[1024,704]{1,0:T(8,128)(2,1)S(1)} %get-tuple-element.310, bf16[1024,704]{1,0:T(8,128)(2,1)S(1)} %get-tuple-element.309), kind=kOutput, calls=%fused_computation.3 | convolution fusion | flops 5913444352 | bytes 12845056 | tf_op jit(solution)/shard_map/dot_general | solution.py:386
  332.9 9.1 %multiply_convert_fusion.1 = (bf16[1024,704]{1,0:T(8,128)(2,1)S(1)}, bf16[1024,704]{1,0:T(8,128)(2,1)S(1)}) fusion(f32[1024,1408]{1,0:T(8,128)} %copy-done.83, bf16[1024,2048]{1,0:T(8,128)(2,1)} %copy-done.30, bf16[704,2048]{1,0:T(8,128)(2,1)} %copy-done.82), kind=kOutput, calls=%fused_computation.7 | convolution fusion | flops 2962161664 | bytes 15728640 | tf_op jit(solution)/shard_map/dot_general | solution.py:386
  341.9 9.2 %convolution_convert_fusion.refs_0_ = bf16[1024,2048]{1,0:T(8,128)(2,1)S(1)} fusion(bf16[2048,1408]{1,0:T(8,128)(2,1)} %copy-done.7, bf16[1024,704]{1,0:T(8,128)(2,1)S(1)} %get-tuple-element.308, bf16[1024,704]{1,0:T(8,128)(2,1)S(1)} %get-tuple-element.307), kind=kOutput, calls=%fused_computation.2 | convolution fusion | flops 5913444352 | bytes 12845056 | tf_op jit(solution)/shard_map/dot_general | solution.py:386
  351.1 3.6 send_rows.6
  356.3 12.1 %fusion.1 = f32[2048,1408]{1,0:T(8,128)} fusion(bf16[1024,2048]{1,0:T(8,128)(2,1)} %join.8, bf16[1024,704]{1,0:T(8,128)(2,1)S(1)} %get-tuple-element.308, bf16[1024,704]{1,0:T(8,128)(2,1)S(1)} %get-tuple-element.307), kind=kOutput, calls=%fused_computation.19 | convolution fusion | flops 5911347200 | bytes 18612224 | tf_op jit(solution)/shard_map/dot_general | solution.py:382
  368.3 10.2 %collective-permute-done.41.refs_2_ = bf16[256,2048]{1,0:T(8,128)(2,1)S(1)} collective-permute-done((bf16[256,2048]{1,0:T(8,128)(2,1)S(1)}, bf16[256,2048]{1,0:T(8,128)(2,1)S(1)}, u32[]{:S(2)}, u32[]{:S(2)}) %collective-permute-start.41) | collective-permute-done | bytes 1048608 | tf_op jit(solution)/shard_map/ppermute | solution.py:26
  382.6 14.0 %add_convert_fusion = bf16[2048,1408]{1,0:T(8,128)(2,1)} fusion(f32[2048,1408]{1,0:T(8,128)} %fusion.1, bf16[1024,2048]{1,0:T(8,128)(2,1)} %collective-permute-done.32, bf16[1024,704]{1,0:T(8,128)(2,1)S(1)} %copy-done.102, bf16[1024,704]{1,0:T(8,128)(2,1)S(1)} %copy-done.100), kind=kOutput, calls=%fused_computation | convolution fusion | flops 5917114368 | bytes 24379392 | tf_op jit(solution)/shard_map/dot_general | solution.py:382
  397.6 7.2 %middle_back.1 = (f32[256,2048]{1,0:T(8,128)}, bf16[256,2048]{1,0:T(8,128)(2,1)}) custom-call(bf16[1024,2048]{1,0:T(8,128)(2,1)} %copy-done.4, bf16[1024,2048]{1,0:T(8,128)(2,1)} %collective-permute-done.39.refs_1_, bf16[256,2048]{1,0:T(8,128)(2,1)} %copy-done.8, bf16[256,2048]{1,0:T(8,128)(2,1)} %copy-done.9, bf16[128,2048]{1,0:T(8,128)(2,1)} %copy-done.90, ...), custom_call_target="tpu_custom_call" | custom-call | flops 2400000000 | bytes 1 | tf_op jit(solution)/shard_map/middle_back/pallas_call | solution.py:144
  417.4 10.0 %collective-permute-done.47.refs_0_ = bf16[256,2048]{1,0:T(8,128)(2,1)S(1)} collective-permute-done((bf16[256,2048]{1,0:T(8,128)(2,1)}, bf16[256,2048]{1,0:T(8,128)(2,1)S(1)}, u32[]{:S(2)}, u32[]{:S(2)}) %collective-permute-start.47) | collective-permute-done | bytes 1048608 | tf_op jit(solution)/shard_map/ppermute | solution.py:26
  427.5 6.4 %collective-permute-done.45.refs_1_ = bf16[256,2048]{1,0:T(8,128)(2,1)S(1)} collective-permute-done((bf16[256,2048]{1,0:T(8,128)(2,1)}, bf16[256,2048]{1,0:T(8,128)(2,1)S(1)}, u32[]{:S(2)}, u32[]{:S(2)}) %collective-permute-start.45) | collective-permute-done | bytes 1048608 | tf_op jit(solution)/shard_map/ppermute | solution.py:26
  437.9 12.5 %attend_back.2 = (bf16[1,4,256,256]{3,2,1,0:T(8,128)(2,1)S(1)}, f32[1,4,256,64]{3,2,1,0:T(8,128)S(1)}, f32[1,4,256,64]{3,2,1,0:T(8,128)S(1)}) custom-call(s32[1]{0:T(128)} %bitcast.m_ref, bf16[256,2048]{1,0:T(8,128)(2,1)S(1)} %copy-done.36, bf16[256,2048]{1,0:T(8,128)(2,1)S(1)} %collective-permute-done.45.refs_1_, bf16[256,2048]{1,0:T(8,128)(2,1)} %copy-done.37, ...), custom_call_target="tpu_custom_call" | custom-call | flops 2000000000 | bytes 1 | tf_op jit(solution)/shard_map/attend_back/pallas_call | solution.py:548
  463.4 11.9 %attend_back.3 = (bf16[1,4,256,256]{3,2,1,0:T(8,128)(2,1)S(1)}, f32[1,4,256,64]{3,2,1,0:T(8,128)S(1)}, f32[1,4,256,64]{3,2,1,0:T(8,128)S(1)}) custom-call(s32[1]{0:T(128)} %bitcast.m_ref, bf16[512,2048]{1,0:T(8,128)(2,1)} %copy-done.34, bf16[512,2048]{1,0:T(8,128)(2,1)} %copy-done.35, bf16[1,4,64,1024]{3,2,1,0:T(8,128)(2,1)S(1)} %copy-done.75, ...), custom_call_target="tpu_custom_call" | custom-call | flops 2000000000 | bytes 1 | tf_op jit(solution)/shard_map/attend_back/pallas_call | solution.py:548
  477.4 4.7 odd_parts.3
  491.0 4.1 fusion.13
  508.1 5.7 all-to-all-start.2
  513.8 5.1 collective-permute-done.61
  521.0 6.4 %collective-permute-done.57.refs_2_ = bf16[256,2048]{1,0:T(8,128)(2,1)} collective-permute-done((bf16[256,2048]{1,0:T(8,128)(2,1)S(1)}, bf16[256,2048]{1,0:T(8,128)(2,1)}, u32[]{:S(2)}, u32[]{:S(2)}) %collective-permute-start.57) | collective-permute-done | bytes 1048608 | tf_op jit(solution)/shard_map/ppermute | solution.py:26
  532.3 7.2 %collective-permute-done.62 = bf16[512,320]{0,1:T(8,128)(2,1)} collective-permute-done((bf16[512,320]{0,1:T(8,128)(2,1)}, bf16[512,320]{0,1:T(8,128)(2,1)}, u32[]{:S(2)}, u32[]{:S(2)}) %collective-permute-start.62) | collective-permute-done | bytes 327712 | tf_op jit(solution)/shard_map/ppermute | solution.py:31
  541.5 5.4 output.1
  547.0 7.2 %collective-permute-done.59.refs_4_ = bf16[128,2048]{1,0:T(8,128)(2,1)} collective-permute-done((bf16[128,2048]{1,0:T(8,128)(2,1)}, bf16[128,2048]{1,0:T(8,128)(2,1)}, u32[]{:S(2)}, u32[]{:S(2)}) %collective-permute-start.59) | collective-permute-done | bytes 524320 | tf_op jit(solution)/shard_map/ppermute | solution.py:26
  557.7 4.4 collective-permute-start.64
  562.1 7.5 %all-to-all-start.3 = ((bf16[8,64,320]{2,1,0:T(8,128)(2,1)}), bf16[8,64,320]{2,1,0:T(8,128)(2,1)S(1)}, u32[]{:S(2)}, u32[]{:S(2)}) async-start(bf16[8,64,320]{2,1,0:T(8,128)(2,1)} %bitcast.76), calls=%async_computation.6 | async-start | bytes 786432 | tf_op jit(solution)/shard_map/all_to_all | solution.py:40
  571.9 6.9 %input_back.1 = bf16[256,2048]{1,0:T(8,128)(2,1)} custom-call(bf16[1024,2048]{1,0:T(8,128)(2,1)} %copy-done.2, bf16[1024,2048]{1,0:T(8,128)(2,1)} %collective-permute-done.55.refs_1_, bf16[256,2048]{1,0:T(8,128)(2,1)} %collective-permute-done.57.refs_2_, bf16[256,2048]{1,0:T(8,128)(2,1)} %collective-permute-done.58.refs_3_, ...), custom_call_target="tpu_custom_call" | custom-call | flops 2400000000 | bytes 1 | tf_op jit(solution)/shard_map/input_back/pallas_call | solution.py:144
  (411 shorter events, 174.1 us)
Async XLA Ops:
  10.6 24.0 %all-to-all-start = ((bf16[8,64,384]{2,1,0:T(8,128)(2,1)}), bf16[8,64,384]{2,1,0:T(8,128)(2,1)S(1)}, u32[]{:S(2)}, u32[]{:S(2)}) async-start(bf16[8,64,384]{2,1,0:T(8,128)(2,1)} %attn_parts.1), calls=%async_computation | async-start | bytes 786432 | tf_op jit(solution)/shard_map/all_to_all | solution.py:40
  34.7 28.5 %collective-permute-start.8 = (bf16[256,2048]{1,0:T(8,128)(2,1)S(1)}, bf16[256,2048]{1,0:T(8,128)(2,1)S(1)}, u32[]{:S(2)}, u32[]{:S(2)}) collective-permute-start(bf16[256,2048]{1,0:T(8,128)(2,1)S(1)} %copy-done.12), channel_id=1, source_target_pairs={{0,4},{1,5},{2,6},{3,7},{4,0},{5,1},{6,2},{7,3},{8,12},{9,13},{10,... | collective-permute-start | bytes 3145736 | tf_op jit(solution)/shard_map/ppermute | solution.py:26
  38.5 24.6 %collective-permute-start.7 = (bf16[256,2048]{1,0:T(8,128)(2,1)S(1)}, bf16[256,2048]{1,0:T(8,128)(2,1)S(1)}, u32[]{:S(2)}, u32[]{:S(2)}) collective-permute-start(bf16[256,2048]{1,0:T(8,128)(2,1)S(1)} %copy-done.12), channel_id=1, source_target_pairs={{0,2},{1,3},{2,0},{3,1},{4,6},{5,7},{6,4},{7,5},{8,10},{9,11},{10,... | collective-permute-start | bytes 3145736 | tf_op jit(solution)/shard_map/ppermute | solution.py:26
  64.0 25.4 %collective-permute-start.12 = (bf16[512,2048]{1,0:T(8,128)(2,1)S(1)}, bf16[512,2048]{1,0:T(8,128)(2,1)}, u32[]{:S(2)}, u32[]{:S(2)}) collective-permute-start(bf16[512,2048]{1,0:T(8,128)(2,1)S(1)} %norm.2.refs_0_), channel_id=1, source_target_pairs={{0,1},{1,0},{2,3},{3,2},{4,5},{5,4},{6,7},{7,6},{8,9},{9,8},{10,11... | collective-permute-start | bytes 6291464 | tf_op jit(solution)/shard_map/ppermute | solution.py:26
  69.8 19.6 %collective-permute-start.16 = (bf16[128,2048]{1,0:T(8,128)(2,1)S(1)}, bf16[128,2048]{1,0:T(8,128)(2,1)S(1)}, u32[]{:S(2)}, u32[]{:S(2)}) collective-permute-start(bf16[128,2048]{1,0:T(8,128)(2,1)S(1)} %slice.48), channel_id=1, source_target_pairs={{0,2},{1,3},{2,0},{3,1},{4,6},{5,7},{6,4},{7,5},{8,10},{9,11},{10,... | collective-permute-start | bytes 1572872 | tf_op jit(solution)/shard_map/ppermute | solution.py:26
  71.0 18.3 %collective-permute-start.15 = (bf16[128,2048]{1,0:T(8,128)(2,1)S(1)}, bf16[128,2048]{1,0:T(8,128)(2,1)S(1)}, u32[]{:S(2)}, u32[]{:S(2)}) collective-permute-start(bf16[128,2048]{1,0:T(8,128)(2,1)S(1)} %slice.47), channel_id=1, source_target_pairs={{0,4},{1,5},{2,6},{3,7},{4,0},{5,1},{6,2},{7,3},{8,12},{9,13},{10,... | collective-permute-start | bytes 1572872 | tf_op jit(solution)/shard_map/ppermute | solution.py:26
  71.6 17.8 %collective-permute-start.13 = (bf16[512,384]{1,0:T(8,128)(2,1)S(1)}, bf16[512,384]{1,0:T(8,128)(2,1)S(1)}, u32[]{:S(2)}, u32[]{:S(2)}) collective-permute-start(bf16[512,384]{1,0:T(8,128)(2,1)S(1)} %collective-permute-done.10.refs_2_), channel_id=1, source_target_pairs={{0,8},{1,9},{2,10},{3,11},{4,12},{5,13},{6,14},{7,15},{8,16},{9,17... | collective-permute-start | bytes 1179656 | tf_op jit(solution)/shard_map/ppermute | solution.py:31
  71.6 17.8 %collective-permute-start.14 = (bf16[64,2048]{1,0:T(8,128)(2,1)S(1)}, bf16[64,2048]{1,0:T(8,128)(2,1)S(1)}, u32[]{:S(2)}, u32[]{:S(2)}) collective-permute-start(bf16[64,2048]{1,0:T(8,128)(2,1)S(1)} %collective-permute-done.11.refs_1_), channel_id=1, source_target_pairs={{0,8},{1,9},{2,10},{3,11},{4,12},{5,13},{6,14},{7,15},{8,16},{9,17... | collective-permute-start | bytes 786440 | tf_op jit(solution)/shard_map/ppermute | solution.py:31
  91.5 29.1 %collective-permute-start.17 = (bf16[512,2048]{1,0:T(8,128)(2,1)}, bf16[512,2048]{1,0:T(8,128)(2,1)}, u32[]{:S(2)}, u32[]{:S(2)}) collective-permute-start(bf16[512,2048]{1,0:T(8,128)(2,1)} %norm.3.refs_0_), channel_id=1, source_target_pairs={{0,1},{1,0},{2,3},{3,2},{4,5},{5,4},{6,7},{7,6},{8,9},{9,8},{10,11... | collective-permute-start | bytes 6291464 | tf_op jit(solution)/shard_map/ppermute | solution.py:26
  92.7 28.0 %all-to-all-start.1 = ((bf16[8,64,1408]{2,1,0:T(8,128)(2,1)}), bf16[8,64,1408]{2,1,0:T(8,128)(2,1)}, u32[]{:S(2)}, u32[]{:S(2)}) async-start(bf16[8,64,1408]{2,1,0:T(8,128)(2,1)} %mlp_parts.1), calls=%async_computation.1 | async-start | bytes 2883584 | tf_op jit(solution)/shard_map/all_to_all | solution.py:40
  96.9 161.0 %all-gather.2.cloned.1.call-start = ((), (), s32[]{:S(2)}) async-start(), calls=%async_computation.7 | async-start | bytes 7208960 | tf_op jit(solution)/shard_map/all_gather | solution.py:51
  100.8 19.9 %collective-permute-start.18 = (bf16[176,2048]{1,0:T(8,128)(2,1)}, bf16[176,2048]{1,0:T(8,128)(2,1)}, u32[]{:S(2)}, u32[]{:S(2)}) collective-permute-start(bf16[176,2048]{1,0:T(8,128)(2,1)} %refs_0_.1), channel_id=1, source_target_pairs={{0,8},{1,9},{2,10},{3,11},{4,12},{5,13},{6,14},{7,15},{8,16},{9,17... | collective-permute-start | bytes 2162696 | tf_op jit(solution)/shard_map/ppermute | solution.py:31
  100.9 30.2 %collective-permute-start.19 = (bf16[64,2048]{1,0:T(8,128)(2,1)}, bf16[64,2048]{1,0:T(8,128)(2,1)}, u32[]{:S(2)}, u32[]{:S(2)}) collective-permute-start(bf16[64,2048]{1,0:T(8,128)(2,1)} %copy-done.58), channel_id=1, source_target_pairs={{0,8},{1,9},{2,10},{3,11},{4,12},{5,13},{6,14},{7,15},{8,16},{9,17... | collective-permute-start | bytes 786440 | tf_op jit(solution)/shard_map/ppermute | solution.py:31
  137.4 259.2 %reduce-scatter.4.cloned.1.call-start = ((), (), s32[]{:S(2)}) async-start(), calls=%async_computation.8 | async-start | bytes 3604480 | tf_op jit(solution)/shard_map/reduce_scatter | solution.py:55
  137.5 25.2 %collective-permute-start.24 = (bf16[256,2048]{1,0:T(8,128)(2,1)S(1)}, bf16[256,2048]{1,0:T(8,128)(2,1)S(1)}, u32[]{:S(2)}, u32[]{:S(2)}) collective-permute-start(bf16[256,2048]{1,0:T(8,128)(2,1)S(1)} %copy-done.15), channel_id=1, source_target_pairs={{0,4},{1,5},{2,6},{3,7},{4,0},{5,1},{6,2},{7,3},{8,12},{9,13},{10,... | collective-permute-start | bytes 3145736 | tf_op jit(solution)/shard_map/ppermute | solution.py:26
  139.1 24.6 %collective-permute-start.23 = (bf16[256,2048]{1,0:T(8,128)(2,1)S(1)}, bf16[256,2048]{1,0:T(8,128)(2,1)S(1)}, u32[]{:S(2)}, u32[]{:S(2)}) collective-permute-start(bf16[256,2048]{1,0:T(8,128)(2,1)S(1)} %copy-done.15), channel_id=1, source_target_pairs={{0,2},{1,3},{2,0},{3,1},{4,6},{5,7},{6,4},{7,5},{8,10},{9,11},{10,... | collective-permute-start | bytes 3145736 | tf_op jit(solution)/shard_map/ppermute | solution.py:26
  146.8 39.4 %collective-permute-start.21 = (bf16[256,2048]{1,0:T(8,128)(2,1)S(1)}, bf16[256,2048]{1,0:T(8,128)(2,1)S(1)}, u32[]{:S(2)}, u32[]{:S(2)}) collective-permute-start(bf16[256,2048]{1,0:T(8,128)(2,1)S(1)} %get-tuple-element.192), channel_id=1, source_target_pairs={{0,2},{1,3},{2,0},{3,1},{4,6},{5,7},{6,4},{7,5},{8,10},{9,11},{10,... | collective-permute-start | bytes 3145736 | tf_op jit(solution)/shard_map/ppermute | solution.py:26
  148.4 37.8 %collective-permute-start.22 = (bf16[256,2048]{1,0:T(8,128)(2,1)S(1)}, bf16[256,2048]{1,0:T(8,128)(2,1)S(1)}, u32[]{:S(2)}, u32[]{:S(2)}) collective-permute-start(bf16[256,2048]{1,0:T(8,128)(2,1)S(1)} %get-tuple-element.193), channel_id=1, source_target_pairs={{0,4},{1,5},{2,6},{3,7},{4,0},{5,1},{6,2},{7,3},{8,12},{9,13},{10,... | collective-permute-start | bytes 3145736 | tf_op jit(solution)/shard_map/ppermute | solution.py:26
  149.6 39.8 %collective-permute-start.27 = (bf16[176,2048]{1,0:T(8,128)(2,1)}, bf16[176,2048]{1,0:T(8,128)(2,1)S(1)}, u32[]{:S(2)}, u32[]{:S(2)}) collective-permute-start(bf16[176,2048]{1,0:T(8,128)(2,1)} %collective-permute-done.18.refs_1_), channel_id=1, source_target_pairs={{0,8},{1,9},{2,10},{3,11},{4,12},{5,13},{6,14},{7,15},{8,16},{9,17... | collective-permute-start | bytes 2162696 | tf_op jit(solution)/shard_map/ppermute | solution.py:31
  203.9 22.7 %collective-permute-start.29 = (bf16[256,2048]{1,0:T(8,128)(2,1)S(1)}, bf16[256,2048]{1,0:T(8,128)(2,1)S(1)}, u32[]{:S(2)}, u32[]{:S(2)}) collective-permute-start(bf16[256,2048]{1,0:T(8,128)(2,1)S(1)} %get-tuple-element.206.refs_0_), channel_id=1, source_target_pairs={{0,4},{1,5},{2,6},{3,7},{4,0},{5,1},{6,2},{7,3},{8,12},{9,13},{10,... | collective-permute-start | bytes 3145736 | tf_op jit(solution)/shard_map/ppermute | solution.py:26
  204.4 22.5 %collective-permute-start.28 = (bf16[256,2048]{1,0:T(8,128)(2,1)S(1)}, bf16[256,2048]{1,0:T(8,128)(2,1)S(1)}, u32[]{:S(2)}, u32[]{:S(2)}) collective-permute-start(bf16[256,2048]{1,0:T(8,128)(2,1)S(1)} %get-tuple-element.206.refs_0_), channel_id=1, source_target_pairs={{0,2},{1,3},{2,0},{3,1},{4,6},{5,7},{6,4},{7,5},{8,10},{9,11},{10,... | collective-permute-start | bytes 3145736 | tf_op jit(solution)/shard_map/ppermute | solution.py:26
  240.4 33.9 %collective-permute-start.32 = (bf16[1024,2048]{1,0:T(8,128)(2,1)}, bf16[1024,2048]{1,0:T(8,128)(2,1)}, u32[]{:S(2)}, u32[]{:S(2)}) collective-permute-start(bf16[1024,2048]{1,0:T(8,128)(2,1)} %join.8), channel_id=1, source_target_pairs={{0,1},{1,0},{2,3},{3,2},{4,5},{5,4},{6,7},{7,6},{8,9},{9,8},{10,11... | collective-permute-start | bytes 12582920 | tf_op jit(solution)/shard_map/ppermute | solution.py:26
  246.2 28.2 %collective-permute-start.36 = (bf16[128,2048]{1,0:T(8,128)(2,1)}, bf16[128,2048]{1,0:T(8,128)(2,1)S(1)}, u32[]{:S(2)}, u32[]{:S(2)}) collective-permute-start(bf16[128,2048]{1,0:T(8,128)(2,1)} %slice.56), channel_id=1, source_target_pairs={{0,2},{1,3},{2,0},{3,1},{4,6},{5,7},{6,4},{7,5},{8,10},{9,11},{10,... | collective-permute-start | bytes 1572872 | tf_op jit(solution)/shard_map/ppermute | solution.py:26
  246.9 27.4 %collective-permute-start.35 = (bf16[128,2048]{1,0:T(8,128)(2,1)}, bf16[128,2048]{1,0:T(8,128)(2,1)S(1)}, u32[]{:S(2)}, u32[]{:S(2)}) collective-permute-start(bf16[128,2048]{1,0:T(8,128)(2,1)} %slice.55), channel_id=1, source_target_pairs={{0,4},{1,5},{2,6},{3,7},{4,0},{5,1},{6,2},{7,3},{8,12},{9,13},{10,... | collective-permute-start | bytes 1572872 | tf_op jit(solution)/shard_map/ppermute | solution.py:26
  257.9 29.2 %collective-permute-start.33 = (bf16[176,2048]{1,0:T(8,128)(2,1)S(1)}, bf16[176,2048]{1,0:T(8,128)(2,1)S(1)}, u32[]{:S(2)}, u32[]{:S(2)}) collective-permute-start(bf16[176,2048]{1,0:T(8,128)(2,1)S(1)} %copy-done.47), channel_id=1, source_target_pairs={{0,8},{1,9},{2,10},{3,11},{4,12},{5,13},{6,14},{7,15},{8,16},{9,17... | collective-permute-start | bytes 2162696 | tf_op jit(solution)/shard_map/ppermute | solution.py:31
  274.7 21.6 %collective-permute-start.37 = (bf16[1024,2048]{1,0:T(8,128)(2,1)S(1)}, bf16[1024,2048]{1,0:T(8,128)(2,1)}, u32[]{:S(2)}, u32[]{:S(2)}) collective-permute-start(bf16[1024,2048]{1,0:T(8,128)(2,1)S(1)} %join.10), channel_id=1, source_target_pairs={{0,1},{1,0},{2,3},{3,2},{4,5},{5,4},{6,7},{7,6},{8,9},{9,8},{10,11... | collective-permute-start | bytes 12582920 | tf_op jit(solution)/shard_map/ppermute | solution.py:26
  330.0 21.1 %collective-permute-start.39 = (bf16[1024,2048]{1,0:T(8,128)(2,1)}, bf16[1024,2048]{1,0:T(8,128)(2,1)}, u32[]{:S(2)}, u32[]{:S(2)}) collective-permute-start(bf16[1024,2048]{1,0:T(8,128)(2,1)} %convolution_convert_fusion.1), channel_id=1, source_target_pairs={{0,1},{1,0},{2,3},{3,2},{4,5},{5,4},{6,7},{7,6},{8,9},{9,8},{10,11... | collective-permute-start | bytes 12582920 | tf_op jit(solution)/shard_map/ppermute | solution.py:26
  330.4 173.3 %reduce-scatter.6.cloned.1.call-start = ((), (), s32[]{:S(2)}) async-start(), calls=%async_computation.9 | async-start | bytes 7208960 | tf_op jit(solution)/shard_map/reduce_scatter | solution.py:55
  330.4 25.0 %collective-permute-start.38 = (bf16[256,2048]{1,0:T(8,128)(2,1)}, bf16[256,2048]{1,0:T(8,128)(2,1)S(1)}, u32[]{:S(2)}, u32[]{:S(2)}) collective-permute-start(bf16[256,2048]{1,0:T(8,128)(2,1)} %copy-done.39), channel_id=1, source_target_pairs={{0,2},{1,3},{2,0},{3,1},{4,6},{5,7},{6,4},{7,5},{8,10},{9,11},{10,... | collective-permute-start | bytes 3145736 | tf_op jit(solution)/shard_map/ppermute | solution.py:26
  331.8 24.5 %collective-permute-start.40 = (bf16[256,2048]{1,0:T(8,128)(2,1)S(1)}, bf16[256,2048]{1,0:T(8,128)(2,1)S(1)}, u32[]{:S(2)}, u32[]{:S(2)}) collective-permute-start(bf16[256,2048]{1,0:T(8,128)(2,1)S(1)} %get-tuple-element.231), channel_id=1, source_target_pairs={{0,4},{1,5},{2,6},{3,7},{4,0},{5,1},{6,2},{7,3},{8,12},{9,13},{10,... | collective-permute-start | bytes 3145736 | tf_op jit(solution)/shard_map/ppermute | solution.py:26
  354.7 23.8 %collective-permute-start.41 = (bf16[256,2048]{1,0:T(8,128)(2,1)S(1)}, bf16[256,2048]{1,0:T(8,128)(2,1)S(1)}, u32[]{:S(2)}, u32[]{:S(2)}) collective-permute-start(bf16[256,2048]{1,0:T(8,128)(2,1)S(1)} %get-tuple-element.229), channel_id=1, source_target_pairs={{0,2},{1,3},{2,0},{3,1},{4,6},{5,7},{6,4},{7,5},{8,10},{9,11},{10,... | collective-permute-start | bytes 3145736 | tf_op jit(solution)/shard_map/ppermute | solution.py:26
  355.1 23.8 %collective-permute-start.42 = (bf16[256,2048]{1,0:T(8,128)(2,1)S(1)}, bf16[256,2048]{1,0:T(8,128)(2,1)S(1)}, u32[]{:S(2)}, u32[]{:S(2)}) collective-permute-start(bf16[256,2048]{1,0:T(8,128)(2,1)S(1)} %get-tuple-element.230), channel_id=1, source_target_pairs={{0,4},{1,5},{2,6},{3,7},{4,0},{5,1},{6,2},{7,3},{8,12},{9,13},{10,... | collective-permute-start | bytes 3145736 | tf_op jit(solution)/shard_map/ppermute | solution.py:26
  381.0 15.7 %collective-permute-start.43 = (bf16[128,2048]{1,0:T(8,128)(2,1)S(1)}, bf16[128,2048]{1,0:T(8,128)(2,1)S(1)}, u32[]{:S(2)}, u32[]{:S(2)}) collective-permute-start(bf16[128,2048]{1,0:T(8,128)(2,1)S(1)} %get-tuple-element.237), channel_id=1, source_target_pairs={{0,2},{1,3},{2,0},{3,1},{4,6},{5,7},{6,4},{7,5},{8,10},{9,11},{10,... | collective-permute-start | bytes 1572872 | tf_op jit(solution)/shard_map/ppermute | solution.py:26
  396.7 158.8 %reduce-scatter.8.cloned.1.call-start = ((), (), s32[]{:S(2)}) async-start(), calls=%async_computation.10 | async-start | bytes 1310720 | tf_op jit(solution)/shard_map/reduce_scatter | solution.py:55
  404.8 22.7 %collective-permute-start.47 = (bf16[256,2048]{1,0:T(8,128)(2,1)}, bf16[256,2048]{1,0:T(8,128)(2,1)S(1)}, u32[]{:S(2)}, u32[]{:S(2)}) collective-permute-start(bf16[256,2048]{1,0:T(8,128)(2,1)} %get-tuple-element.251.refs_0_), channel_id=1, source_target_pairs={{0,4},{1,5},{2,6},{3,7},{4,0},{5,1},{6,2},{7,3},{8,12},{9,13},{10,... | collective-permute-start | bytes 3145736 | tf_op jit(solution)/shard_map/ppermute | solution.py:26
  405.5 21.9 %collective-permute-start.46 = (bf16[256,2048]{1,0:T(8,128)(2,1)}, bf16[256,2048]{1,0:T(8,128)(2,1)S(1)}, u32[]{:S(2)}, u32[]{:S(2)}) collective-permute-start(bf16[256,2048]{1,0:T(8,128)(2,1)} %get-tuple-element.251.refs_0_), channel_id=1, source_target_pairs={{0,1},{1,0},{2,3},{3,2},{4,5},{5,4},{6,7},{7,6},{8,9},{9,8},{10,11... | collective-permute-start | bytes 3145736 | tf_op jit(solution)/shard_map/ppermute | solution.py:26
  408.8 25.1 %collective-permute-start.45 = (bf16[256,2048]{1,0:T(8,128)(2,1)}, bf16[256,2048]{1,0:T(8,128)(2,1)S(1)}, u32[]{:S(2)}, u32[]{:S(2)}) collective-permute-start(bf16[256,2048]{1,0:T(8,128)(2,1)} %get-tuple-element.251.refs_0_), channel_id=1, source_target_pairs={{0,2},{1,3},{2,0},{3,1},{4,6},{5,7},{6,4},{7,5},{8,10},{9,11},{10,... | collective-permute-start | bytes 3145736 | tf_op jit(solution)/shard_map/ppermute | solution.py:26
  434.7 15.7 %collective-permute-start.51 = (bf16[128,2048]{1,0:T(8,128)(2,1)S(1)}, bf16[128,2048]{1,0:T(8,128)(2,1)S(1)}, u32[]{:S(2)}, u32[]{:S(2)}) collective-permute-start(bf16[128,2048]{1,0:T(8,128)(2,1)S(1)} %slice.61), channel_id=1, source_target_pairs={{0,2},{1,3},{2,0},{3,1},{4,6},{5,7},{6,4},{7,5},{8,10},{9,11},{10,... | collective-permute-start | bytes 1572872 | tf_op jit(solution)/shard_map/ppermute | solution.py:26
  434.8 15.7 %collective-permute-start.50 = (bf16[128,2048]{1,0:T(8,128)(2,1)S(1)}, bf16[128,2048]{1,0:T(8,128)(2,1)S(1)}, u32[]{:S(2)}, u32[]{:S(2)}) collective-permute-start(bf16[128,2048]{1,0:T(8,128)(2,1)S(1)} %slice.60), channel_id=1, source_target_pairs={{0,4},{1,5},{2,6},{3,7},{4,0},{5,1},{6,2},{7,3},{8,12},{9,13},{10,... | collective-permute-start | bytes 1572872 | tf_op jit(solution)/shard_map/ppermute | solution.py:26
  482.1 16.2 %collective-permute-start.55 = (bf16[1024,2048]{1,0:T(8,128)(2,1)}, bf16[1024,2048]{1,0:T(8,128)(2,1)}, u32[]{:S(2)}, u32[]{:S(2)}) collective-permute-start(bf16[1024,2048]{1,0:T(8,128)(2,1)} %odd_parts.3), channel_id=1, source_target_pairs={{0,1},{1,0},{2,3},{3,2},{4,5},{5,4},{6,7},{7,6},{8,9},{9,8},{10,11... | collective-permute-start | bytes 12582920 | tf_op jit(solution)/shard_map/ppermute | solution.py:26
  503.7 23.8 %collective-permute-start.57 = (bf16[256,2048]{1,0:T(8,128)(2,1)S(1)}, bf16[256,2048]{1,0:T(8,128)(2,1)}, u32[]{:S(2)}, u32[]{:S(2)}) collective-permute-start(bf16[256,2048]{1,0:T(8,128)(2,1)S(1)} %get-tuple-element.278), channel_id=1, source_target_pairs={{0,2},{1,3},{2,0},{3,1},{4,6},{5,7},{6,4},{7,5},{8,10},{9,11},{10,... | collective-permute-start | bytes 3145736 | tf_op jit(solution)/shard_map/ppermute | solution.py:26
  504.9 23.2 %collective-permute-start.58 = (bf16[256,2048]{1,0:T(8,128)(2,1)S(1)}, bf16[256,2048]{1,0:T(8,128)(2,1)}, u32[]{:S(2)}, u32[]{:S(2)}) collective-permute-start(bf16[256,2048]{1,0:T(8,128)(2,1)S(1)} %get-tuple-element.279), channel_id=1, source_target_pairs={{0,4},{1,5},{2,6},{3,7},{4,0},{5,1},{6,2},{7,3},{8,12},{9,13},{10,... | collective-permute-start | bytes 3145736 | tf_op jit(solution)/shard_map/ppermute | solution.py:26
  508.1 46.7 %all-to-all-start.2 = ((bf16[8,64,1408]{2,1,0:T(8,128)(2,1)}), bf16[8,64,1408]{2,1,0:T(8,128)(2,1)S(1)}, u32[]{:S(2)}, u32[]{:S(2)}) async-start(bf16[8,64,1408]{2,1,0:T(8,128)(2,1)} %bitcast.77), calls=%async_computation.4 | async-start | bytes 2883584 | tf_op jit(solution)/shard_map/all_to_all | solution.py:40
  520.9 18.6 %collective-permute-start.62 = (bf16[512,320]{0,1:T(8,128)(2,1)}, bf16[512,320]{0,1:T(8,128)(2,1)}, u32[]{:S(2)}, u32[]{:S(2)}) collective-permute-start(bf16[512,320]{0,1:T(8,128)(2,1)} %add_convert_fusion.4), channel_id=1, source_target_pairs={{0,8},{1,9},{2,10},{3,11},{4,12},{5,13},{6,14},{7,15},{8,16},{9,17... | collective-permute-start | bytes 983048 | tf_op jit(solution)/shard_map/ppermute | solution.py:31
  531.2 23.0 %collective-permute-start.59 = (bf16[128,2048]{1,0:T(8,128)(2,1)}, bf16[128,2048]{1,0:T(8,128)(2,1)}, u32[]{:S(2)}, u32[]{:S(2)}) collective-permute-start(bf16[128,2048]{1,0:T(8,128)(2,1)} %get-tuple-element.287), channel_id=1, source_target_pairs={{0,2},{1,3},{2,0},{3,1},{4,6},{5,7},{6,4},{7,5},{8,10},{9,11},{10,... | collective-permute-start | bytes 1572872 | tf_op jit(solution)/shard_map/ppermute | solution.py:26
  532.3 22.5 %collective-permute-start.60 = (bf16[128,2048]{1,0:T(8,128)(2,1)}, bf16[128,2048]{1,0:T(8,128)(2,1)}, u32[]{:S(2)}, u32[]{:S(2)}) collective-permute-start(bf16[128,2048]{1,0:T(8,128)(2,1)} %get-tuple-element.288), channel_id=1, source_target_pairs={{0,4},{1,5},{2,6},{3,7},{4,0},{5,1},{6,2},{7,3},{8,12},{9,13},{10,... | collective-permute-start | bytes 1572872 | tf_op jit(solution)/shard_map/ppermute | solution.py:26
  557.7 23.0 %collective-permute-start.64 = (bf16[64,2048]{1,0:T(8,128)(2,1)}, bf16[64,2048]{1,0:T(8,128)(2,1)}, u32[]{:S(2)}, u32[]{:S(2)}) collective-permute-start(bf16[64,2048]{1,0:T(8,128)(2,1)} %reduce-scatter.8.cloned.1.call-done), channel_id=1, source_target_pairs={{0,0},{8,1},{16,2},{24,3},{1,4},{9,5},{17,6},{25,7},{2,8},{10,9},{... | collective-permute-start | bytes 786440 | tf_op jit(solution)/shard_map/ppermute | solution.py:857
  562.1 20.3 %all-to-all-start.3 = ((bf16[8,64,320]{2,1,0:T(8,128)(2,1)}), bf16[8,64,320]{2,1,0:T(8,128)(2,1)S(1)}, u32[]{:S(2)}, u32[]{:S(2)}) async-start(bf16[8,64,320]{2,1,0:T(8,128)(2,1)} %bitcast.76), calls=%async_computation.6 | async-start | bytes 786432 | tf_op jit(solution)/shard_map/all_to_all | solution.py:40
  (131 other events, 1502.2 us)
Sparse Core Ops, SparseCore 0:
  137.5 120.3 all-gather.1
  330.5 56.8 reduce-scatter.3
  396.8 104.5 reduce-scatter.5
  504.1 36.6 reduce-scatter.7
